TPU v7x, 32 devices: a whole 2x2x4 slice. The times are simulated.
32 devices in a mesh: dp: 8 (over y, x, core), tensor: 4 (over z).
Axes of the slice: x: 2, y: 2, z: 4, core: 2. Of those that a mesh axis runs over, the one named last changes fastest.
Arguments:
- tokens: bfloat16 [8192, 1024], P(('dp', 'tensor')), may hold values from -6 to 6
- query_proj: bfloat16 [1024, 512], P('dp', 'tensor'), may hold values from -0.1875 to 0.1875
- attend_out: bfloat16 [512, 1024], P('tensor', 'dp'), may hold values from -3 to 3
- inner_proj: bfloat16 [2, 1024, 1536], P(None, 'dp', 'tensor'), may hold values from -0.1875 to 0.1875
- step_proj: bfloat16 [1024, 24], P('dp', 'tensor'), may hold values from -0.1875 to 0.1875
- mamba_out: bfloat16 [1536, 1024], P('tensor', 'dp'), may hold values from -0.15625 to 0.15625
- hidden_proj: bfloat16 [2, 1024, 2048], P(None, 'dp', 'tensor'), may hold values from -0.1875 to 0.1875
- down_proj: bfloat16 [2048, 1024], P('tensor', 'dp'), may hold values from -0.125 to 0.125
- channel_taps: bfloat16 [5, 24, 64], P(None, 'tensor', 'dp'), may hold values from -3 to 3
- mixer_gain: bfloat16 [24, 64], P('tensor', 'dp'), may hold values from 0.25 to 1.75
- decay_log: bfloat16 [24], P('tensor'), may hold values from -4 to 0
- step_bias: bfloat16 [24], P('tensor'), may hold values from -6 to -2
- skip_weight: bfloat16 [24], P('tensor'), may hold values from 0.5 to 2
- shared_proj: bfloat16 [1024, 512], P(('dp', 'tensor')), may hold values from -0.1875 to 0.1875
- norm_gains: bfloat16 [2, 1024], P(None, ('dp', 'tensor')), may hold values from 0.25 to 1.75
- shared_taps: bfloat16 [5, 256], P(None, ('dp', 'tensor')), may hold values from -3 to 3
- cotangent: bfloat16 [8192, 1024], P(('dp', 'tensor')), may hold values from -6 to 6
Outputs:
- layer_out: bfloat16 [8192, 1024], P(('dp', 'tensor'))
- gradient_tokens: bfloat16 [8192, 1024], P(('dp', 'tensor'))
- gradient_query: float32 [1024, 512], P('dp', 'tensor')
- gradient_attend: float32 [512, 1024], P('tensor', 'dp')
- gradient_inner: float32 [2, 1024, 1536], P(None, 'dp', 'tensor')
- gradient_step: float32 [1024, 24], P('dp', 'tensor')
- gradient_mamba: float32 [1536, 1024], P('tensor', 'dp')
- gradient_hidden: float32 [2, 1024, 2048], P(None, 'dp', 'tensor')
- gradient_down: float32 [2048, 1024], P('tensor', 'dp')
- gradient_channel: float32 [5, 24, 64], P(None, 'tensor', 'dp')
- gradient_mixer: float32 [24, 64], P('tensor', 'dp')
- gradient_decay: float32 [24], P('tensor')
- gradient_bias: float32 [24], P('tensor')
- gradient_skip: float32 [24], P('tensor')
- gradient_shared: float32 [1024, 512], P(('dp', 'tensor'))
- gradient_norms: float32 [2, 1024], P(None, ('dp', 'tensor'))
- gradient_taps: float32 [5, 256], P(None, ('dp', 'tensor'))
All inputs are finite; a program needn't handle non-finite values.
Results may differ from a plain program's by a relative error of at most 0.024.
Values may be sent and summed in bfloat16 or wider, within the bound.
A program may use at most 192 MiB of HBM per device.

v0:
```python
from functools import partial

import numpy as np
import jax
import jax.numpy as jnp
from jax import lax
from jax.experimental import pallas as pl
from jax.experimental.pallas import tpu as pltpu
from jax.sharding import PartitionSpec as P

MESH = pl.DeviceIdType.MESH

QHEADS = 8
KVHEADS = 2
HEAD_SIZE = 64
SSM_DIM = 64
CONV = 4


epsilon = 1e-05
rope_base = 100000000000.0
neg_large = -1e30
block_len = 128


def norm_apply(values, gain):
    factor = lax.rsqrt(jnp.mean(values * values, axis=-1, keepdims=True) + epsilon)
    return values * factor * gain


def dp_bits(index):
    core = lax.rem(index, 2)
    xbit = lax.rem(index // 2, 2)
    ybit = lax.rem(index // 4, 2)
    return core, xbit, ybit


def remote_copy(src, dst, send, recv, dev):
    return pltpu.make_async_remote_copy(
        src_ref=src, dst_ref=dst, send_sem=send, recv_sem=recv, device_id=dev, device_id_type=MESH
    )


def greet(peers):
    barrier = pltpu.get_barrier_semaphore()
    for peer in peers:
        pl.semaphore_signal(barrier, inc=1, device_id=peer, device_id_type=MESH)
    pl.semaphore_wait(barrier, len(peers))


def other_quarters(d, z, nt):
    return [(d, lax.rem(z + k, nt)) for k in range(1, nt)]


def cube_peers(d):
    core, xbit, ybit = dp_bits(d)
    return d + 1 - 2 * core, d + 2 - 4 * xbit, d + 4 - 8 * ybit


class CubeGather:
    def __init__(self, items, via_y, send, recv, d, z):
        self.items, self.via_y, self.send, self.recv = items, via_y, send, recv
        self.d, self.z = d, z
        self.d_core, self.d_x, self.d_y = cube_peers(d)
        self.d_xy = self.d_x + self.d_y - d
        self.sent = []

    def push(self, i, j, src, dst, peer):
        def make():
            return remote_copy(src(), dst(), self.send.at[i, j], self.recv.at[i, j], (peer, self.z))

        make().start()
        self.sent.append(make)

    def landed(self, i, j, slot):
        at = self.items[i][1]
        remote_copy(
            at(slot), at(slot), self.send.at[i, j], self.recv.at[i, j], (self.d_core, self.z)
        ).wait_recv()

    def start(self, i):
        src, at = self.items[i]
        for j, peer in enumerate((self.d_x, self.d_y, self.d_core)):
            self.push(i, j, lambda: src, lambda: at(self.d), peer)

    def near(self, i):
        d_x, d_y, d_core = self.d_x, self.d_y, self.d_core
        self.landed(i, 0, d_x)
        if i in self.via_y:
            self.hand_on(i, 3, d_x, d_y)
        self.hand_on(i, 4, d_x, d_core)
        self.landed(i, 1, d_y)
        if i not in self.via_y:
            self.hand_on(i, 3, d_y, d_x)
        self.hand_on(i, 5, d_y, d_core)

    def hand_on(self, i, j, slot, peer):
        at = self.items[i][1]
        self.push(i, j, lambda: at(slot), lambda: at(slot), peer)

    def far(self, i):
        self.landed(i, 3, self.d_xy)
        self.hand_on(i, 6, self.d_xy, self.d_core)

    def finish(self):
        for i in range(len(self.items)):
            self.landed(i, 2, self.d_core)
            for j in (4, 5, 6):
                self.landed(i, j, self.d_core)
        for make in self.sent:
            make().wait_send()


def gather_kernel(nt, *refs):
    (tok, que, att, inn, mam, sha, sma) = refs[:7]
    (tok_f, que_f, att_f, inn_f, mam_f, sha_f, sma_f) = refs[7:14]
    (lsem, zs_send, zs_recv, t_send, t_recv, d_send, d_recv) = refs[14:]
    d = lax.axis_index("dp")
    z = lax.axis_index("tensor")
    greet([(p, z) for p in cube_peers(d)] + other_quarters(d, z, nt))

    small = []
    for i, (src, dst) in enumerate(((sha, sha_f), (sma, sma_f))):
        for k, peer in enumerate(other_quarters(d, z, nt)):
            small.append(remote_copy(src, dst.at[d, z], zs_send.at[i, k], zs_recv.at[i, k], peer))
            small[-1].start()
    q_rows = que.shape[0]
    cols = att.shape[1]
    i_rows = inn.shape[1]
    items = [
        (inn, lambda s: inn_f.at[:, pl.ds(s * i_rows, i_rows)]),
        (que, lambda s: que_f.at[pl.ds(s * q_rows, q_rows)]),
        (att, lambda s: att_f.at[:, pl.ds(pl.multiple_of(s * cols, cols), cols)]),
        (mam, lambda s: mam_f.at[:, pl.ds(pl.multiple_of(s * cols, cols), cols)]),
        (sha_f.at[d], lambda s: sha_f.at[s]),
        (sma_f.at[d], lambda s: sma_f.at[s]),
    ]
    cube = CubeGather(items, (0, 5), d_send, d_recv, d, z)
    locals_ = []
    for i, (src, dst) in enumerate(
        [(sha, sha_f.at[d, z]), (sma, sma_f.at[d, z]), (tok, tok_f.at[z])]
        + [(src, at(d)) for src, at in items[:4]]
    ):
        copy = pltpu.make_async_copy(src, dst, lsem.at[i])
        copy.start()
        locals_.append(copy)
    for i in range(4):
        cube.start(i)
    chain = ChainGather(tok, tok_f, t_send, t_recv, d, z, nt)
    chain.start()
    locals_[0].wait()
    locals_[1].wait()
    for copy in small:
        copy.wait()
    cube.start(4)
    cube.start(5)
    for i in range(4):
        cube.near(i)
    chain.hop(1)
    for i in (4, 5):
        cube.near(i)
    for i in range(6):
        cube.far(i)
    for dist in range(2, nt):
        chain.hop(dist)
    cube.finish()
    for copy in locals_[2:]:
        copy.wait()
    chain.drain()


def gather_start(tok, que, att, inn, mam, sha, sma, nd, nt):
    if nd != 8:
        shared = lax.all_gather(sha, ("dp", "tensor"), axis=0)
        small = lax.all_gather(sma, ("dp", "tensor"), axis=0)
        return (
            lax.all_gather(tok, "tensor", axis=0),
            lax.all_gather(que, "dp", axis=0, tiled=True),
            lax.all_gather(att, "dp", axis=1, tiled=True),
            lax.all_gather(inn, "dp", axis=1, tiled=True),
            lax.all_gather(mam, "dp", axis=1, tiled=True),
            shared.reshape((nd, nt) + sha.shape),
            small.reshape((nd, nt) + sma.shape),
        )
    bf = jnp.bfloat16
    outs = (
        (nt,) + tok.shape,
        (nd * que.shape[0], que.shape[1]),
        (att.shape[0], nd * att.shape[1]),
        (2, nd * inn.shape[1], inn.shape[2]),
        (mam.shape[0], nd * mam.shape[1]),
        (nd, nt) + sha.shape,
        (nd, nt) + sma.shape,
    )
    anywhere = pl.BlockSpec(memory_space=pl.ANY)
    dma = pltpu.SemaphoreType.DMA
    return pl.pallas_call(
        partial(gather_kernel, nt),
        out_shape=[jax.ShapeDtypeStruct(s, bf) for s in outs],
        in_specs=[pl.BlockSpec(memory_space=pltpu.VMEM)] * 7,
        out_specs=[anywhere] * 7,
        scratch_shapes=[
            dma((7,)), dma((2, nt)), dma((2, nt)), dma((2, nt)), dma((2, nt)),
            dma((6, 7)), dma((6, 7)),
        ],
        compiler_params=pltpu.CompilerParams(collective_id=0, has_side_effects=True),
        name="gather_start",
    )(tok, que, att, inn, mam, sha, sma)


def pack_kernel(taps, gain, norms, staps, step, out, rows):
    heads = step.shape[1]
    f32 = jnp.float32
    rows[...] = jnp.zeros(rows.shape, f32)
    rows[0:2, 0:32] = norms[...].astype(f32)
    rows[0 : CONV + 1, 32:40] = staps[...].astype(f32)
    rows[0:heads, 40:48] = gain[...].astype(f32)
    for j in range(CONV + 1):
        rows[0:heads, 48 + 8 * j : 56 + 8 * j] = taps[j].astype(f32)
    wide = jnp.concatenate([step[...].astype(f32), jnp.zeros((128, 128 - heads), f32)], axis=1)
    rows[8:16, :] = wide.T[0:8, :]
    out[...] = rows[...].astype(jnp.bfloat16)


def pack_small(taps, gain, norms, staps, step):
    vmem = pl.BlockSpec(memory_space=pltpu.VMEM)
    return pl.pallas_call(
        pack_kernel,
        in_specs=[vmem] * 5,
        out_specs=vmem,
        out_shape=jax.ShapeDtypeStruct((16, 128), jnp.bfloat16),
        scratch_shapes=[pltpu.VMEM((16, 128), jnp.float32)],
        name="pack_small",
    )(taps, gain, norms, staps, step)


def unpack_kernel(
    heads, where, scal, packed, first_o, second_o, gain_o, tapx_o, tapb_o, step_o, decay_o, bias_o, skip_o
):
    z = where[0]
    f32 = jnp.float32
    nd, nt = packed.shape[:2]
    tiles = [[packed[k, q].astype(f32) for q in range(nt)] for k in range(nd)]
    for k in range(nd):
        both = jnp.concatenate([tiles[k][q][0:8, 0:32] for q in range(nt)], axis=1)
        first_o[:, 128 * k : 128 * k + 128] = both[0:1]
        second_o[:, 128 * k : 128 * k + 128] = both[1:2]
        step_o[:, 128 * k : 128 * k + 128] = packed[k, z].astype(f32)[8:16, :].astype(jnp.bfloat16)
    half = nd // 2
    for k in range(2):
        tapb_o[:, 128 * k : 128 * k + 128] = jnp.concatenate(
            [tiles[half * k + i][q][0:8, 32:40] for i in range(half) for q in range(nt)], axis=1
        )
    own = [packed[k, z].astype(f32) for k in range(nd)]

    def by_head(lane):
        wide = jnp.concatenate([own[k][0:8, lane : lane + 8] for k in range(nd)], axis=1)
        return jnp.concatenate([wide[h : h + 1, :] for h in range(heads)], axis=1)

    gain_o[...] = by_head(40)
    tapx_o[...] = jnp.zeros(tapx_o.shape, f32)
    tapb_o[CONV + 1 :, :] = jnp.zeros((7 - CONV, tapb_o.shape[1]), f32)
    for j in range(CONV + 1):
        tapx_o[j : j + 1, :] = by_head(48 + 8 * j)
    sub = lax.broadcasted_iota(jnp.int32, (8, 128), 0)
    decay = jnp.zeros((8, 128), f32)
    bias = jnp.zeros((8, 128), f32)
    for h in range(heads):
        decay = jnp.where(sub == h, scal[0, h], decay)
        bias = jnp.where(sub == h, scal[1, h], bias)
        skip_o[:, SSM_DIM * h : SSM_DIM * (h + 1)] = jnp.full((1, SSM_DIM), scal[2, h], f32)
    decay_o[...] = jnp.where(sub < heads, -jnp.exp(decay), 0.0)
    bias_o[...] = bias


def unpack_small(heads, where, scal, packed, width):
    inner = heads * SSM_DIM
    vmem = pl.BlockSpec(memory_space=pltpu.VMEM)
    smem = pl.BlockSpec(memory_space=pltpu.SMEM)
    sds = jax.ShapeDtypeStruct
    f32 = jnp.float32
    shapes = [(1, width), (1, width), (1, inner), (8, inner), (8, 256)]
    return pl.pallas_call(
        partial(unpack_kernel, heads),
        in_specs=[smem, smem, vmem],
        out_specs=[vmem] * 9,
        out_shape=[sds(s, f32) for s in shapes]
        + [sds((8, width), jnp.bfloat16), sds((8, 128), f32), sds((8, 128), f32), sds((1, inner), f32)],
        name="unpack_small",
    )(where, scal, packed)


def pick(values, index, axis=0):
    return lax.dynamic_index_in_dim(values, index, axis, keepdims=False)


def add_low(left, right):
    return (left.astype(jnp.float32) + right.astype(jnp.float32)).astype(jnp.bfloat16)


def chain_scatter(parts, nt):
    z = lax.axis_index("tensor")
    right = left = None
    for t in range(nt - 1):
        to_right = pick(parts, jnp.clip(nt - 1 - t + z, 0, nt - 1))
        to_left = pick(parts, jnp.clip(t - (nt - 1) + z, 0, nt - 1))
        if t > 0:
            to_right = add_low(to_right, right)
            to_left = add_low(to_left, left)
        right = lax.ppermute(to_right, "tensor", [(i, i + 1) for i in range(t + 1)])
        left = lax.ppermute(
            to_left, "tensor", [(nt - 1 - i, nt - 2 - i) for i in range(t + 1)]
        )
    f32 = jnp.float32
    return pick(parts, z).astype(f32) + right.astype(f32) + left.astype(f32)


def cube_scatter(parts, nd, last=jnp.float32):
    return lax.psum_scatter(parts, "dp", scatter_dimension=0, tiled=False).astype(last)


F32, BF16 = jnp.float32, jnp.bfloat16
VMEM_LIMIT = 56 * 1024 * 1024


def dot_nn(a, b):
    return lax.dot_general(a, b, (((1,), (0,)), ((), ())), preferred_element_type=F32)


def dot_nt(a, b):
    return lax.dot_general(a, b, (((1,), (1,)), ((), ())), preferred_element_type=F32)


def dot_tn(a, b):
    return lax.dot_general(a, b, (((0,), (0,)), ((), ())), preferred_element_type=F32)


def sigmoid(v):
    return 1.0 / (1.0 + jnp.exp(-v))


def lanes_of(shape):
    return lax.broadcasted_iota(jnp.int32, shape, len(shape) - 1)


def turn(values, cosine, sine):
    lane = lanes_of(values.shape)
    other = jnp.where(
        lax.rem(lane, HEAD_SIZE) < HEAD_SIZE // 2,
        pltpu.roll(values, 128 - HEAD_SIZE // 2, 1),
        pltpu.roll(values, HEAD_SIZE // 2, 1),
    )
    return values * cosine + other * sine


def softplus(v):
    return jnp.maximum(v, 0.0) + jnp.log1p(jnp.exp(-jnp.abs(v)))


def running_sum(rows):
    lane = lanes_of(rows.shape)
    step = 1
    while step < rows.shape[1]:
        rows = rows + jnp.where(lane >= step, pltpu.roll(rows, step, 1), 0.0)
        step *= 2
    return rows


def running_sum_back(rows):
    lane = lanes_of(rows.shape)
    width = rows.shape[1]
    step = 1
    while step < width:
        rows = rows + jnp.where(lane < width - step, pltpu.roll(rows, width - step, 1), 0.0)
        step *= 2
    return rows


def stack_columns(rows_list):
    used = sum(r.shape[0] for r in rows_list)
    filler = jnp.zeros((128 - used, 128), F32)
    return jnp.concatenate(rows_list + [filler], axis=0).T


def widen(cols, base, heads):
    low = lanes_of((cols.shape[0], 128)) < SSM_DIM
    return jnp.concatenate(
        [
            jnp.where(low, cols[:, base + 2 * p : base + 2 * p + 1],
                      cols[:, base + 2 * p + 1 : base + 2 * p + 2])
            for p in range(heads // 2)
        ],
        axis=1,
    )


def conv_rows(ref, taps, first, rows):
    total = taps[CONV : CONV + 1, :] + taps[0:1, :] * ref[pl.ds(first, rows), :]
    for j in range(1, CONV):
        total = total + taps[j : j + 1, :] * ref[pl.ds(first + j, rows), :]
    return total


class FeedGather:
    def __init__(self, step, nt, hid, dwn, hid_f, dwn_f, hid_z, dwn_z, lsem, sems):
        self.step, self.nt = step, nt
        d = lax.axis_index("dp")
        z = lax.axis_index("tensor")
        self.d, self.z = d, z
        self.cube = CubeGather(
            [(hid, lambda s: hid_f.at[s, z]), (dwn, lambda s: dwn_f.at[s, z])], (0,), sems[0], sems[1], d, z
        )
        self.chains = [
            ChainGather(hid, hid_z, sems[2], sems[3], d, z, nt),
            ChainGather(dwn, dwn_z, sems[4], sems[5], d, z, nt),
        ]
        self.own = lambda: [
            pltpu.make_async_copy(hid, hid_f.at[d, z], lsem.at[0]),
            pltpu.make_async_copy(dwn, dwn_f.at[d, z], lsem.at[1]),
        ]

    def at(self, step, act):
        pl.when(self.step == step)(act)

    def begin(self):
        def act():
            greet([(p, self.z) for p in cube_peers(self.d)] + other_quarters(self.d, self.z, self.nt))
            for chain in self.chains:
                chain.start()
            for i in range(2):
                self.cube.start(i)
            for copy in self.own():
                copy.start()

        self.at(0, act)
        def late():
            for chain in self.chains:
                chain.hop(2)

        self.at(3, late)

    def middle(self):
        def near():
            for chain in self.chains:
                chain.hop(1)
            for i in range(2):
                self.cube.near(i)

        def far():
            for i in range(2):
                self.cube.far(i)

        self.at(1, near)
        self.at(2, far)

    def end(self):
        def act():
            for chain in self.chains:
                chain.hop(3)
            self.cube.finish()
            for copy in self.own():
                copy.wait()
            for chain in self.chains:
                chain.drain()

        self.at(3, act)


def forward_kernel(heads, nt, feed, *refs):
    if feed:
        beside = FeedGather(
            pl.program_id(0), nt, *refs[14:16], *refs[29:33], refs[38], refs[39:45]
        )
        refs = refs[:14] + refs[16:29] + refs[33:38]
        beside.begin()
        forward_step(heads, beside.middle, *refs)
        beside.end()
    else:
        forward_step(heads, lambda: None, *refs)


def forward_step(
    heads, middle, kvh, tok, gain, wq, win, stp, wsh, cosine, sine, tapx, tapb, decay, bias, skip,
    a1_o, q_o, k_o, v_o, lse_o, o_o, x_o, z_o, b_o, y_o, t_o, s_o, sq_o,
    keys, vals, xs, bs, state,
):
    step = pl.program_id(0)
    rows = tok.shape[0]
    second = kvh[0] == 1

    @pl.when(step == 0)
    def _():
        xs[0:8, :] = jnp.zeros((8, xs.shape[1]), F32)
        bs[0:8, :] = jnp.zeros((8, bs.shape[1]), F32)
        state[...] = jnp.zeros(state.shape, F32)

    t = tok[...].astype(F32)
    r = lax.rsqrt(jnp.mean(t * t, axis=1, keepdims=True) + epsilon)
    a1 = (t * r * gain[...]).astype(BF16)
    a1_o[...] = a1
    q = turn(dot_nn(a1, wq[...]), cosine[...], sine[...]).astype(BF16)
    q_o[...] = q
    s = dot_nn(a1, wsh[...])
    low = lanes_of((rows, 128)) < HEAD_SIZE
    k = turn(s[:, :128], cosine[...], sine[...])
    v = s[:, 128:256]
    pick_own = low != second
    k2 = jnp.where(pick_own, k, pltpu.roll(k, 64, 1)).astype(BF16)
    v2 = jnp.where(pick_own, v, pltpu.roll(v, 64, 1))
    k_o[...] = k2
    v_o[...] = v2.astype(BF16)
    place = pl.ds(pl.multiple_of(step * rows, rows), rows)
    keys[place, :] = k2
    vals[:, place] = v2.T.astype(BF16)

    scale = HEAD_SIZE**-0.5

    def attend(blocks):
        n = blocks * rows
        shape = (rows, rows)
        allowed = lax.broadcasted_iota(jnp.int32, shape, 0) <= lanes_of(shape)
        parts = []
        for h in range(2):
            qh = jnp.where(low == (h == 0), q, jnp.zeros_like(q))
            sc = dot_nt(keys[0:n, :], qh) * scale
            last = jnp.where(allowed, sc[n - rows :, :], neg_large)
            sc = jnp.concatenate([sc[: n - rows, :], last], axis=0) if blocks > 1 else last
            top = jnp.max(sc, axis=0, keepdims=True)
            e = jnp.exp(sc - top)
            total = jnp.sum(e, axis=0, keepdims=True)
            lse_o[h : h + 1, :] = top + jnp.log(total)
            parts.append(dot_nn(vals[:, 0:n], e.astype(BF16)) / total)
        sub = lax.broadcasted_iota(jnp.int32, parts[0].shape, 0)
        o_o[...] = jnp.where(sub < HEAD_SIZE, parts[0], parts[1]).T.astype(BF16)

    for i in range(keys.shape[0] // rows):
        pl.when(step == i)(partial(attend, i + 1))

    middle()
    zr = dot_nn(a1, win[0])
    z_o[...] = zr
    xr = dot_nn(a1, win[1])
    x_o[...] = xr
    br = s[:, 256:]
    b_o[...] = br
    xs[8 : 8 + rows, :] = xr
    bs[8 : 8 + rows, :] = br
    u = conv_rows(xs, tapx, 5, rows)
    x = u * sigmoid(u)
    u = conv_rows(bs, tapb, 5, rows)
    bc = (u * sigmoid(u)).astype(BF16)
    xs[0:8, :] = xs[rows : rows + 8, :]
    bs[0:8, :] = bs[rows : rows + 8, :]
    tr = dot_nt(stp[...], a1)
    t_o[...] = tr
    n_state = bc.shape[1] // 2
    tri_shape = (block_len, block_len)
    lower = lax.broadcasted_iota(jnp.int32, tri_shape, 0) >= lanes_of(tri_shape)
    half = lanes_of(tri_shape) < SSM_DIM
    for c in range(rows // block_len):
        part = slice(c * block_len, (c + 1) * block_len)
        dt = softplus(tr[:, part] + bias[...])
        cum = running_sum(dt * decay[...])
        end = cum[:, block_len - 1 :]
        cols = stack_columns([cum, jnp.exp(cum), dt * jnp.exp(end - cum)])
        xc = x[part]
        x_low = xc.astype(BF16)
        b_low = bc[part, :n_state]
        c_low = bc[part, n_state:]
        cross = dot_nt(c_low, b_low)
        grow = widen(cols, 8, heads)
        y = dot_nn(c_low, state[...].astype(BF16)) * grow + skip[...] * xc
        inner = []
        for p in range(heads // 2):
            mats = []
            for h in (2 * p, 2 * p + 1):
                gap = jnp.where(lower, cols[:, h : h + 1] - cum[h : h + 1, :], neg_large)
                mats.append((cross * jnp.exp(gap) * dt[h : h + 1, :]).astype(BF16))
            xp = x_low[:, 128 * p : 128 * p + 128]
            zero = jnp.zeros_like(xp)
            both = jnp.concatenate([jnp.where(half, xp, zero), jnp.where(half, zero, xp)], axis=0)
            inner.append(dot_nn(jnp.concatenate(mats, axis=1), both))
        y = y + jnp.concatenate(inner, axis=1)
        y_o[part, :] = y
        s_o[c] = state[...]
        carried = (xc * widen(cols, 16, heads)).astype(BF16)
        state[...] = grow[block_len - 1 :, :] * state[...] + dot_tn(b_low, carried)
        zc = zr[part]
        w = y * (zc * sigmoid(zc))
        total = jnp.sum(w * w, axis=1, keepdims=True)
        sq_o[:, part] = jnp.broadcast_to(total, (block_len, 128)).T[0:8, :]


def mixers_forward(
    heads, nt, kvh, tok, gain, wq, win, stp, wsh, cosine, sine, tapx, tapb, decay, bias, skip, feed=()
):
    total, width = tok.shape
    rows = 256
    inner = heads * SSM_DIM
    pair = wsh.shape[1] - 256
    state = pair // 2
    chunks = rows // block_len

    def whole(v):
        return pl.BlockSpec(v.shape, lambda i: (0,) * v.ndim)

    def tall(n):
        return pl.BlockSpec((rows, n), lambda i: (i, 0))

    wide = pl.BlockSpec((8, rows), lambda i: (0, i))
    sds = jax.ShapeDtypeStruct
    more_in, more_out, more_shape, more_scratch, extra = [], [], [], [], {}
    if feed:
        nd = 8
        dma = pltpu.SemaphoreType.DMA
        more_in = [whole(v) for v in feed]
        more_out = [pl.BlockSpec(memory_space=pl.ANY)] * 4
        more_shape = [sds((nd, nt) + v.shape, BF16) for v in feed] + [sds((nt,) + v.shape, BF16) for v in feed]
        more_scratch = [dma((2,)), dma((2, 7)), dma((2, 7))] + [dma((2, nt - 1))] * 4
        extra = dict(collective_id=6, has_side_effects=True)
    return pl.pallas_call(
        partial(forward_kernel, heads, nt, bool(feed)),
        grid=(total // rows,),
        in_specs=[pl.BlockSpec(memory_space=pltpu.SMEM), tall(width), whole(gain), whole(wq), whole(win),
                  whole(stp), whole(wsh), tall(128), tall(128), whole(tapx), whole(tapb),
                  whole(decay), whole(bias), whole(skip)] + more_in,
        out_specs=[tall(width), tall(128), tall(128), tall(128), wide, tall(128), tall(inner),
                   tall(inner), tall(pair), tall(inner), wide,
                   pl.BlockSpec((chunks, state, inner), lambda i: (i, 0, 0)), wide] + more_out,
        out_shape=[sds((total, width), BF16), sds((total, 128), BF16), sds((total, 128), BF16),
                   sds((total, 128), BF16), sds((8, total), F32), sds((total, 128), BF16),
                   sds((total, inner), F32), sds((total, inner), F32), sds((total, pair), F32),
                   sds((total, inner), F32), sds((8, total), F32),
                   sds((total // block_len, state, inner), F32), sds((8, total), F32)] + more_shape,
        scratch_shapes=[pltpu.VMEM((total, 128), BF16), pltpu.VMEM((128, total), BF16),
                        pltpu.VMEM((rows + 8, inner), F32), pltpu.VMEM((rows + 8, pair), F32),
                        pltpu.VMEM((state, inner), F32)] + more_scratch,
        compiler_params=pltpu.CompilerParams(vmem_limit_bytes=VMEM_LIMIT, **extra),
        cost_estimate=pl.CostEstimate(flops=int(5e9), bytes_accessed=int(15e6), transcendentals=int(4e6)),
        name="mixers_forward",
    )(kvh, tok, gain, wq, win, stp, wsh, cosine, sine, tapx, tapb, decay, bias, skip, *feed)


def attend_back(step, kvh, q, k2, v2, lse, do, cosine, sine, cos_all, sin_all, dq_o, dkv_o, dk, dv):
    rows = q.shape[0]
    steps = k2.shape[0] // rows
    scale = HEAD_SIZE**-0.5
    low = lanes_of((rows, 128)) < HEAD_SIZE

    @pl.when(step == 0)
    def _():
        dk[...] = jnp.zeros(dk.shape, F32)
        dv[...] = jnp.zeros(dv.shape, F32)

    def back(blocks):
        n = blocks * rows
        shape = (rows, rows)
        allowed = lax.broadcasted_iota(jnp.int32, shape, 0) <= lanes_of(shape)
        qs, dos, ps, dss, dqs = [], [], [], [], []
        for h in range(2):
            mine = low == (h == 0)
            qh = jnp.where(mine, q[...], jnp.zeros_like(q[...]))
            doh = jnp.where(mine, do[...], jnp.zeros_like(do[...]))
            sc = dot_nt(k2[0:n, :], qh) * scale - lse[h : h + 1, :]
            last = jnp.where(allowed, sc[n - rows :, :], neg_large)
            sc = jnp.concatenate([sc[: n - rows, :], last], axis=0) if blocks > 1 else last
            p = jnp.exp(sc)
            dp = dot_nt(v2[0:n, :], doh)
            centre = jnp.sum(p * dp, axis=0, keepdims=True)
            ds = (p * (dp - centre)).astype(BF16)
            qs.append(qh)
            dos.append(doh)
            ps.append(p.astype(BF16))
            dss.append(ds)
            dqs.append(dot_tn(ds, k2[0:n, :]) * scale)
        dk[0:n, :] += dot_nn(jnp.concatenate(dss, axis=1), jnp.concatenate(qs, axis=0)) * scale
        dv[0:n, :] += dot_nn(jnp.concatenate(ps, axis=1), jnp.concatenate(dos, axis=0))
        dq_o[...] = turn(jnp.where(low, dqs[0], dqs[1]), cosine[...], -sine[...]).astype(BF16)

    for i in range(steps):
        pl.when(step == 2 * i)(partial(back, i + 1))

    @pl.when(step == 2 * steps - 1)
    def _():
        own = (lanes_of(dk.shape) < HEAD_SIZE) != (kvh[0] == 1)
        g = dk[...]
        g = turn(g + pltpu.roll(g, 64, 1), cos_all[...], -sin_all[...])
        dkv_o[:, 0:128] = jnp.where(own, g, 0.0).astype(BF16)
        g = dv[...]
        g = g + pltpu.roll(g, 64, 1)
        dkv_o[:, 128:256] = jnp.where(own, g, 0.0).astype(BF16)


def back_kernel(heads, channels, nt, feed, *refs):
    step = pl.program_id(0)
    if feed:
        d = lax.axis_index("dp")
        z = lax.axis_index("tensor")
        feed_in, feed_o, came, f_send, f_recv = refs[0], refs[38], refs[46], refs[47], refs[48]
        copies = [
            remote_copy(feed_in.at[k], came.at[k], f_send.at[k], f_recv.at[k], peer)
            for k, peer in enumerate(other_quarters(d, z, nt))
        ]

        @pl.when(step == 0)
        def _():
            greet(other_quarters(d, z, nt))
            for copy in copies:
                copy.start()

        refs = refs[1:38] + refs[39:46]
    attend_back(step, *refs[:10], *refs[27:29], *refs[37:39])
    scan_back(heads, channels, step, *refs[10:27], *refs[29:37], *refs[39:44])
    if feed:

        @pl.when(step == pl.num_programs(0) - 1)
        def _():
            total = None
            for k, copy in enumerate(copies):
                copy.wait()
                value = came[k].astype(F32)
                total = value if total is None else total + value
            feed_o[...] = total


def scan_back(
    heads, channels, step, dm, y, zr, xr, xp, br, bp, trow, states, rsum, dots, gain, tapx, tapb, decay,
    bias, skip,
    dz_o, dx_o, db_o, dt_o, gx_o, gb_o, gm_o, gh_o,
    xs, bs, dxs, dbs, dstate,
):
    last_step = pl.num_programs(0) - 1
    first = step == last_step
    rows = block_len
    inner = heads * SSM_DIM
    n_state = br.shape[1] // 2

    @pl.when(step == 0)
    def _():
        dxs[rows : rows + 8, :] = jnp.zeros((8, inner), F32)
        dbs[rows : rows + 8, :] = jnp.zeros((8, 2 * n_state), F32)
        dstate[...] = jnp.zeros(dstate.shape, F32)
        gx_o[...] = jnp.zeros(gx_o.shape, F32)
        gb_o[...] = jnp.zeros(gb_o.shape, F32)
        gm_o[...] = jnp.zeros(gm_o.shape, F32)
        gh_o[...] = jnp.zeros(gh_o.shape, F32)

    xs[0:8, :] = jnp.where(first, 0.0, xp[...])
    bs[0:8, :] = jnp.where(first, 0.0, bp[...])
    xs[8 : 8 + rows, :] = xr[...]
    bs[8 : 8 + rows, :] = br[...]
    ux = conv_rows(xs, tapx, 5, rows)
    sx = sigmoid(ux)
    x = ux * sx
    ub = conv_rows(bs, tapb, 5, rows)
    sb = sigmoid(ub)
    bc = (ub * sb).astype(BF16)
    b_low, c_low = bc[:, :n_state], bc[:, n_state:]

    pre = trow[...] + bias[...]
    dt = softplus(pre)
    cum = running_sum(dt * decay[...])
    end = cum[:, rows - 1 :]
    fade = jnp.exp(end - cum)
    inv = lax.rsqrt(rsum[...] / channels + epsilon)
    cols = stack_columns(
        [cum, jnp.exp(cum), dt * fade, dt, inv, inv * inv * inv * dots[...] / channels]
    )
    r = cols[:, 32:33]
    kk = cols[:, 40:41]
    z = zr[...]
    sz = sigmoid(z)
    silu_z = z * sz
    yv = y[...]
    w = yv * silu_z
    dmv = dm[...]
    dw = r * gain[...] * dmv - w * kk
    gm_o[0:1, :] += jnp.sum(dmv * w * r, axis=0, keepdims=True)
    dy = dw * silu_z
    dz_o[...] = (dw * yv * sz * (1.0 + z * (1.0 - sz))).astype(BF16)
    gm_o[1:2, :] += jnp.sum(dy * x, axis=0, keepdims=True)

    grow = widen(cols, 8, heads)
    tail = widen(cols, 16, heads)
    dt_wide = widen(cols, 24, heads)
    x_low = x.astype(BF16)
    dy_low = dy.astype(BF16)
    state = states[0]
    state_low = state.astype(BF16)
    ds = dstate[...]
    ds_low = ds.astype(BF16)
    cross = dot_nt(b_low, c_low)
    shape = (rows, rows)
    upper = lax.broadcasted_iota(jnp.int32, shape, 0) <= lanes_of(shape)
    half = lanes_of(shape) < SSM_DIM
    lane = lanes_of(shape)
    dcross = jnp.zeros(shape, F32)
    col_sums = jnp.zeros(shape, F32)
    row_sums = []
    mids = []
    for p in range(heads // 2):
        span = slice(128 * p, 128 * p + 128)
        xpair, dypair = x_low[:, span], dy_low[:, span]
        zero = jnp.zeros_like(xpair)
        dys = (jnp.where(half, dypair, zero), jnp.where(half, zero, dypair))
        mats = []
        for k in range(2):
            h = 2 * p + k
            gap = jnp.where(upper, cum[h : h + 1, :] - cols[:, h : h + 1], neg_large)
            faded = jnp.exp(gap)
            mats.append((cross * faded).astype(BF16))
            t = dot_nt(xpair, dys[k]) * faded
            dt_col = cols[:, 24 + h : 25 + h]
            td = t * dt_col
            dcross = dcross + td
            row_sums.append(jnp.sum(td * cross, axis=0, keepdims=True))
            col = jnp.sum(t * cross, axis=1, keepdims=True)
            col_sums = jnp.where(lane == h, col, col_sums)
        mids.append(dot_nn(jnp.concatenate(mats, axis=1), jnp.concatenate(dys, axis=0)))
    mid = jnp.concatenate(mids, axis=1)
    row_sums = jnp.concatenate(row_sums + [jnp.zeros((8 - heads, rows), F32)], axis=0)
    col_sums = col_sums.T[0:8, :]

    dye = dy * grow
    dye_low = dye.astype(BF16)
    xd = x * tail
    xd_low = xd.astype(BF16)
    from_b = dot_nn(b_low, ds_low)
    through = dot_nn(c_low, state_low)
    dcross_low = dcross.astype(BF16)
    db = dot_nn(dcross_low, c_low) + dot_nt(xd_low, ds_low)
    dc = dot_tn(dcross_low, b_low) + dot_nt(dye_low, state_low)

    head_of = lax.broadcasted_iota(jnp.int32, (8, inner), 0)
    chan = lanes_of((8, inner)) // SSM_DIM
    ones = jnp.where(head_of == chan, 1.0, 0.0).astype(BF16)

    def by_head(v):
        high = v.astype(BF16)
        rest = (v - high.astype(F32)).astype(BF16)
        return dot_nt(ones, high) + dot_nt(ones, rest)

    grown = by_head(dye * through)
    ended = by_head(x * from_b)
    kept = jnp.sum(ds * state, axis=0, keepdims=True) * grow[rows - 1 :, :]
    kept = jnp.where(head_of == chan, kept, 0.0).sum(axis=1, keepdims=True)
    pulled = dt * fade * ended
    lane8 = lanes_of((8, rows))
    at_end = kept + jnp.sum(pulled, axis=1, keepdims=True)
    dcum = row_sums - dt * col_sums + grown - pulled + jnp.where(lane8 == rows - 1, at_end, 0.0)
    da = running_sum_back(dcum)
    ddt = col_sums + fade * ended + decay[...] * da
    dpre = ddt * sigmoid(pre)
    dt_o[...] = dpre
    gh_o[0:8, :] += da * dt * decay[...]
    gh_o[8:16, :] += dpre

    dstate[...] = grow[rows - 1 :, :] * ds + dot_tn(c_low, dye_low)
    dx = skip[...] * dy + dt_wide * mid + tail * from_b
    dux = dx * sx * (1.0 + ux * (1.0 - sx))
    dub = jnp.concatenate([db, dc], axis=1) * sb * (1.0 + ub * (1.0 - sb))
    for taps, src, d, buf, acc, out in (
        (tapx, xs, dux, dxs, gx_o, dx_o),
        (tapb, bs, dub, dbs, gb_o, db_o),
    ):
        buf[0:rows, :] = d
        total = taps[CONV - 1 : CONV, :] * d
        for j in range(CONV - 1):
            total = total + taps[j : j + 1, :] * buf[pl.ds(CONV - 1 - j, rows), :]
        out[...] = total.astype(BF16)
        for j in range(CONV):
            acc[j : j + 1, :] += jnp.sum(d * src[pl.ds(5 + j, rows), :], axis=0, keepdims=True)
        acc[CONV : CONV + 1, :] += jnp.sum(d, axis=0, keepdims=True)
        buf[rows : rows + 8, :] = d[0:8, :]


def mixers_back(
    heads, channels, nt, kvh, q, k2, v2, lse, do, cosine, sine, dm, y, zr, xr, br, trow, states, rsum, dots,
    gain, tapx, tapb, decay, bias, skip, feed=None,
):
    total, inner = y.shape
    pair = br.shape[1]
    rows = block_len
    steps = total // rows
    per = rows // 8
    q_rows = 2 * rows

    def whole(v):
        return pl.BlockSpec(v.shape, lambda i: (0,) * v.ndim)

    def tall(n):
        return pl.BlockSpec((rows, n), lambda i: (steps - 1 - i, 0))

    def before(n):
        return pl.BlockSpec((8, n), lambda i: (jnp.maximum((steps - 1 - i) * per - 1, 0), 0))

    wide = pl.BlockSpec((8, rows), lambda i: (0, steps - 1 - i))
    ask = pl.BlockSpec((q_rows, 128), lambda i: (i // 2, 0))
    sds = jax.ShapeDtypeStruct

    def fixed(*shape):
        return pl.BlockSpec(shape, lambda i: (0,) * len(shape))

    in_specs = [pl.BlockSpec(memory_space=pltpu.SMEM), ask, whole(k2), whole(v2),
                pl.BlockSpec((8, q_rows), lambda i: (0, i // 2)), ask, ask, ask, whole(cosine), whole(sine),
                tall(inner), tall(inner), tall(inner), tall(inner), before(inner), tall(pair),
                before(pair), wide, pl.BlockSpec((1, pair // 2, inner), lambda i: (steps - 1 - i, 0, 0)),
                wide, wide, whole(gain), whole(tapx), whole(tapb), whole(decay), whole(bias), whole(skip)]
    out_specs = [ask, fixed(total, 256), tall(inner), tall(inner), tall(pair), wide, fixed(8, inner),
                 fixed(8, pair), fixed(8, inner), fixed(16, rows)]
    out_shape = [sds((total, 128), BF16), sds((total, 256), BF16), sds((total, inner), BF16),
                 sds((total, inner), BF16), sds((total, pair), BF16), sds((8, total), F32),
                 sds((8, inner), F32), sds((8, pair), F32), sds((8, inner), F32), sds((16, rows), F32)]
    scratch = [pltpu.VMEM((total, 128), F32), pltpu.VMEM((total, 128), F32),
               pltpu.VMEM((rows + 8, inner), F32), pltpu.VMEM((rows + 8, pair), F32),
               pltpu.VMEM((rows + 8, inner), F32), pltpu.VMEM((rows + 8, pair), F32),
               pltpu.VMEM((pair // 2, inner), F32)]
    args = [kvh, q, k2, v2, lse, do, cosine, sine, cosine, sine, dm, y, zr, xr, xr, br, br, trow, states,
            rsum, dots, gain, tapx, tapb, decay, bias, skip]
    extra = {}
    if feed is not None:
        dma = pltpu.SemaphoreType.DMA
        args = [feed] + args
        in_specs = [whole(feed)] + in_specs
        out_specs = out_specs + [fixed(*feed.shape[1:])]
        out_shape = out_shape + [sds(feed.shape[1:], F32)]
        scratch = scratch + [pltpu.VMEM(feed.shape, BF16), dma((nt - 1,)), dma((nt - 1,))]
        extra = dict(collective_id=5, has_side_effects=True)
    return pl.pallas_call(
        partial(back_kernel, heads, channels, nt, feed is not None),
        grid=(steps,),
        in_specs=in_specs,
        out_specs=out_specs,
        out_shape=out_shape,
        scratch_shapes=scratch,
        compiler_params=pltpu.CompilerParams(vmem_limit_bytes=VMEM_LIMIT, **extra),
        cost_estimate=pl.CostEstimate(flops=int(6e9), bytes_accessed=int(18e6), transcendentals=int(7e6)),
        name="mixers_back",
    )(*args)


def whole_spec(v):
    return pl.BlockSpec(v.shape, lambda i: (0,) * v.ndim)


def feed_open(hid, gain, a2, a2t, acc, dacc):
    v = hid[...]
    f = lax.rsqrt(jnp.mean(v * v, axis=1, keepdims=True) + epsilon)
    low = (v * f * gain[...]).astype(BF16)
    a2[...] = low
    a2t[...] = low.T
    acc[...] = jnp.zeros(acc.shape, F32)
    dacc[...] = jnp.zeros(dacc.shape, F32)


def feed_tile(a2, cot, whid, wdown, acc, dacc):
    width = a2.shape[1]
    units = whid.shape[4]
    w_gate = whid[:, 0, 0].reshape(width, units)
    w_up = whid[:, 0, 1].reshape(width, units)
    w_down = jnp.concatenate([wdown[k, 0] for k in range(width // 128)], axis=1)
    g = dot_nn(a2[...], w_gate)
    u = dot_nn(a2[...], w_up)
    s = sigmoid(g)
    f_low = (g * s * u).astype(BF16)
    acc[...] += dot_nn(f_low, w_down)
    df = dot_nt(cot[...], w_down)
    du = (df * g * s).astype(BF16)
    dg = (df * u * s * (1.0 + g * (1.0 - s))).astype(BF16)
    dacc[...] += dot_nt(dg, w_gate) + dot_nt(du, w_up)
    return f_low, dg, du


def feed_close(hid, gain, cot, acc, dacc, out_o, dh_o, gg_o):
    v = hid[...]
    out_o[...] = (v + acc[...]).astype(BF16)
    f = lax.rsqrt(jnp.mean(v * v, axis=1, keepdims=True) + epsilon)
    dy = dacc[...]
    gg_o[...] = jnp.sum(dy * v * f, axis=0, keepdims=True)
    gdy = dy * gain[...]
    lean = jnp.sum(gdy * v, axis=1, keepdims=True) * (f * f * f / v.shape[1])
    dh = cot[...].astype(F32) + (f * gdy - v * lean)
    dh_o[...] = dh
    return dh.astype(BF16)


def feed_grads(a2t, cot, f_low, dg, du):
    blocks = a2t.shape[0] // 128
    values = []
    for grad in (dg, du):
        full = dot_nn(a2t[...], grad).astype(BF16)
        for cb in range(grad.shape[1] // 128):
            values.append(full[:, 128 * cb : 128 * cb + 128].reshape(blocks, 128, 128))
    full = dot_tn(f_low, cot[...]).astype(BF16)
    values.append(jnp.stack([full[:, 128 * k : 128 * k + 128] for k in range(blocks)]))
    return values


def piece_rows(part, units, quarter_units):
    rows = [
        (k * quarter_units + part * units + cb * 128, 128) for k in range(2) for cb in range(units // 128)
    ]
    return rows + [(2 * quarter_units + part * units, units)]


def feed_kernel(hid, gain, cot, whid, wdown, out_o, dh_o, dmix_o, gg_o, piece_o, a2, a2t, acc, dacc):
    step = pl.program_id(0)
    pl.when(step == 0)(lambda: feed_open(hid, gain, a2, a2t, acc, dacc))
    values = feed_grads(a2t, cot, *feed_tile(a2, cot, whid, wdown, acc, dacc))
    units = whid.shape[4]
    quarter_units = piece_o.shape[2] // 3
    tiles_per = quarter_units // units
    rows = piece_rows(lax.rem(step, tiles_per), units, quarter_units)
    for value, (row, n) in zip(values, rows):
        piece_o[:, step // tiles_per, pl.ds(pl.multiple_of(row, 128), n), :] = value

    @pl.when(step == pl.num_programs(0) - 1)
    def _():
        dmix_o[...] = feed_close(hid, gain, cot, acc, dacc, out_o, dh_o, gg_o)


def feed_forward(hid, gain, cot, whid, wdown):
    rows, width = hid.shape
    blocks, nt, _, depth, units = whid.shape
    tile = 256
    per = units // tile
    hid_spec = pl.BlockSpec((blocks, 1, 2, depth, tile), lambda i: (0, i // per, 0, 0, lax.rem(i, per)))
    down_spec = pl.BlockSpec((blocks, 1, tile, 128), lambda i: (0, i // per, lax.rem(i, per), 0))
    sds = jax.ShapeDtypeStruct
    piece = (blocks, nt, 3 * units, 128)

    def fixed(*shape):
        return pl.BlockSpec(shape, lambda i: (0,) * len(shape))

    return pl.pallas_call(
        feed_kernel,
        grid=(nt * per,),
        in_specs=[fixed(rows, width), fixed(1, width), fixed(rows, width), hid_spec, down_spec],
        out_specs=[fixed(rows, width), fixed(rows, width), fixed(rows, width), fixed(1, width),
                   fixed(*piece)],
        out_shape=[sds((rows, width), BF16), sds((rows, width), F32), sds((rows, width), BF16),
                   sds((1, width), F32), sds(piece, BF16)],
        scratch_shapes=[pltpu.VMEM((rows, width), BF16), pltpu.VMEM((width, rows), BF16),
                        pltpu.VMEM((rows, width), F32), pltpu.VMEM((rows, width), F32)],
        compiler_params=pltpu.CompilerParams(vmem_limit_bytes=VMEM_LIMIT),
        name="feed_forward",
    )(hid, gain, cot, whid, wdown)


def row_columns(rows_list, rows):
    return jnp.concatenate(
        [stack_columns([r[:, c : c + 128] for r in rows_list]) for c in range(0, rows, 128)], axis=0
    )


def down_rows(at, dq, dz, dx, dkv, db, drow, wq, win, stp, wsh):
    total = dot_nt(dq[at, :], wq[...]) + dot_nt(dz[at, :], win[0]) + dot_nt(dx[at, :], win[1])
    total = total + dot_nt(dkv[at, :], wsh[:, 0:256]) + dot_nt(db[at, :], wsh[:, 256:])
    return total + dot_tn(drow[:, at].astype(BF16), stp[...])


def down_kernel(dq, dz, dx, dkv, db, drow, wq, win, stp, wsh, part_o):
    every = slice(None)
    part_o[...] = down_rows(every, dq, dz, dx, dkv, db, drow, wq, win, stp, wsh).astype(BF16)


def down_parts(dq, dz, dx, dkv, db, drow, wq, win, stp, wsh):
    total, inner = dz.shape
    width = wq.shape[0]
    rows = 256

    def tall(v):
        return pl.BlockSpec((rows, v.shape[1]), lambda i: (i, 0))

    wide = pl.BlockSpec((8, rows), lambda i: (0, i))
    return pl.pallas_call(
        down_kernel,
        grid=(total // rows,),
        in_specs=[tall(dq), tall(dz), tall(dx), tall(dkv), tall(db), wide, whole_spec(wq), whole_spec(win),
                  whole_spec(stp), whole_spec(wsh)],
        out_specs=pl.BlockSpec((rows, width), lambda i: (i, 0)),
        out_shape=jax.ShapeDtypeStruct((total, width), BF16),
        compiler_params=pltpu.CompilerParams(vmem_limit_bytes=VMEM_LIMIT),
        cost_estimate=pl.CostEstimate(flops=int(3e9), bytes_accessed=int(8e6), transcendentals=0),
        name="down_parts",
    )(dq, dz, dx, dkv, db, drow, wq, win, stp, wsh)


def weight_columns(a, g, dq, dz, dx, dkv, db, ot, mt, put, put_shared):
    at = a.T
    inner = dz.shape[1]

    def by_rows(values, first):
        for j in range(values.shape[1] // 128):
            for k in range(2):
                put(k, first + 128 * j, values[128 * k : 128 * (k + 1), 128 * j : 128 * (j + 1)])

    def by_lanes(values, first):
        for k in range(2):
            put(k, first, values[:, 128 * k : 128 * (k + 1)])

    by_rows(dot_nn(at, dq[...]).astype(BF16), 0)
    by_lanes(dot_nn(ot[...], g).astype(BF16), 128)
    by_rows(dot_nn(at, dz[...]).astype(BF16), 256)
    by_rows(dot_nn(at, dx[...]).astype(BF16), 256 + inner)
    by_lanes(dot_nn(mt[...], g).astype(BF16), 256 + 2 * inner)
    for first, values in ((0, dot_nn(at, dkv[...]).astype(BF16)), (256, dot_nn(at, db[...]).astype(BF16))):
        for k in range(2):
            put_shared(k, first, values[128 * k : 128 * (k + 1)])


def weight_kernel(a1, dq, dz, dx, dkv, db, drow, o, m, dmix, piece_o, shared_o, step_o, ot, mt):
    @pl.when(pl.program_id(0) == 0)
    def _():
        ot[...] = o[...].T
        mt[...] = m[...].T

    step_o[...] = dot_nn(drow[...].astype(BF16), a1[...])

    def put(k, first, values):
        piece_o[k, first : first + values.shape[0], :] = values

    def put_shared(k, first, values):
        shared_o[k, :, first : first + values.shape[1]] = values

    weight_columns(a1[...], dmix[...], dq, dz, dx, dkv, db, ot, mt, put, put_shared)


def weight_pieces(a1, dq, dz, dx, dkv, db, drow, o, m, dmix):
    total, width = a1.shape
    inner = dz.shape[1]
    n = 256 + 3 * inner
    shared = 256 + db.shape[1]
    cols = pl.BlockSpec((total, 256), lambda i: (0, i))
    sds = jax.ShapeDtypeStruct
    args = (dq, dz, dx, dkv, db, drow, o, m)
    return pl.pallas_call(
        weight_kernel,
        grid=(width // 256,),
        in_specs=[cols] + [whole_spec(v) for v in args] + [cols],
        out_specs=[pl.BlockSpec((2, n, 128), lambda i: (i, 0, 0)),
                   pl.BlockSpec((2, 128, shared), lambda i: (i, 0, 0)),
                   pl.BlockSpec((8, 256), lambda i: (0, i))],
        out_shape=[sds((width // 128, n, 128), BF16), sds((width // 128, 128, shared), BF16),
                   sds((8, width), F32)],
        scratch_shapes=[pltpu.VMEM((128, total), BF16), pltpu.VMEM((inner, total), BF16)],
        compiler_params=pltpu.CompilerParams(vmem_limit_bytes=VMEM_LIMIT),
        cost_estimate=pl.CostEstimate(flops=int(4e9), bytes_accessed=int(12e6), transcendentals=0),
        name="weight_pieces",
    )(a1, *args, dmix)


class Exchange:
    def __init__(self, own, landed, send, recv, d, z, nt):
        self.own, self.landed, self.z, self.nt = own, landed, z, nt
        self.copies = [
            remote_copy(own, landed.at[k - 1], send.at[k - 1], recv.at[k - 1], peer)
            for k, peer in enumerate(other_quarters(d, z, nt), 1)
        ]

    def start(self):
        for copy in self.copies:
            copy.start()

    def wait(self):
        for copy in self.copies:
            copy.wait()

    def total(self):
        total = None
        for q in range(self.nt):
            value = jnp.where(self.z == q, self.own[...].astype(F32), 0.0)
            for k in range(1, self.nt):
                value = value + jnp.where(
                    lax.rem(self.z - k + self.nt, self.nt) == q, self.landed[k - 1].astype(F32), 0.0
                )
            total = value if total is None else total + value
        return total


class ChainScatter:
    def __init__(self, parts, bufs, landed, send, recv, d, z, nt):
        self.parts, self.bufs, self.landed = parts, bufs, landed
        self.send, self.recv = send, recv
        self.d, self.z, self.nt = d, z, nt

    def active(self, way, t):
        z, nt = self.z, self.nt
        if way == 0:
            return (z <= t) & (z < nt - 1)
        return (nt - 1 - z <= t) & (z > 0)

    def copy(self, way, t):
        dev = (self.d, self.z + 1 if way == 0 else self.z - 1)
        return remote_copy(
            self.bufs.at[way, t], self.landed.at[way, t], self.send.at[way, t], self.recv.at[way, t], dev
        )

    def arrives(self, way, t):
        z, nt = self.z, self.nt
        if way == 0:
            return (z >= 1) & (z - 1 <= t)
        return (z < nt - 1) & (nt - 2 - z <= t)

    def step(self, t):
        z, nt = self.z, self.nt
        for way in range(2):
            q = nt - 1 - t + z if way == 0 else t - (nt - 1) + z

            def run():
                value = self.parts[q]
                if t > 0:
                    came = self.arrives(way, t - 1)

                    @pl.when(came)
                    def _():
                        self.copy(way, t - 1).wait_recv()
                        total = value.astype(F32) + self.landed[way, t - 1].astype(F32)
                        self.bufs[way, t] = total.astype(BF16)

                    @pl.when(jnp.logical_not(came))
                    def _():
                        self.bufs[way, t] = value
                else:
                    self.bufs[way, t] = value
                self.copy(way, t).start()

            pl.when(self.active(way, t))(run)

    def finish(self, out):
        out[...] = self.parts[self.z].astype(F32)
        t = self.nt - 2
        for way in range(2):

            @pl.when(self.arrives(way, t))
            def _():
                self.copy(way, t).wait_recv()
                out[...] += self.landed[way, t].astype(F32)

    def drain(self):
        for way in range(2):
            for t in range(self.nt - 1):
                pl.when(self.active(way, t))(self.copy(way, t).wait_send)


def chain_scratch(nt, rows, width):
    dma = pltpu.SemaphoreType.DMA
    return [
        pltpu.VMEM((2, nt - 1, rows, width), BF16),
        pltpu.VMEM((2, nt - 1, rows, width), BF16),
        dma((2, nt - 1)),
        dma((2, nt - 1)),
    ]


def mix_scatter_kernel(channels, nt, feed, *refs):
    (o, y, z_in, sq, gain, watt, wmam, tok), refs = refs[:8], refs[8:]
    if feed:
        (hid_z, dwn_z), refs = refs[2:4], refs[4:]
        (m_o, sq_o, hid_o, hid_f, dwn_f), refs = refs[:5], refs[5:]
        (lsem, f_send, f_recv), refs = refs[:3], refs[3:]
    else:
        (m_o, sq_o, hid_o), refs = refs[:3], refs[3:]
    (sq_land, sq_send, sq_recv, parts, bufs, landed, c_send, c_recv) = refs
    d = lax.axis_index("dp")
    z = lax.axis_index("tensor")
    rows = tok.shape[0]
    peers = [(p, z) for p in cube_peers(d)] if feed else []
    greet(peers + other_quarters(d, z, nt))
    squares = Exchange(sq, sq_land, sq_send, sq_recv, d, z, nt)
    squares.start()
    n = 2 * (nt - 1)
    if feed:
        items = []
        for k in range(1, nt):
            q = lax.rem(z - k + nt, nt)
            items.append((hid_z.at[q], lambda s, q=q: hid_f.at[s, q]))
            items.append((dwn_z.at[q], lambda s, q=q: dwn_f.at[s, q]))
        cube = CubeGather(items, (0, 3, 4), f_send, f_recv, d, z)
        for i in range(n):
            cube.start(i)
        locals_ = []
        for i, (src, dst) in enumerate([(src, at(d)) for src, at in items]):
            locals_.append(pltpu.make_async_copy(src, dst, lsem.at[i]))
            locals_[-1].start()
    chain = ChainScatter(parts, bufs, landed, c_send, c_recv, d, z, nt)
    squares.wait()
    sq_o[...] = squares.total()

    def part(q):
        at = pl.ds(pl.multiple_of(q * rows, rows), rows)
        total = sq_o[:, at]
        r = row_columns([lax.rsqrt(total / channels + epsilon)], rows)[:, 0:1]
        zv = z_in[at, :]
        m = (y[at, :] * (zv * sigmoid(zv)) * r * gain[...]).astype(BF16)
        m_o[at, :] = m
        parts[q] = (dot_nn(o[at, :], watt[...]) + dot_nn(m, wmam[...])).astype(BF16)

    first = jnp.where(z < nt // 2, nt - 1, 0)
    part(first)
    chain.step(0)

    def rest(i, carry):
        part(lax.rem(first + 1 + i, nt))
        return carry

    lax.fori_loop(0, nt - 1, rest, 0)
    if feed:
        cube.near(0)
        cube.near(1)
    for t in range(1, nt - 1):
        chain.step(t)
        if feed:
            cube.near(2 * t)
            cube.near(2 * t + 1)
            cube.far(2 * t - 2)
            cube.far(2 * t - 1)
    if feed:
        cube.far(n - 2)
        cube.far(n - 1)
    chain.finish(hid_o)
    hid_o[...] += tok[...].astype(F32)
    chain.drain()
    if feed:
        cube.finish()
        for copy in locals_:
            copy.wait()


def mix_scatter(channels, nt, o, y, zr, sq, gain, watt, wmam, tok, feed=()):
    total, inner = y.shape
    rows, width = tok.shape
    dma = pltpu.SemaphoreType.DMA
    sds = jax.ShapeDtypeStruct
    vmem = pl.BlockSpec(memory_space=pltpu.VMEM)
    anywhere = pl.BlockSpec(memory_space=pl.ANY)
    outs = [sds((total, inner), BF16), sds((8, total), F32), sds((rows, width), F32)]
    scratch = []
    n = 2 * (nt - 1)
    if feed:
        for v in feed[:2]:
            outs.append(sds(v.shape, BF16))
        scratch = [dma((n,)), dma((n, 7)), dma((n, 7))]
    return pl.pallas_call(
        partial(mix_scatter_kernel, channels, nt, bool(feed)),
        in_specs=[vmem] * 8 + [anywhere] * len(feed[:2]) + [vmem] * len(feed[2:]),
        out_specs=[vmem] * 3 + [anywhere] * (len(outs) - 3),
        out_shape=outs,
        input_output_aliases={8: 3, 9: 4} if feed else {},
        scratch_shapes=scratch + [pltpu.VMEM((nt - 1, 8, total), F32), dma((nt - 1,)), dma((nt - 1,)),
                        pltpu.VMEM((nt, rows, width), BF16)] + chain_scratch(nt, rows, width),
        compiler_params=pltpu.CompilerParams(
            vmem_limit_bytes=VMEM_LIMIT, collective_id=1, has_side_effects=True
        ),
        cost_estimate=pl.CostEstimate(flops=int(1e9), bytes_accessed=int(130e6), transcendentals=int(4e5)),
        name="mix_scatter",
    )(o, y, zr, sq, gain, watt, wmam, tok, *feed)


class ChainGather:
    def __init__(self, own, slots, send, recv, d, z, nt):
        self.own, self.slots, self.send, self.recv = own, slots, send, recv
        self.d, self.z, self.nt = d, z, nt

    def copy(self, way, dist):
        dev = (self.d, self.z + 1 if way == 0 else self.z - 1)
        slot = self.z - dist if way == 0 else self.z + dist
        src = self.own if dist == 0 else self.slots.at[slot]
        return remote_copy(src, self.slots.at[slot], self.send.at[way, dist], self.recv.at[way, dist], dev)

    def landing(self, way, dist):
        slot = self.z - dist if way == 0 else self.z + dist
        return remote_copy(
            self.slots.at[slot], self.slots.at[slot], self.send.at[way, dist - 1],
            self.recv.at[way, dist - 1], (self.d, self.z),
        )

    def has(self, way, dist):
        return self.z >= dist if way == 0 else self.z + dist < self.nt

    def goes_on(self, way):
        return self.z < self.nt - 1 if way == 0 else self.z > 0

    def start(self):
        for way in range(2):
            pl.when(self.goes_on(way))(self.copy(way, 0).start)

    def hop(self, dist):
        for way in range(2):
            pl.when(self.has(way, dist))(self.landing(way, dist).wait_recv)
            if dist < self.nt - 1:
                pl.when(self.has(way, dist) & self.goes_on(way))(self.copy(way, dist).start)

    def drain(self):
        for way in range(2):
            pl.when(self.goes_on(way))(self.copy(way, 0).wait_send)
            for dist in range(1, self.nt - 1):
                pl.when(self.has(way, dist) & self.goes_on(way))(self.copy(way, dist).wait_send)


class Unmix:
    def __init__(self, y, z_in, gain, watt, wmam, g_o, do_o, dm_o, dots, rows):
        self.ins = (y, z_in, gain, watt, wmam)
        self.outs = (g_o, do_o, dm_o, dots)
        self.rows = rows

    def __call__(self, q, g):
        y, z_in, gain, watt, wmam = self.ins
        g_o, do_o, dm_o, dots_o = self.outs
        rows = self.rows
        at = pl.ds(pl.multiple_of(q * rows, rows), rows)
        g_o[at, :] = g
        do_o[at, :] = dot_nt(g, watt[...]).astype(BF16)
        dm = dot_nt(g, wmam[...])
        dm_o[at, :] = dm
        zv = z_in[at, :]
        dots = jnp.sum(dm * gain[...] * (y[at, :] * (zv * sigmoid(zv))), axis=1, keepdims=True)
        turned = [jnp.broadcast_to(dots[c : c + 128], (128, 128)).T[0:8, :] for c in range(0, rows, 128)]
        dots_o[:, at] = jnp.concatenate(turned, axis=1)

    def around(self, z, dist, nt, slots):
        def side(way, carry):
            q = jnp.where(way == 0, z - dist, z + dist)

            @pl.when((q >= 0) & (q < nt))
            def _():
                self(q, slots[q])

            return carry

        lax.fori_loop(0, 2, side, 0)


def unmix_gather_kernel(nt, *refs):
    (dmix, y, z_in, gain, watt, wmam), refs = refs[:6], refs[6:]
    (g_o, do_o, dm_o, dot_o), refs = refs[:4], refs[4:]
    (slots, g_send, g_recv, dot_own, dot_land, d_send, d_recv) = refs
    d = lax.axis_index("dp")
    z = lax.axis_index("tensor")
    greet(other_quarters(d, z, nt))
    chain = ChainGather(dmix, slots, g_send, g_recv, d, z, nt)
    chain.start()
    work = Unmix(y, z_in, gain, watt, wmam, g_o, do_o, dm_o, dot_own, dmix.shape[0])
    work(z, dmix[...])
    for dist in range(1, nt):
        chain.hop(dist)
        work.around(z, dist, nt, slots)
    dots = Exchange(dot_own, dot_land, d_send, d_recv, d, z, nt)
    dots.start()
    chain.drain()
    dots.wait()
    dot_o[...] = dots.total()


def unmix_shapes(total, width, inner):
    sds = jax.ShapeDtypeStruct
    return [sds((total, width), BF16), sds((total, 128), BF16), sds((total, inner), F32),
            sds((8, total), F32)]


def unmix_scratch(nt, rows, width, total):
    dma = pltpu.SemaphoreType.DMA
    return [pltpu.VMEM((nt, rows, width), BF16), dma((2, nt - 1)), dma((2, nt - 1)),
            pltpu.VMEM((8, total), F32), pltpu.VMEM((nt - 1, 8, total), F32), dma((nt - 1,)), dma((nt - 1,))]


def unmix_gather(nt, dmix, y, zr, gain, watt, wmam):
    total, inner = y.shape
    rows, width = dmix.shape
    vmem = pl.BlockSpec(memory_space=pltpu.VMEM)
    return pl.pallas_call(
        partial(unmix_gather_kernel, nt),
        in_specs=[vmem] * 6,
        out_specs=[vmem] * 4,
        out_shape=unmix_shapes(total, width, inner),
        scratch_shapes=unmix_scratch(nt, rows, width, total),
        compiler_params=pltpu.CompilerParams(
            vmem_limit_bytes=VMEM_LIMIT, collective_id=2, has_side_effects=True
        ),
        name="unmix_gather",
    )(dmix, y, zr, gain, watt, wmam)


BOXES = 4


def feed_unmix_kernel(nt, *refs):
    (hid, gain, cot, whid, wdown, y, z_in, mgain, watt, wmam), refs = refs[:10], refs[10:]
    (out_o, dh_o, gg_o, g_o, do_o, dm_o, dot_o, own_o, sum_o), refs = refs[:9], refs[9:]
    (a2, a2t, acc, dacc, fs, dgs, dus, dmix, piece, sent, came, b_send, b_recv), refs = refs[:13], refs[13:]
    boxes, refs = refs[: 8 * (nt - 1)], refs[8 * (nt - 1) :]
    (slots, g_send, g_recv, dot_own, dot_land, d_send, d_recv) = refs
    step = pl.program_id(0)
    tiles = pl.num_programs(0) // 2
    d = lax.axis_index("dp")
    z = lax.axis_index("tensor")
    core = lax.rem(d, 2)
    bits = dp_bits(d)
    peers = cube_peers(d)
    chain = ChainGather(dmix, slots, g_send, g_recv, d, z, nt)
    cubes = []
    for k in range(1, nt):
        q = lax.rem(z + k, nt)
        box = boxes[8 * k - 8 : 8 * k]
        cubes.append(
            SquareScatter(lambda i, j, q=q: (2 * i + j, q), piece, box[:6], box[6], box[7], peers, bits, z)
        )

    @pl.when(step == 0)
    def _():
        greet([(p, z) for p in peers] + other_quarters(d, z, nt))
        feed_open(hid, gain, a2, a2t, acc, dacc)

    @pl.when(step < tiles)
    def _():
        fs[step], dgs[step], dus[step] = feed_tile(a2, cot, whid, wdown, acc, dacc)

    @pl.when(step == tiles - 1)
    def _():
        dmix[...] = feed_close(hid, gain, cot, acc, dacc, out_o, dh_o, gg_o)
        chain.start()

    units = whid.shape[4]
    quarter_units = piece.shape[2] // 3
    tiles_per = quarter_units // units

    def swap(turn_):
        box = lax.rem(turn_, BOXES)
        return remote_copy(
            sent.at[box], came.at[box], b_send.at[box], b_recv.at[box], (peers[0], z)
        )

    def places(turn_):
        quarter = lax.rem(z + 1 + turn_ // tiles_per, nt)
        part = lax.rem(turn_, tiles_per)
        return quarter, part, piece_rows(part, units, quarter_units)

    def take(turn_):
        swap(turn_).wait_recv()
        quarter, _, rows = places(turn_)
        box = lax.rem(turn_, BOXES)
        first = 0
        for row, n in rows:
            at = pl.ds(pl.multiple_of(row, 128), n)
            piece[:, quarter, at, :] = add_refs(
                piece[:, quarter, at, :], came[box, :, first : first + n, :]
            ).astype(BF16)
            first += n

    @pl.when(step >= tiles)
    def _():
        turn_ = step - tiles
        quarter, part, rows = places(turn_)
        tile = quarter * tiles_per + part
        box = lax.rem(turn_, BOXES)
        pl.when(turn_ >= BOXES)(lambda: swap(turn_ - BOXES).wait_send())
        first = 0
        for value, (row, n) in zip(feed_grads(a2t, cot, fs[tile], dgs[tile], dus[tile]), rows):
            at = pl.ds(pl.multiple_of(row, 128), n)
            value = value.reshape(value.shape[0] // 2, 2, n, 128)
            even, odd = value[:, 0], value[:, 1]
            piece[:, quarter, at, :] = jnp.where(core == 0, even, odd)
            sent[box, :, first : first + n, :] = jnp.where(core == 0, odd, even)
            first += n
        swap(turn_).start()
        pl.when(turn_ >= 1)(lambda: take(turn_ - 1))
        for k in range(1, nt):
            pl.when(turn_ == k * tiles_per)(cubes[k - 1].start)

    @pl.when(step == 2 * tiles - 1)
    def _():
        take(tiles - 1)
        for i in range(BOXES):
            swap(tiles - BOXES + i).wait_send()
        own_o[...] = piece[:, z]
        work = Unmix(y, z_in, mgain, watt, wmam, g_o, do_o, dm_o, dot_own, hid.shape[0])
        work(z, dmix[...])
        for dist in range(1, nt):
            chain.hop(dist)
            work.around(z, dist, nt, slots)
            if dist == 1:
                cubes[0].middle()
            if dist < nt - 1:
                cubes[dist].middle()
            elif dist == nt - 1:
                dots = Exchange(dot_own, dot_land, d_send, d_recv, d, z, nt)
                dots.start()
        for k, cube in enumerate(cubes):
            cube.finish(sum_o.at[k])
        chain.drain()
        for cube in cubes:
            cube.drain()
        dots.wait()
        dot_o[...] = dots.total()


def feed_unmix(nt, hid, gain, cot, whid, wdown, y, zr, mgain, watt, wmam):
    rows, width = hid.shape
    total, inner = y.shape
    blocks, _, _, depth, units = whid.shape
    tile = 256
    per = units // tile
    tiles = nt * per
    kept = blocks // 2
    n = 3 * units
    dma = pltpu.SemaphoreType.DMA
    sds = jax.ShapeDtypeStruct

    def fixed(v):
        return pl.BlockSpec(v.shape, lambda i: (0,) * len(v.shape), pipeline_mode=pl.Buffered(1))

    def at_tile(i):
        return jnp.minimum(i, tiles - 1)

    hid_spec = pl.BlockSpec(
        (blocks, 1, 2, depth, tile), lambda i: (0, at_tile(i) // per, 0, 0, lax.rem(at_tile(i), per))
    )
    down_spec = pl.BlockSpec(
        (blocks, 1, tile, 128), lambda i: (0, at_tile(i) // per, lax.rem(at_tile(i), per), 0)
    )
    out_shape = [sds((rows, width), BF16), sds((rows, width), F32), sds((1, width), F32)]
    out_shape += unmix_shapes(total, width, inner)
    out_shape += [sds((kept, n, 128), BF16), sds((nt - 1, n, 128), BF16)]
    box = pltpu.VMEM((BOXES, kept, 3 * tile, 128), BF16)
    kept_tile = pltpu.VMEM((tiles, rows, tile), BF16)
    scratch = [pltpu.VMEM((rows, width), BF16), pltpu.VMEM((width, rows), BF16),
               pltpu.VMEM((rows, width), F32), pltpu.VMEM((rows, width), F32), kept_tile, kept_tile, kept_tile,
               pltpu.VMEM((rows, width), BF16), pltpu.VMEM((kept, nt, n, 128), BF16), box, box, dma((BOXES,)),
               dma((BOXES,))]
    for _ in range(nt - 1):
        scratch += square_scratch(n, 128)
    return pl.pallas_call(
        partial(feed_unmix_kernel, nt),
        grid=(2 * tiles,),
        in_specs=[fixed(hid), fixed(gain), fixed(cot), hid_spec, down_spec, fixed(y), fixed(zr), fixed(mgain),
                  fixed(watt), fixed(wmam)],
        out_specs=[fixed(v) for v in out_shape],
        out_shape=out_shape,
        scratch_shapes=scratch + unmix_scratch(nt, rows, width, total),
        compiler_params=pltpu.CompilerParams(
            vmem_limit_bytes=60 * 1024 * 1024, collective_id=4, has_side_effects=True
        ),
        cost_estimate=pl.CostEstimate(flops=int(1e10), bytes_accessed=int(150e6), transcendentals=int(9e5)),
        name="feed_unmix",
    )(hid, gain, cot, whid, wdown, y, zr, mgain, watt, wmam)


def add_refs(left, right):
    return left.astype(F32) + right.astype(F32)


class SquareScatter:
    def __init__(self, place, held, bufs, send, recv, peers, bits, z):
        (self.r1, self.r2, self.ob, self.tb, self.r3, self.r4) = bufs
        self.place, self.held = place, held
        n = held.shape[-2]
        half = n // 2
        self.lo, self.hi = pl.ds(0, half), pl.ds(half, n - half)
        self.half = half
        _, self.x, self.y = bits
        x, y = self.x, self.y
        _, d_x, d_y = peers
        self.copies = []
        for i in range(2):
            self.copies.append(
                remote_copy(held.at[place(i, 1 - x) + (self.lo,)], self.r1.at[i], send.at[i], recv.at[i],
                            (d_x, z))
            )
        for j in range(2):
            self.copies.append(
                remote_copy(held.at[place(1 - y, j) + (self.hi,)], self.r2.at[j], send.at[2 + j],
                            recv.at[2 + j], (d_y, z))
            )
        self.copies.append(remote_copy(self.ob.at[1 - y], self.r3, send.at[4], recv.at[4], (d_y, z)))
        self.copies.append(remote_copy(self.tb.at[1 - x], self.r4, send.at[5], recv.at[5], (d_x, z)))

    def start(self):
        for copy in self.copies[:4]:
            copy.start()

    def middle(self):
        for i in range(2):
            self.copies[i].wait_recv()
            self.ob[i] = add_refs(self.held[self.place(i, self.x) + (self.lo,)], self.r1[i]).astype(BF16)
        self.copies[4].start()
        for j in range(2):
            self.copies[2 + j].wait_recv()
            self.tb[j] = add_refs(self.held[self.place(self.y, j) + (self.hi,)], self.r2[j]).astype(BF16)
        self.copies[5].start()

    def finish(self, out):
        self.copies[4].wait_recv()
        out[0 : self.half] = add_refs(self.ob[self.y], self.r3[...]).astype(out.dtype)
        self.copies[5].wait_recv()
        out[self.half :] = add_refs(self.tb[self.x], self.r4[...]).astype(out.dtype)

    def drain(self):
        for copy in self.copies:
            copy.wait_send()


def square_scratch(n, lanes):
    dma = pltpu.SemaphoreType.DMA
    half = n // 2
    return [
        pltpu.VMEM((2, half, lanes), BF16),
        pltpu.VMEM((2, n - half, lanes), BF16),
        pltpu.VMEM((2, half, lanes), BF16),
        pltpu.VMEM((2, n - half, lanes), BF16),
        pltpu.VMEM((half, lanes), BF16),
        pltpu.VMEM((n - half, lanes), BF16),
        dma((6,)),
        dma((6,)),
    ]


class CubeScatter:
    def __init__(self, pieces, bufs, peers, bits, z):
        (self.rc, self.held, send, recv) = bufs[:4]
        self.p = pieces
        self.core = bits[0]
        self.first = remote_copy(
            pieces.at[:, 1 - self.core], self.rc, send.at[0], recv.at[0], (peers[0], z)
        )
        self.square = SquareScatter(
            lambda i, j: (2 * i + j,), self.held, bufs[4:10], bufs[10], bufs[11], peers, bits, z
        )

    def start(self):
        self.first.start()

    def middle(self):
        self.first.wait_recv()
        for i in range(4):
            self.held[i] = add_refs(self.p[i, self.core], self.rc[i]).astype(BF16)
        self.square.start()

    def last(self):
        self.square.middle()

    def finish(self, out):
        self.square.finish(out)

    def drain(self):
        self.first.wait_send()
        self.square.drain()


def cube_scratch(n, lanes):
    dma = pltpu.SemaphoreType.DMA
    return [
        pltpu.VMEM((4, n, lanes), BF16),
        pltpu.VMEM((4, n, lanes), BF16),
        dma((1,)),
        dma((1,)),
    ] + square_scratch(n, lanes)


class CubeTotal:
    def __init__(self, held, landed, send, recv, peers, z):
        self.held, self.landed = held, landed
        self.copies = [
            remote_copy(held.at[i], landed.at[i], send.at[i], recv.at[i], (peer, z))
            for i, peer in enumerate(peers)
        ]

    def start(self, i):
        self.copies[i].start()

    def take(self, i):
        self.copies[i].wait_recv()
        self.held[i + 1] = self.held[i] + self.landed[i]

    def drain(self):
        for copy in self.copies:
            copy.wait_send()


def norm_back(dy, tok, gain, dh, out, ggain):
    v = tok[...].astype(F32)
    width = v.shape[1]
    f = lax.rsqrt(jnp.mean(v * v, axis=1, keepdims=True) + epsilon)
    ggain(jnp.sum(dy * v * f, axis=0, keepdims=True))
    gdy = dy * gain[...]
    lean = jnp.sum(gdy * v, axis=1, keepdims=True) * (f * f * f / width)
    out[...] = (dh[...] + (f * gdy - v * lean)).astype(BF16)


SMALL_ALL = 24
SMALL_ROWS = 152


def tail_kernel(
    nt, tok, gain, dh, a1, dmix, o, m, dq, dz, dx, dkv, db, drow, wq, win, stp, wsh,
    gg, gtb, gtx, grows, gheads, feed_own, feed_rest,
    gt_o, mixed_o, fed_o, sh_o, small_o, norm_o,
    da, parts, pieces, shared, ot, mt, bufs, landed, c_send, c_recv, *rest,
):
    cube_a, rest = rest[:12], rest[12:]
    cube_b, rest = rest[:12], rest[12:]
    square_c, rest = rest[:8], rest[8:]
    (sh_sum, sh_land, sh_send, sh_recv) = rest[:4]
    (sm_held, sm_land, sm_send, sm_recv, all_own, all_land, all_send, all_recv) = rest[4:12]
    (ng_held, ng_land, ng_send, ng_recv, ngz_land, ngz_send, ngz_recv) = rest[12:]
    d = lax.axis_index("dp")
    z = lax.axis_index("tensor")
    bits = dp_bits(d)
    peers = cube_peers(d)
    rows = tok.shape[0]
    greet([(p, z) for p in peers] + other_quarters(d, z, nt))
    three = SquareScatter(
        lambda i, j: (i, j), feed_own, square_c[:6], square_c[6], square_c[7], peers, bits, z
    )
    three.start()
    chain = ChainScatter(parts, bufs, landed, c_send, c_recv, d, z, nt)

    def part(q):
        at = pl.ds(pl.multiple_of(q * rows, rows), rows)
        parts[q] = down_rows(at, dq, dz, dx, dkv, db, drow, wq, win, stp, wsh).astype(BF16)

    first = jnp.where(z < nt // 2, nt - 1, 0)
    part(first)
    chain.step(0)

    def others(i, carry):
        part(lax.rem(first + 1 + i, nt))
        return carry

    lax.fori_loop(0, nt - 1, others, 0)
    ot[...] = o[...].T
    mt[...] = m[...].T

    def columns(i, carry):
        at = pl.ds(pl.multiple_of(i * 256, 256), 256)

        def put(k, first, values):
            pieces[i, k, first : first + values.shape[0], :] = values

        def put_shared(k, first, values):
            shared[i, k, :, first : first + values.shape[1]] = values

        weight_columns(a1[:, at], dmix[:, at], dq, dz, dx, dkv, db, ot, mt, put, put_shared)
        return carry

    lax.fori_loop(0, 2, columns, 0)
    chain.step(1)
    lax.fori_loop(2, 4, columns, 0)
    one = CubeScatter(pieces, cube_a, peers, bits, z)
    two = CubeScatter(shared, cube_b, peers, bits, z)
    sums = CubeTotal(sm_held, sm_land, sm_send, sm_recv, peers, z)
    for k in range(8):
        sm_held[0, k : k + 1, :] = gg[:, 128 * k : 128 * k + 128]
    for first_row, ref in ((8, gtb), (SMALL_ALL, gtx), (48, grows)):
        for k in range(ref.shape[1] // 128):
            sm_held[0, first_row + 8 * k : first_row + 8 * k + 8, :] = ref[:, 128 * k : 128 * k + 128]
    sm_held[0, 72:88, :] = gheads[...]
    steps = dot_nn(drow[...].astype(BF16), a1[...])
    for k in range(8):
        sm_held[0, 88 + 8 * k : 96 + 8 * k, :] = steps[:, 128 * k : 128 * k + 128]
    sums.start(0)
    two.start()
    one.start()
    three.middle()
    sums.take(0)
    sums.start(1)
    two.middle()
    one.middle()
    sums.take(1)
    sums.start(2)
    for t in range(2, nt - 1):
        chain.step(t)
    sums.take(2)
    all_own[...] = sm_held[3, 0:SMALL_ALL, :]
    over_all = Exchange(all_own, all_land, all_send, all_recv, d, z, nt)
    over_all.start()
    three.finish(fed_o)
    fed_o[...] += feed_rest[...]
    two.last()
    one.last()
    two.finish(sh_sum)
    per = sh_sum.shape[0] // nt
    copies = []
    for k in range(1, nt):
        q = lax.rem(z + k, nt)
        at = pl.ds(pl.multiple_of(q * per, per), per)
        copies.append(
            remote_copy(sh_sum.at[at], sh_land.at[k - 1], sh_send.at[k - 1], sh_recv.at[k - 1], (d, q))
        )
        copies[-1].start()
    one.finish(mixed_o)
    chain.finish(da)

    def keep(row):
        for k in range(8):
            ng_held[0, k : k + 1, :] = row[:, 128 * k : 128 * k + 128]

    norm_back(da[...], tok, gain, dh, gt_o, keep)
    norms = CubeTotal(ng_held, ng_land, ng_send, ng_recv, peers, z)
    norms.start(0)
    small_o[...] = sm_held[3]
    over_all.wait()
    small_o[0:SMALL_ALL, :] = over_all.total()
    norms.take(0)
    norms.start(1)
    for copy in copies:
        copy.wait()
    total = sh_sum[pl.ds(pl.multiple_of(z * per, per), per), :].astype(F32)
    for k in range(nt - 1):
        total = total + sh_land[k].astype(F32)
    sh_o[...] = total
    norms.take(1)
    norms.start(2)
    norms.take(2)
    last = Exchange(ng_held.at[3], ngz_land, ngz_send, ngz_recv, d, z, nt)
    last.start()
    last.wait()
    norm_o[...] = last.total()
    for thing in (chain, one, two, three, sums, norms):
        thing.drain()


def tail(nt, *args):
    tok, a1, dz = args[0], args[3], args[8]
    feed_own = args[-2]
    rows, width = tok.shape
    total = a1.shape[0]
    inner = dz.shape[1]
    n, lanes = 256 + 3 * inner, 128
    s_rows, s_lanes = 128, args[16].shape[1]
    f_rows = feed_own.shape[2]
    dma = pltpu.SemaphoreType.DMA
    sds = jax.ShapeDtypeStruct
    vmem = pl.BlockSpec(memory_space=pltpu.VMEM)
    return pl.pallas_call(
        partial(tail_kernel, nt),
        in_specs=[vmem] * len(args),
        out_specs=[vmem] * 6,
        out_shape=[sds((rows, width), BF16), sds((n, lanes), F32), sds((f_rows, 128), F32),
                   sds((s_rows // nt, s_lanes), F32), sds((SMALL_ROWS, 128), F32), sds((8, 128), F32)],
        scratch_shapes=[pltpu.VMEM((rows, width), F32), pltpu.VMEM((nt, rows, width), BF16),
                        pltpu.VMEM((4, 2, n, lanes), BF16), pltpu.VMEM((4, 2, s_rows, s_lanes), BF16),
                        pltpu.VMEM((128, total), BF16), pltpu.VMEM((inner, total), BF16)]
        + chain_scratch(nt, rows, width)
        + cube_scratch(n, lanes) + cube_scratch(s_rows, s_lanes) + square_scratch(f_rows, 128)
        + [pltpu.VMEM((s_rows, s_lanes), BF16), pltpu.VMEM((nt - 1, s_rows // nt, s_lanes), BF16),
           dma((nt - 1,)), dma((nt - 1,)),
           pltpu.VMEM((4, SMALL_ROWS, 128), F32), pltpu.VMEM((3, SMALL_ROWS, 128), F32), dma((3,)), dma((3,)),
           pltpu.VMEM((SMALL_ALL, 128), F32), pltpu.VMEM((nt - 1, SMALL_ALL, 128), F32), dma((nt - 1,)),
           dma((nt - 1,)),
           pltpu.VMEM((4, 8, 128), F32), pltpu.VMEM((3, 8, 128), F32), dma((3,)), dma((3,)),
           pltpu.VMEM((nt - 1, 8, 128), F32), dma((nt - 1,)), dma((nt - 1,))],
        compiler_params=pltpu.CompilerParams(
            vmem_limit_bytes=VMEM_LIMIT, collective_id=3, has_side_effects=True
        ),
        cost_estimate=pl.CostEstimate(flops=int(7e9), bytes_accessed=int(150e6), transcendentals=0),
        name="tail",
    )(*args)


def finish_kernel(
    heads, place, mixed, fed, small, norm,
    que_o, att_o, inn_o, mam_o, hid_o, dwn_o, norms_o, taps_o, chan_o, gain_o, step_o, heads_o,
):
    d, p = place[0], place[1]
    block = que_o.shape[0]
    inner = mam_o.shape[0]
    first = 0
    for j in range(que_o.shape[1] // 128):
        que_o[:, 128 * j : 128 * j + 128] = mixed[first : first + block]
        first += block
    att_o[...] = mixed[first : first + att_o.shape[0]]
    first += att_o.shape[0]
    for i in range(2):
        for j in range(inner // 128):
            inn_o[i, :, 128 * j : 128 * j + 128] = mixed[first : first + block]
            first += block
    mam_o[...] = mixed[first : first + inner]
    first = 0
    for i in range(2):
        for j in range(hid_o.shape[2] // 128):
            hid_o[i, :, 128 * j : 128 * j + 128] = fed[first : first + block]
            first += block
    dwn_o[...] = fed[first:]

    def lanes_from(values, lane):
        return pltpu.roll(values, lax.rem(128 - lane, 128), 1)

    width = norms_o.shape[1]
    per = 128 // width
    for i, ref in enumerate((norm, small)):
        row = lanes_from(jnp.broadcast_to(ref[pl.ds(p // per, 1), :], (8, 128)), lax.rem(p, per) * width)
        norms_o[i : i + 1, :] = row[0:1, 0:width]
    width = taps_o.shape[1]
    per = 128 // width
    row = small[pl.ds(pl.multiple_of(8 + 8 * (p // per), 8), 8), :]
    taps_o[...] = lanes_from(row, lax.rem(p, per) * width)[0 : CONV + 1, 0:width]
    width = gain_o.shape[1]
    sums = jnp.zeros((8, 128), F32)
    lane = lanes_of(sums.shape)
    sub = lax.broadcasted_iota(jnp.int32, sums.shape, 0)
    for b in range(heads // 2):
        rows = lanes_from(small[SMALL_ALL + 8 * b : SMALL_ALL + 8 * b + 8, :], d * width)
        raw = small[48 + 8 * b : 56 + 8 * b, :]
        gains = lanes_from(raw, d * width)
        for k in range(2):
            h = 2 * b + k
            at = slice(64 * k, 64 * k + width)
            chan_o[:, h, :] = rows[0 : CONV + 1, at]
            gain_o[h : h + 1, :] = gains[0:1, at]
            skip = jnp.sum(jnp.where(lane // SSM_DIM == k, raw[1:2, :], 0.0), axis=1, keepdims=True)
            sums = jnp.where((sub == h) & (lane == 2), skip, sums)
    for k in range(2):
        total = jnp.sum(small[72 + 8 * k : 80 + 8 * k, :], axis=1, keepdims=True)
        sums = jnp.where(lane == k, total, sums)
    heads_o[...] = sums
    steps = small[pl.ds(pl.multiple_of(88 + 8 * d, 8), 8), :]
    steps = jnp.concatenate([steps, jnp.zeros((120, 128), F32)], axis=0).T
    step_o[...] = steps[:, 0:heads]


def finish(heads, place, mixed, fed, small, norm, shapes):
    vmem = pl.BlockSpec(memory_space=pltpu.VMEM)
    sds = jax.ShapeDtypeStruct
    return pl.pallas_call(
        partial(finish_kernel, heads),
        in_specs=[pl.BlockSpec(memory_space=pltpu.SMEM)] + [vmem] * 4,
        out_specs=[vmem] * (len(shapes) + 1),
        out_shape=[sds(s, F32) for s in shapes] + [sds((8, 128), F32)],
        compiler_params=pltpu.CompilerParams(vmem_limit_bytes=VMEM_LIMIT),
        name="finish",
    )(place, mixed, fed, small, norm)


def rope_wide(length):
    half = HEAD_SIZE // 2
    inverse = rope_base ** (-np.arange(half) * (2.0 / HEAD_SIZE))
    angles = np.arange(length)[:, None] * inverse[None, :]
    c, s = np.cos(angles), np.sin(angles)
    return (
        jnp.asarray(np.concatenate([c, c, c, c], axis=1), F32),
        jnp.asarray(np.concatenate([-s, s, -s, s], axis=1), F32),
    )


def to_blocks(full, axis, nt):
    if axis == 1:
        two, width, cols = full.shape
        return full.reshape(2, 8, width // 8, nt, cols // nt).transpose(1, 3, 0, 2, 4)
    rows, width = full.shape
    return full.reshape(nt, rows // nt, 8, width // 8).transpose(2, 0, 1, 3)


def per_device(
    nd,
    nt,
    tokens,
    query_proj,
    attend_out,
    inner_proj,
    step_proj,
    mamba_out,
    hidden_proj,
    down_proj,
    channel_taps,
    mixer_gain,
    decay_log,
    step_bias,
    skip_weight,
    shared_proj,
    norm_gains,
    shared_taps,
    cotangent,
):
    tensor_index = lax.axis_index("tensor")
    d = lax.axis_index("dp")
    local_rows, width = tokens.shape
    group_rows = local_rows * nt
    heads = step_proj.shape[1]
    inner = heads * SSM_DIM
    channels = inner * nt
    units = down_proj.shape[0]
    feed = ()
    if nd == 8:
        small = pack_small(channel_taps, mixer_gain, norm_gains, shared_taps, step_proj)
        (tok_full, full_query, full_attend, full_inner, full_mamba, sha, sma) = gather_start(
            tokens, query_proj, attend_out, inner_proj, mamba_out, shared_proj, small, nd, nt
        )
        scal = jnp.stack([decay_log, step_bias, skip_weight]).astype(F32)
        where = tensor_index.astype(jnp.int32).reshape(1)
        (
            gain_first, gain_second, gain_mix, taps_x, taps_b, step_rows, decay, bias, skip,
        ) = unpack_small(heads, where, scal, sma, width)
        full_shared = sha.reshape(width, -1)
        feed = (hidden_proj, down_proj)
    else:
        small_parts = [channel_taps, mixer_gain, norm_gains, shared_taps, step_proj.T]
        flat = jnp.concatenate([p.reshape(-1) for p in small_parts])
        small_len = -(-flat.shape[0] // 2048) * 2048
        small = jnp.pad(flat, (0, small_len - flat.shape[0])).reshape(-1, 128)
        (tok_full, full_query, full_attend, full_inner, full_mamba, sha, sma) = gather_start(
            tokens, query_proj, attend_out, inner_proj, mamba_out, shared_proj, small, nd, nt
        )
        full_hidden = lax.all_gather(hidden_proj, "tensor", axis=2, tiled=True)
        full_hidden = to_blocks(lax.all_gather(full_hidden, "dp", axis=1, tiled=True), 1, nt)
        full_down = lax.all_gather(down_proj, "tensor", axis=0, tiled=True)
        full_down = to_blocks(lax.all_gather(full_down, "dp", axis=1, tiled=True), 0, nt)

        full_shared = sha.reshape(width, -1)
        sma = sma.reshape(nd, nt, small_len)

        def small_piece(index):
            start = sum(p.size for p in small_parts[:index])
            part = small_parts[index]
            return sma[:, :, start : start + part.size].reshape((nd, nt) + part.shape)

        taps_x = pick(small_piece(0), tensor_index, 1).transpose(1, 2, 0, 3).reshape(CONV + 1, inner)
        gain_mix = pick(small_piece(1), tensor_index, 1).transpose(1, 0, 2).reshape(1, inner)
        full_norms = small_piece(2).transpose(2, 0, 1, 3).reshape(2, width).astype(F32)
        taps_b = small_piece(3).transpose(2, 0, 1, 3).reshape(CONV + 1, -1)
        step_rows = pick(small_piece(4), tensor_index, 1).transpose(1, 0, 2).reshape(heads, width)
        step_rows = jnp.pad(step_rows, ((0, 8 - heads), (0, 0)))
        taps_x = jnp.pad(taps_x.astype(F32), ((0, 7 - CONV), (0, 0)))
        taps_b = jnp.pad(taps_b.astype(F32), ((0, 7 - CONV), (0, 0)))
        gain_mix = gain_mix.astype(F32)
        gain_first = full_norms[0:1]
        gain_second = full_norms[1:2]

        def head_rows(values):
            return jnp.pad(jnp.broadcast_to(values[:, None], (heads, 128)), ((0, 8 - heads), (0, 0)))

        decay = head_rows(-jnp.exp(decay_log.astype(F32)))
        bias = head_rows(step_bias.astype(F32))
        skip = jnp.repeat(skip_weight.astype(F32), SSM_DIM)[None, :]
    q_heads = query_proj.shape[1] // HEAD_SIZE
    kv_head = (tensor_index * q_heads // (QHEADS // KVHEADS)).astype(jnp.int32).reshape(1)
    cosine, sine = rope_wide(group_rows)

    (a1, q, k2, v2, lse, o, xr, zr, br, y, trow, states, squares, *feed) = mixers_forward(
        heads, nt, kv_head, tok_full.reshape(group_rows, width), gain_first, full_query, full_inner, step_rows,
        full_shared, cosine, sine, taps_x, taps_b, decay, bias, skip, feed,
    )
    mixed = mix_scatter(
        channels, nt, o, y, zr, squares, gain_mix, full_attend, full_mamba, tokens, tuple(feed)
    )
    m, squares, hidden = mixed[:3]
    if nd == 8:
        full_hidden, full_down = mixed[3:]
    if nd == 8:
        layer_out, dh, grad_gain_two, grad_mix, do, dm, dots, feed_own, feed_sums = feed_unmix(
            nt, hidden, gain_second, cotangent, full_hidden, full_down, y, zr, gain_mix, full_attend, full_mamba
        )
        feed_own = feed_own.reshape((2, 2) + feed_own.shape[1:])
    else:
        layer_out, dh, dmix, grad_gain_two, feed_pieces = feed_forward(
            hidden, gain_second, cotangent, full_hidden, full_down
        )
        grad_mix, do, dm, dots = unmix_gather(nt, dmix, y, zr, gain_mix, full_attend, full_mamba)
        hid_full = feed_pieces[:, :, : 2 * units].reshape(8, nt, 2, units // 128, width // 8, 128)
        hid_full = hid_full.transpose(2, 0, 4, 1, 3, 5).reshape(2, nd, width // nd, nt, units)
        hid_sum = cube_scatter(hid_full.transpose(1, 3, 0, 2, 4), nd, BF16)
        down_full = feed_pieces[:, :, 2 * units :].transpose(1, 2, 0, 3)
        down_full = down_full.reshape(nt, units, nd, width // nd)
        down_sum = cube_scatter(down_full.transpose(2, 0, 1, 3), nd, BF16)
        gradient_hidden = chain_scatter(hid_sum, nt)
        gradient_down = chain_scatter(down_sum, nt)

    back = mixers_back(
        heads, channels, nt, kv_head, q, k2, v2, lse, do, cosine, sine, dm, y, zr, xr, br, trow, states,
        squares, dots, gain_mix, taps_x, taps_b, decay, bias, skip, feed_sums if nd == 8 else None,
    )
    dq, dkv, dz, dx, db, drow, grad_tx, grad_tb, grad_rows, grad_heads = back[:10]
    if nd == 8:
        sums = tail(
            nt, tokens, gain_first, dh, a1, grad_mix, o, m, dq, dz, dx, dkv, db, drow, full_query, full_inner,
            step_rows, full_shared, grad_gain_two, grad_tb, grad_tx, grad_rows, grad_heads, feed_own, back[10],
        )
        gradient_tokens, mixed, fed, gradient_shared, small_sums, grad_gain_one = sums
        place = jnp.stack([d, d * nt + tensor_index]).astype(jnp.int32)
        shapes = [
            query_proj.shape, attend_out.shape, inner_proj.shape, mamba_out.shape, hidden_proj.shape,
            down_proj.shape, norm_gains.shape, shared_taps.shape, channel_taps.shape, mixer_gain.shape,
            step_proj.shape,
        ]
        (
            gradient_query,
            gradient_attend,
            gradient_inner,
            gradient_mamba,
            gradient_hidden,
            gradient_down,
            gradient_norms,
            gradient_taps,
            gradient_channel,
            gradient_mixer,
            gradient_step,
            head_sums,
        ) = finish(heads, place, mixed, fed, small_sums, grad_gain_one, shapes)
        return (
            layer_out,
            gradient_tokens,
            gradient_query,
            gradient_attend,
            gradient_inner,
            gradient_step,
            gradient_mamba,
            gradient_hidden,
            gradient_down,
            gradient_channel,
            gradient_mixer,
            head_sums[:heads, 0],
            head_sums[:heads, 1],
            head_sums[:heads, 2],
            gradient_shared,
            gradient_norms,
            gradient_taps,
        )

    part_one = down_parts(dq, dz, dx, dkv, db, drow, full_query, full_inner, step_rows, full_shared)
    pieces, shared_pieces, grad_step = weight_pieces(a1, dq, dz, dx, dkv, db, drow, o, m, grad_mix)
    block = width // nd
    q_cols = query_proj.shape[1]
    cuts = [0, q_cols, q_cols + attend_out.shape[0]]
    cuts += [cuts[2] + inner, cuts[2] + 2 * inner, cuts[2] + 3 * inner]

    def from_rows(values):
        return values.reshape(8, -1, 128, 128).transpose(0, 2, 1, 3).reshape(width, -1)

    def from_lanes(values):
        return values.transpose(1, 0, 2).reshape(-1, width)

    n_tap = CONV + 1
    over_all = jnp.concatenate([grad_gain_two.reshape(-1), grad_tb[:n_tap].reshape(-1)])
    over_dp = jnp.concatenate(
        [
            grad_tx[:n_tap].reshape(-1),
            grad_rows[0],
            grad_rows[1].reshape(heads, SSM_DIM).sum(axis=1),
            grad_heads[:heads].sum(axis=1),
            grad_heads[8 : 8 + heads].sum(axis=1),
            grad_step[:heads].reshape(-1),
        ]
    )

    def in_rows(values):
        return jnp.pad(values, (0, -values.shape[0] % 1024)).reshape(-1, 128)

    rows_all = in_rows(over_all)
    n_all = rows_all.shape[0]
    small_sums = jnp.concatenate([rows_all, in_rows(over_dp)], axis=0)
    parts = part_one.reshape(nt, local_rows, width)
    token_f32 = tokens.astype(F32)
    _, norm_one_back = jax.vjp(norm_apply, token_f32, gain_first[0])
    grad_from_one, grad_gain_one = norm_one_back(chain_scatter(parts, nt))
    gradient_tokens = (dh + grad_from_one).astype(BF16)
    got = [pieces[:, cuts[i] : cuts[i + 1]] for i in range(5)]

    def over_rows(values):
        return cube_scatter(from_rows(values).reshape(nd, block, -1), nd)

    def over_lanes(values):
        return cube_scatter(from_lanes(values).reshape(-1, nd, block).transpose(1, 0, 2), nd)

    gradient_query = over_rows(got[0])
    gradient_attend = over_lanes(got[1])
    gradient_inner = jnp.stack([over_rows(got[2]), over_rows(got[3])])
    gradient_mamba = over_lanes(got[4])
    shared_cut = shared_pieces.reshape(nd, nt, width // (nd * nt), -1)
    gradient_shared = chain_scatter(cube_scatter(shared_cut, nd, BF16), nt)
    small_sums = lax.psum(small_sums, "dp")
    small_sums = jnp.concatenate(
        [lax.psum(small_sums[:n_all], "tensor"), small_sums[n_all:]], axis=0
    )
    grad_gain_one = lax.psum(grad_gain_one, ("dp", "tensor")).reshape(1, width)
    over_all = small_sums[:n_all].reshape(-1)
    over_dp = small_sums[n_all:].reshape(-1)
    place = d * nt + tensor_index
    norm_w = width // (nd * nt)
    both_norms = jnp.concatenate([grad_gain_one, over_all[:width].reshape(1, width)], axis=0)
    gradient_norms = lax.dynamic_slice_in_dim(both_norms, place * norm_w, norm_w, 1)
    tap_w = shared_taps.shape[1]
    tap_all = over_all[width : width + n_tap * taps_b.shape[1]].reshape(n_tap, -1)
    gradient_taps = lax.dynamic_slice_in_dim(tap_all, place * tap_w, tap_w, 1)
    part = mixer_gain.shape[1]
    n_taps = n_tap * inner
    chan = over_dp[:n_taps].reshape(n_tap, heads, SSM_DIM)
    gain = over_dp[n_taps : n_taps + inner].reshape(heads, SSM_DIM)
    gradient_channel = lax.dynamic_slice_in_dim(chan, d * part, part, 2)
    gradient_mixer = lax.dynamic_slice_in_dim(gain, d * part, part, 1)
    rest = over_dp[n_taps + inner :]
    gradient_skip = rest[:heads]
    gradient_decay = rest[heads : 2 * heads]
    gradient_bias = rest[2 * heads : 3 * heads]
    step_all = rest[3 * heads : 3 * heads + heads * width].reshape(heads, width)
    gradient_step = lax.dynamic_slice_in_dim(step_all, d * block, block, 1).T
    return (
        layer_out,
        gradient_tokens,
        gradient_query,
        gradient_attend,
        gradient_inner,
        gradient_step,
        gradient_mamba,
        gradient_hidden,
        gradient_down,
        gradient_channel,
        gradient_mixer,
        gradient_decay,
        gradient_bias,
        gradient_skip,
        gradient_shared,
        gradient_norms,
        gradient_taps,
    )


def solution(mesh):
    placed = (
        P(("dp", "tensor"), None),
        P("dp", "tensor"),
        P("tensor", "dp"),
        P(None, "dp", "tensor"),
        P("dp", "tensor"),
        P("tensor", "dp"),
        P(None, "dp", "tensor"),
        P("tensor", "dp"),
        P(None, "tensor", "dp"),
        P("tensor", "dp"),
        P("tensor"),
        P("tensor"),
        P("tensor"),
        P(("dp", "tensor"), None),
        P(None, ("dp", "tensor")),
        P(None, ("dp", "tensor")),
        P(("dp", "tensor"), None),
    )
    return jax.shard_map(
        partial(per_device, mesh.shape["dp"], mesh.shape["tensor"]),
        mesh=mesh,
        in_specs=placed,
        out_specs=(
            P(("dp", "tensor"), None),
            P(("dp", "tensor"), None),
            P("dp", "tensor"),
            P("tensor", "dp"),
            P(None, "dp", "tensor"),
            P("dp", "tensor"),
            P("tensor", "dp"),
            P(None, "dp", "tensor"),
            P("tensor", "dp"),
            P(None, "tensor", "dp"),
            P("tensor", "dp"),
            P("tensor"),
            P("tensor"),
            P("tensor"),
            P(("dp", "tensor"), None),
            P(None, ("dp", "tensor")),
            P(None, ("dp", "tensor")),
        ),
        check_vma=False,
    )
```

profile of v0, /device:TPU:0, one launch (start us, length us, event | category | flops | bytes accessed | tf_op | source)
XLA Modules:
  0.0 316.7 jit_solution(17264998550394318281)
XLA Ops:
  0.7 0.6 pad_add_fusion.place
  1.3 1.3 maximum_convert_fusion.scal
  2.5 1.4 copy.40.step
  3.9 1.5 pack_small.1.refs_6_
  5.5 47.0 %gather_start.1 = (bf16[4,256,1024]{2,1,0:T(8,128)(2,1)}, bf16[1024,128]{1,0:T(8,128)(2,1)}, bf16[128,1024]{1,0:T(8,128)(2,1)}, bf16[2,1024,384]{2,1,0:T(8,128)(...) custom-call(bf16[256,1024]{1,0:T(8,128)(2,1)} %tok.1, ...), custom_call_target="tpu_custom_call" | custom-call | tf_op jit(solution)/shard_map/gather_start/pallas_call | solution.py:197
  52.5 1.7 unpack_small.1
  54.2 33.1 %mixers_forward.1 = (bf16[1024,1024]{1,0:T(8,128)(2,1)}, bf16[1024,128]{1,0:T(8,128)(2,1)}, bf16[1024,128]{1,0:T(8,128)(2,1)}, bf16[1024,128]{1,0:T(8,128)(2,1)}...) custom-call(s32[1]{0:T(128)} %bitcast.refs_0_.refs_1_, ...), custom_call_target="tpu_custom_call" | custom-call | flops 5000000000 | bytes 15000000 | tf_op jit(solution)/shard_map/mixers_forward/pallas_call | solution.py:621
  87.3 48.6 %mix_scatter.1 = (bf16[1024,384]{1,0:T(8,128)(2,1)}, f32[8,1024]{1,0:T(8,128)}, f32[256,1024]{1,0:T(8,128)}, bf16[8,4,2,128,512]{4,3,2,1,0:T(8,128)(2,1)}, bf16[8,4,512,128]{3,2,1,0:T(8,128)(2,1)}) custom-call(bf16[1024,128]{1,0:T(8,128)(2,1)} %get-tuple-element.105.refs_0_.o, ...), custom_call_target="tpu_custom_call", output_to_operand_aliasing={{3}: (8, {}), {4}: (9, {})} | custom-call | flops 1000000000 | bytes 130000000 | tf_op jit(solution)/shard_map/mix_scatter/pallas_call | solution.py:1344
  135.9 71.8 %feed_unmix.1 = (bf16[256,1024]{1,0:T(8,128)(2,1)}, f32[256,1024]{1,0:T(8,128)}, f32[1,1024]{1,0:T(1,128)}, bf16[1024,1024]{1,0:T(8,128)(2,1)}, bf16[1024,128]{1...) custom-call(f32[256,1024]{1,0:T(8,128)} %get-tuple-element.116.refs_, ...), custom_call_target="tpu_custom_call" | custom-call | flops 10000000000 | bytes 150000000 | tf_op jit(solution)/shard_map/feed_unmix/pallas_call | solution.py:1632
  207.6 35.4 %mixers_back.1 = (bf16[1024,128]{1,0:T(8,128)(2,1)}, bf16[1024,256]{1,0:T(8,128)(2,1)}, bf16[1024,384]{1,0:T(8,128)(2,1)}, bf16[1024,384]{1,0:T(8,128)(2,1)}, bf...) custom-call(bf16[3,1536,128]{2,1,0:T(8,128)(2,1)} %get-tuple-element, ...), custom_call_target="tpu_custom_call" | custom-call | flops 6000000000 | bytes 18000000 | tf_op jit(solution)/shard_map/mixers_back/pallas_call | solution.py:929
  243.0 65.6 %tail.1 = (bf16[256,1024]{1,0:T(8,128)(2,1)}, f32[1408,128]{1,0:T(8,128)}, f32[1536,128]{1,0:T(8,128)}, f32[32,512]{1,0:T(8,128)}, f32[152,128]{1,0:T(8,128)}, /*index=5*/f32[8,128]{1,0:T(8,128)}) custom-call(bf16[256,1024]{1,0:T(8,128)(2,1)} %tok.1, f32[1,1024]{1,0:T(1,128)} %get-tuple-element.95.refs_2_.gain, f32[256,1024]{1,0:T(8,128)} %get-tuple-element.121.dh, ...), custom_call_target="tpu_custom_call" | custom-call | flops 7000000000 | bytes 150000000 | tf_op jit(solution)/shard_map/tail/pallas_call | solution.py:1934
  308.6 0.0 copy-start
  308.6 0.0 copy-start.1
  308.6 0.0 copy-start.2
  308.6 2.8 finish.1
  311.4 1.5 slice_reduce_fusion
  313.0 1.5 copy.41
  314.5 0.0 copy-done
  314.5 0.8 copy.47
  315.3 0.0 copy-done.1
  315.3 0.8 copy.48
  316.1 0.0 copy-done.2
  316.1 0.6 copy.49
Async XLA Ops:
  308.6 5.8 %copy-start = (bf16[256,1024]{1,0:T(8,128)(2,1)S(1)}, bf16[256,1024]{1,0:T(8,128)(2,1)}, u32[]{:S(2)}) copy-start(bf16[256,1024]{1,0:T(8,128)(2,1)} %get-tuple-element.223) | copy-start | bytes 1572868
  308.6 6.6 %copy-start.1 = (bf16[256,1024]{1,0:T(8,128)(2,1)S(1)}, bf16[256,1024]{1,0:T(8,128)(2,1)}, u32[]{:S(2)}) copy-start(bf16[256,1024]{1,0:T(8,128)(2,1)} %get-tuple-element.224) | copy-start | bytes 1572868
  308.6 7.4 %copy-start.2 = (f32[32,512]{1,0:T(8,128)S(1)}, f32[32,512]{1,0:T(8,128)}, u32[]{:S(2)}) copy-start(f32[32,512]{1,0:T(8,128)} %get-tuple-element.237) | copy-start | bytes 196612
where the time goes:
time: 317 us
  Pallas kernels  307 us (97%)
  local copies, waits for them, and re-layouts  6.67 us (2%)
    pallas_call x1, Pallas kernels, feed_unmix(): pl.pallas_call(partial(feed_unmix_kernel, nt), grid=(2 * tiles,), in_spec...  71.8 us
    pallas_call x1, Pallas kernels, tail(): pl.pallas_call(partial(tail_kernel, nt), in_specs=[vmem] * len(args), out...  65.6 us
    pallas_call x1, Pallas kernels, mix_scatter(): pl.pallas_call(partial(mix_scatter_kernel, channels, nt, bool(feed)), in_...  48.6 us
    pallas_call x1, Pallas kernels, gather_start(): pl.pallas_call(partial(gather_kernel, nt), out_shape=[jax.ShapeDtypeStruc...  47 us
    pallas_call x1, Pallas kernels, mixers_back(): pl.pallas_call(partial(back_kernel, heads, channels, nt, feed is not None...  35.4 us
    pallas_call x1, Pallas kernels, mixers_forward(): pl.pallas_call(partial(forward_kernel, heads, nt, bool(feed)), grid=(tota...  33.1 us

commit v1 on v0

--- a/solution.py
+++ b/solution.py
@@ -209,7 +209,7 @@
 
 
 def pack_kernel(taps, gain, norms, staps, step, out, rows):
-    heads = step.shape[1]
+    heads = step.shape[0]
     f32 = jnp.float32
     rows[...] = jnp.zeros(rows.shape, f32)
     rows[0:2, 0:32] = norms[...].astype(f32)
@@ -217,8 +217,7 @@
     rows[0:heads, 40:48] = gain[...].astype(f32)
     for j in range(CONV + 1):
         rows[0:heads, 48 + 8 * j : 56 + 8 * j] = taps[j].astype(f32)
-    wide = jnp.concatenate([step[...].astype(f32), jnp.zeros((128, 128 - heads), f32)], axis=1)
-    rows[8:16, :] = wide.T[0:8, :]
+    rows[8 : 8 + heads, :] = step[...].astype(f32)
     out[...] = rows[...].astype(jnp.bfloat16)
 
 
@@ -433,12 +432,6 @@
                 copy.start()
 
         self.at(0, act)
-        def late():
-            for chain in self.chains:
-                chain.hop(2)
-
-        self.at(3, late)
-
     def middle(self):
         def near():
             for chain in self.chains:
@@ -447,6 +440,8 @@
                 self.cube.near(i)
 
         def far():
+            for chain in self.chains:
+                chain.hop(2)
             for i in range(2):
                 self.cube.far(i)
 
@@ -696,19 +691,33 @@
     if feed:
         d = lax.axis_index("dp")
         z = lax.axis_index("tensor")
-        feed_in, feed_o, came, f_send, f_recv = refs[0], refs[38], refs[46], refs[47], refs[48]
+        sums, raw, refs = refs[0], refs[1], refs[2:]
+        feed_o, refs = refs[37], refs[:37] + refs[38:]
+        (came, f_send, f_recv, held), box, refs = refs[44:48], refs[48:56], refs[:44]
+        peers = cube_peers(d)
+        square = SquareScatter(
+            lambda i, j: (2 * i + j,), raw, box[:6], box[6], box[7], peers, dp_bits(d), z
+        )
+        sources = [sums.at[k] for k in range(nt - 2)] + [held]
         copies = [
-            remote_copy(feed_in.at[k], came.at[k], f_send.at[k], f_recv.at[k], peer)
+            remote_copy(sources[k], came.at[k], f_send.at[k], f_recv.at[k], peer)
             for k, peer in enumerate(other_quarters(d, z, nt))
         ]
 
         @pl.when(step == 0)
         def _():
-            greet(other_quarters(d, z, nt))
-            for copy in copies:
+            greet([(p, z) for p in peers[1:]] + other_quarters(d, z, nt))
+            for copy in copies[:-1]:
                 copy.start()
-
-        refs = refs[1:38] + refs[39:46]
+            square.start()
+
+        pl.when(step == 3)(square.middle)
+
+        @pl.when(step == 4)
+        def _():
+            square.finish(held)
+            copies[-1].start()
+
     attend_back(step, *refs[:10], *refs[27:29], *refs[37:39])
     scan_back(heads, channels, step, *refs[10:27], *refs[29:37], *refs[39:44])
     if feed:
@@ -721,6 +730,7 @@
                 value = came[k].astype(F32)
                 total = value if total is None else total + value
             feed_o[...] = total
+            square.drain()
 
 
 def scan_back(
@@ -920,11 +930,13 @@
     extra = {}
     if feed is not None:
         dma = pltpu.SemaphoreType.DMA
-        args = [feed] + args
-        in_specs = [whole(feed)] + in_specs
-        out_specs = out_specs + [fixed(*feed.shape[1:])]
-        out_shape = out_shape + [sds(feed.shape[1:], F32)]
-        scratch = scratch + [pltpu.VMEM(feed.shape, BF16), dma((nt - 1,)), dma((nt - 1,))]
+        piece = feed[0].shape[1:]
+        args = list(feed) + args
+        in_specs = [whole(v) for v in feed] + in_specs
+        out_specs = out_specs + [fixed(*piece)]
+        out_shape = out_shape + [sds(piece, F32)]
+        scratch = scratch + [pltpu.VMEM((nt - 1,) + piece, BF16), dma((nt - 1,)), dma((nt - 1,)),
+                             pltpu.VMEM(piece, BF16)] + square_scratch(*piece)
         extra = dict(collective_id=5, has_side_effects=True)
     return pl.pallas_call(
         partial(back_kernel, heads, channels, nt, feed is not None),
@@ -1254,17 +1266,32 @@
 
 
 def mix_scatter_kernel(channels, nt, feed, *refs):
-    (o, y, z_in, sq, gain, watt, wmam, tok), refs = refs[:8], refs[8:]
+    (o, y_in, gate_in, sq, gain, watt, wmam, tok), refs = refs[:8], refs[8:]
     if feed:
         (hid_z, dwn_z), refs = refs[2:4], refs[4:]
         (m_o, sq_o, hid_o, hid_f, dwn_f), refs = refs[:5], refs[5:]
         (lsem, f_send, f_recv), refs = refs[:3], refs[3:]
     else:
         (m_o, sq_o, hid_o), refs = refs[:3], refs[3:]
-    (sq_land, sq_send, sq_recv, parts, bufs, landed, c_send, c_recv) = refs
+    (y, z_in, in_sem, sq_land, sq_send, sq_recv, parts, bufs, landed, c_send, c_recv) = refs
     d = lax.axis_index("dp")
     z = lax.axis_index("tensor")
     rows = tok.shape[0]
+
+    def rows_of(q):
+        return pl.ds(pl.multiple_of(q * rows, rows), rows)
+
+    def load(q):
+        at = rows_of(q)
+        return [
+            pltpu.make_async_copy(y_in.at[at], y.at[at], in_sem.at[0, q]),
+            pltpu.make_async_copy(gate_in.at[at], z_in.at[at], in_sem.at[1, q]),
+        ]
+
+    first = jnp.where(z < nt // 2, nt - 1, 0)
+    for k in range(nt):
+        for copy in load(lax.rem(first + k, nt)):
+            copy.start()
     peers = [(p, z) for p in cube_peers(d)] if feed else []
     greet(peers + other_quarters(d, z, nt))
     squares = Exchange(sq, sq_land, sq_send, sq_recv, d, z, nt)
@@ -1288,7 +1315,9 @@
     sq_o[...] = squares.total()
 
     def part(q):
-        at = pl.ds(pl.multiple_of(q * rows, rows), rows)
+        at = rows_of(q)
+        for copy in load(q):
+            copy.wait()
         total = sq_o[:, at]
         r = row_columns([lax.rsqrt(total / channels + epsilon)], rows)[:, 0:1]
         zv = z_in[at, :]
@@ -1296,7 +1325,6 @@
         m_o[at, :] = m
         parts[q] = (dot_nn(o[at, :], watt[...]) + dot_nn(m, wmam[...])).astype(BF16)
 
-    first = jnp.where(z < nt // 2, nt - 1, 0)
     part(first)
     chain.step(0)
 
@@ -1305,19 +1333,14 @@
         return carry
 
     lax.fori_loop(0, nt - 1, rest, 0)
-    if feed:
-        cube.near(0)
-        cube.near(1)
     for t in range(1, nt - 1):
         chain.step(t)
-        if feed:
-            cube.near(2 * t)
-            cube.near(2 * t + 1)
-            cube.far(2 * t - 2)
-            cube.far(2 * t - 1)
+        if feed and t == 1:
+            for i in range(n):
+                cube.near(i)
     if feed:
-        cube.far(n - 2)
-        cube.far(n - 1)
+        for i in range(n):
+            cube.far(i)
     chain.finish(hid_o)
     hid_o[...] += tok[...].astype(F32)
     chain.drain()
@@ -1343,11 +1366,12 @@
         scratch = [dma((n,)), dma((n, 7)), dma((n, 7))]
     return pl.pallas_call(
         partial(mix_scatter_kernel, channels, nt, bool(feed)),
-        in_specs=[vmem] * 8 + [anywhere] * len(feed[:2]) + [vmem] * len(feed[2:]),
+        in_specs=[vmem, anywhere, anywhere] + [vmem] * 5 + [anywhere] * len(feed[:2]) + [vmem] * len(feed[2:]),
         out_specs=[vmem] * 3 + [anywhere] * (len(outs) - 3),
         out_shape=outs,
         input_output_aliases={8: 3, 9: 4} if feed else {},
-        scratch_shapes=scratch + [pltpu.VMEM((nt - 1, 8, total), F32), dma((nt - 1,)), dma((nt - 1,)),
+        scratch_shapes=scratch + [pltpu.VMEM((total, inner), F32), pltpu.VMEM((total, inner), F32),
+                                  dma((2, nt)), pltpu.VMEM((nt - 1, 8, total), F32), dma((nt - 1,)), dma((nt - 1,)),
                         pltpu.VMEM((nt, rows, width), BF16)] + chain_scratch(nt, rows, width),
         compiler_params=pltpu.CompilerParams(
             vmem_limit_bytes=VMEM_LIMIT, collective_id=1, has_side_effects=True
@@ -1409,7 +1433,8 @@
         g_o, do_o, dm_o, dots_o = self.outs
         rows = self.rows
         at = pl.ds(pl.multiple_of(q * rows, rows), rows)
-        g_o[at, :] = g
+        if g_o is not None:
+            g_o[at, :] = g
         do_o[at, :] = dot_nt(g, watt[...]).astype(BF16)
         dm = dot_nt(g, wmam[...])
         dm_o[at, :] = dm
@@ -1418,13 +1443,14 @@
         turned = [jnp.broadcast_to(dots[c : c + 128], (128, 128)).T[0:8, :] for c in range(0, rows, 128)]
         dots_o[:, at] = jnp.concatenate(turned, axis=1)
 
-    def around(self, z, dist, nt, slots):
+    def around(self, z, dist, nt, slots, after=lambda q: None):
         def side(way, carry):
             q = jnp.where(way == 0, z - dist, z + dist)
 
             @pl.when((q >= 0) & (q < nt))
             def _():
                 self(q, slots[q])
+                after(q)
 
             return carry
 
@@ -1485,10 +1511,11 @@
 
 
 def feed_unmix_kernel(nt, *refs):
-    (hid, gain, cot, whid, wdown, y, z_in, mgain, watt, wmam), refs = refs[:10], refs[10:]
-    (out_o, dh_o, gg_o, g_o, do_o, dm_o, dot_o, own_o, sum_o), refs = refs[:9], refs[9:]
+    (hid, gain, cot, whid, wdown, y_in, gate_in, mgain, watt_in, wmam_in), refs = refs[:10], refs[10:]
+    (out_o, dh_o, gg_o, g_o, do_o, dm_o, dot_o, own_o, raw_o, sum_o), refs = refs[:10], refs[10:]
+    (y, z_in, watt, wmam, out, dh, dm, in_sem, out_sem, g_sem, dm_sem), refs = refs[:11], refs[11:]
     (a2, a2t, acc, dacc, fs, dgs, dus, dmix, piece, sent, came, b_send, b_recv), refs = refs[:13], refs[13:]
-    boxes, refs = refs[: 8 * (nt - 1)], refs[8 * (nt - 1) :]
+    boxes, refs = refs[: 8 * (nt - 2)], refs[8 * (nt - 2) :]
     (slots, g_send, g_recv, dot_own, dot_land, d_send, d_recv) = refs
     step = pl.program_id(0)
     tiles = pl.num_programs(0) // 2
@@ -1499,15 +1526,45 @@
     peers = cube_peers(d)
     chain = ChainGather(dmix, slots, g_send, g_recv, d, z, nt)
     cubes = []
-    for k in range(1, nt):
+    for k in range(1, nt - 1):
         q = lax.rem(z + k, nt)
         box = boxes[8 * k - 8 : 8 * k]
         cubes.append(
             SquareScatter(lambda i, j, q=q: (2 * i + j, q), piece, box[:6], box[6], box[7], peers, bits, z)
         )
 
+    rows = hid.shape[0]
+    late = [
+        pltpu.make_async_copy(src, dst, in_sem.at[i])
+        for i, (src, dst) in enumerate(((y_in, y), (gate_in, z_in), (watt_in, watt), (wmam_in, wmam)))
+    ]
+
+    def rows_of(q):
+        return pl.ds(pl.multiple_of(q * rows, rows), rows)
+
+    def store_g(q):
+        return pltpu.make_async_copy(slots.at[q], g_o.at[rows_of(q)], g_sem.at[q])
+
+    def store_dm(q):
+        return pltpu.make_async_copy(dm.at[rows_of(q)], dm_o.at[rows_of(q)], dm_sem.at[q])
+
+    ready = [
+        pltpu.make_async_copy(src, dst, out_sem.at[i])
+        for i, (src, dst) in enumerate(
+            (
+                (out, out_o),
+                (dh, dh_o),
+                (dmix, g_o.at[rows_of(z)]),
+                (piece.at[:, z], own_o),
+                (piece.at[:, lax.rem(z + nt - 1, nt)], raw_o),
+            )
+        )
+    ]
+
     @pl.when(step == 0)
     def _():
+        for copy in late:
+            copy.start()
         greet([(p, z) for p in peers] + other_quarters(d, z, nt))
         feed_open(hid, gain, a2, a2t, acc, dacc)
 
@@ -1517,8 +1574,10 @@
 
     @pl.when(step == tiles - 1)
     def _():
-        dmix[...] = feed_close(hid, gain, cot, acc, dacc, out_o, dh_o, gg_o)
+        dmix[...] = feed_close(hid, gain, cot, acc, dacc, out, dh, gg_o)
         chain.start()
+        for copy in ready[:3]:
+            copy.start()
 
     units = whid.shape[4]
     quarter_units = piece.shape[2] // 3
@@ -1564,7 +1623,7 @@
             first += n
         swap(turn_).start()
         pl.when(turn_ >= 1)(lambda: take(turn_ - 1))
-        for k in range(1, nt):
+        for k in range(1, nt - 1):
             pl.when(turn_ == k * tiles_per)(cubes[k - 1].start)
 
     @pl.when(step == 2 * tiles - 1)
@@ -1572,15 +1631,24 @@
         take(tiles - 1)
         for i in range(BOXES):
             swap(tiles - BOXES + i).wait_send()
-        own_o[...] = piece[:, z]
-        work = Unmix(y, z_in, mgain, watt, wmam, g_o, do_o, dm_o, dot_own, hid.shape[0])
+        for copy in ready[3:]:
+            copy.start()
+        for copy in late:
+            copy.wait()
+        work = Unmix(y, z_in, mgain, watt, wmam, None, do_o, dm, dot_own, rows)
         work(z, dmix[...])
+        store_dm(z).start()
+
+        def after(q):
+            store_g(q).start()
+            store_dm(q).start()
+
         for dist in range(1, nt):
             chain.hop(dist)
-            work.around(z, dist, nt, slots)
+            work.around(z, dist, nt, slots, after)
             if dist == 1:
                 cubes[0].middle()
-            if dist < nt - 1:
+            if dist < nt - 2:
                 cubes[dist].middle()
             elif dist == nt - 1:
                 dots = Exchange(dot_own, dot_land, d_send, d_recv, d, z, nt)
@@ -1592,6 +1660,11 @@
             cube.drain()
         dots.wait()
         dot_o[...] = dots.total()
+        for copy in ready:
+            copy.wait()
+        for q in range(nt):
+            store_dm(q).wait()
+            pl.when(z != q)(store_g(q).wait)
 
 
 def feed_unmix(nt, hid, gain, cot, whid, wdown, y, zr, mgain, watt, wmam):
@@ -1620,23 +1693,26 @@
     )
     out_shape = [sds((rows, width), BF16), sds((rows, width), F32), sds((1, width), F32)]
     out_shape += unmix_shapes(total, width, inner)
-    out_shape += [sds((kept, n, 128), BF16), sds((nt - 1, n, 128), BF16)]
+    out_shape += [sds((kept, n, 128), BF16), sds((kept, n, 128), BF16), sds((nt - 2, n, 128), BF16)]
+    anywhere = pl.BlockSpec(memory_space=pl.ANY)
+    late = [pltpu.VMEM(v.shape, v.dtype) for v in (y, zr, watt, wmam) + tuple(out_shape[:2])]
+    late += [pltpu.VMEM((total, inner), F32), dma((4,)), dma((5,)), dma((nt,)), dma((nt,))]
     box = pltpu.VMEM((BOXES, kept, 3 * tile, 128), BF16)
     kept_tile = pltpu.VMEM((tiles, rows, tile), BF16)
     scratch = [pltpu.VMEM((rows, width), BF16), pltpu.VMEM((width, rows), BF16),
                pltpu.VMEM((rows, width), F32), pltpu.VMEM((rows, width), F32), kept_tile, kept_tile, kept_tile,
                pltpu.VMEM((rows, width), BF16), pltpu.VMEM((kept, nt, n, 128), BF16), box, box, dma((BOXES,)),
                dma((BOXES,))]
-    for _ in range(nt - 1):
+    for _ in range(nt - 2):
         scratch += square_scratch(n, 128)
     return pl.pallas_call(
         partial(feed_unmix_kernel, nt),
         grid=(2 * tiles,),
-        in_specs=[fixed(hid), fixed(gain), fixed(cot), hid_spec, down_spec, fixed(y), fixed(zr), fixed(mgain),
-                  fixed(watt), fixed(wmam)],
-        out_specs=[fixed(v) for v in out_shape],
+        in_specs=[fixed(hid), fixed(gain), fixed(cot), hid_spec, down_spec, anywhere, anywhere, fixed(mgain),
+                  anywhere, anywhere],
+        out_specs=[anywhere if i in (0, 1, 3, 5, 7, 8) else fixed(v) for i, v in enumerate(out_shape)],
         out_shape=out_shape,
-        scratch_shapes=scratch + unmix_scratch(nt, rows, width, total),
+        scratch_shapes=late + scratch + unmix_scratch(nt, rows, width, total),
         compiler_params=pltpu.CompilerParams(
             vmem_limit_bytes=60 * 1024 * 1024, collective_id=4, has_side_effects=True
         ),
@@ -1776,42 +1852,47 @@
             copy.wait_send()
 
 
-def norm_back(dy, tok, gain, dh, out, ggain):
-    v = tok[...].astype(F32)
-    width = v.shape[1]
+def norm_back(dy, v, gain, dh):
     f = lax.rsqrt(jnp.mean(v * v, axis=1, keepdims=True) + epsilon)
-    ggain(jnp.sum(dy * v * f, axis=0, keepdims=True))
-    gdy = dy * gain[...]
-    lean = jnp.sum(gdy * v, axis=1, keepdims=True) * (f * f * f / width)
-    out[...] = (dh[...] + (f * gdy - v * lean)).astype(BF16)
-
-
-SMALL_ALL = 24
-SMALL_ROWS = 152
+    gdy = dy * gain
+    lean = jnp.sum(gdy * v, axis=1, keepdims=True) * (f * f * f / v.shape[1])
+    return dh + (f * gdy - v * lean)
+
+
+SMALL_ALL = 32
+SMALL_ROWS = 160
 
 
 def tail_kernel(
-    nt, tok, gain, dh, a1, dmix, o, m, dq, dz, dx, dkv, db, drow, wq, win, stp, wsh,
-    gg, gtb, gtx, grows, gheads, feed_own, feed_rest,
-    gt_o, mixed_o, fed_o, sh_o, small_o, norm_o,
-    da, parts, pieces, shared, ot, mt, bufs, landed, c_send, c_recv, *rest,
+    nt, tok_in, gain, dh_in, a1_in, dmix_in, o_in, m_in, dq, dz, dx, dkv, db, drow, wq, win, stp, wsh,
+    gg, gtb, gtx, grows, gheads, own_in, rest_in,
+    gt_o, mixed_o, fed_o, sh_o, small_o,
+    feed_own, a1, o, m, dmix, feed_rest, tok, dh, lsem,
+    da, gone, parts, pieces, shared, ot, mt, bufs, landed, c_send, c_recv, *rest,
 ):
     cube_a, rest = rest[:12], rest[12:]
     cube_b, rest = rest[:12], rest[12:]
     square_c, rest = rest[:8], rest[8:]
     (sh_sum, sh_land, sh_send, sh_recv) = rest[:4]
-    (sm_held, sm_land, sm_send, sm_recv, all_own, all_land, all_send, all_recv) = rest[4:12]
-    (ng_held, ng_land, ng_send, ng_recv, ngz_land, ngz_send, ngz_recv) = rest[12:]
+    (sm_held, sm_land, sm_send, sm_recv, all_own, all_land, all_send, all_recv) = rest[4:]
     d = lax.axis_index("dp")
     z = lax.axis_index("tensor")
     bits = dp_bits(d)
     peers = cube_peers(d)
     rows = tok.shape[0]
+    late = [
+        pltpu.make_async_copy(src, dst, lsem.at[i])
+        for i, (src, dst) in enumerate(
+            [(own_in, feed_own), (a1_in, a1), (o_in, o), (m_in, m), (dmix_in, dmix), (rest_in, feed_rest),
+             (tok_in, tok), (dh_in, dh)]
+        )
+    ]
+    for copy in late:
+        copy.start()
     greet([(p, z) for p in peers] + other_quarters(d, z, nt))
     three = SquareScatter(
         lambda i, j: (i, j), feed_own, square_c[:6], square_c[6], square_c[7], peers, bits, z
     )
-    three.start()
     chain = ChainScatter(parts, bufs, landed, c_send, c_recv, d, z, nt)
 
     def part(q):
@@ -1826,7 +1907,11 @@
         part(lax.rem(first + 1 + i, nt))
         return carry
 
+    late[0].wait()
+    three.start()
     lax.fori_loop(0, nt - 1, others, 0)
+    for copy in late[1:5]:
+        copy.wait()
     ot[...] = o[...].T
     mt[...] = m[...].T
 
@@ -1845,18 +1930,28 @@
     lax.fori_loop(0, 2, columns, 0)
     chain.step(1)
     lax.fori_loop(2, 4, columns, 0)
+    gone[...] = jnp.zeros(gone.shape, F32)
+
+    def gain_sums(q, carry):
+        at = pl.ds(pl.multiple_of(q * rows, rows), rows)
+        gone[...] += jnp.sum(parts[q].astype(F32) * a1[at, :].astype(F32), axis=0, keepdims=True)
+        return carry
+
+    lax.fori_loop(0, nt, gain_sums, 0)
+    gone[...] = gone[...] / gain[...]
     one = CubeScatter(pieces, cube_a, peers, bits, z)
     two = CubeScatter(shared, cube_b, peers, bits, z)
     sums = CubeTotal(sm_held, sm_land, sm_send, sm_recv, peers, z)
     for k in range(8):
         sm_held[0, k : k + 1, :] = gg[:, 128 * k : 128 * k + 128]
-    for first_row, ref in ((8, gtb), (SMALL_ALL, gtx), (48, grows)):
+        sm_held[0, 24 + k : 25 + k, :] = gone[:, 128 * k : 128 * k + 128]
+    for first_row, ref in ((8, gtb), (SMALL_ALL, gtx), (56, grows)):
         for k in range(ref.shape[1] // 128):
             sm_held[0, first_row + 8 * k : first_row + 8 * k + 8, :] = ref[:, 128 * k : 128 * k + 128]
-    sm_held[0, 72:88, :] = gheads[...]
+    sm_held[0, 80:96, :] = gheads[...]
     steps = dot_nn(drow[...].astype(BF16), a1[...])
     for k in range(8):
-        sm_held[0, 88 + 8 * k : 96 + 8 * k, :] = steps[:, 128 * k : 128 * k + 128]
+        sm_held[0, 96 + 8 * k : 104 + 8 * k, :] = steps[:, 128 * k : 128 * k + 128]
     sums.start(0)
     two.start()
     one.start()
@@ -1874,6 +1969,8 @@
     over_all = Exchange(all_own, all_land, all_send, all_recv, d, z, nt)
     over_all.start()
     three.finish(fed_o)
+    for copy in late[5:]:
+        copy.wait()
     fed_o[...] += feed_rest[...]
     two.last()
     one.last()
@@ -1888,34 +1985,18 @@
         )
         copies[-1].start()
     one.finish(mixed_o)
-    chain.finish(da)
-
-    def keep(row):
-        for k in range(8):
-            ng_held[0, k : k + 1, :] = row[:, 128 * k : 128 * k + 128]
-
-    norm_back(da[...], tok, gain, dh, gt_o, keep)
-    norms = CubeTotal(ng_held, ng_land, ng_send, ng_recv, peers, z)
-    norms.start(0)
     small_o[...] = sm_held[3]
     over_all.wait()
     small_o[0:SMALL_ALL, :] = over_all.total()
-    norms.take(0)
-    norms.start(1)
     for copy in copies:
         copy.wait()
     total = sh_sum[pl.ds(pl.multiple_of(z * per, per), per), :].astype(F32)
     for k in range(nt - 1):
         total = total + sh_land[k].astype(F32)
     sh_o[...] = total
-    norms.take(1)
-    norms.start(2)
-    norms.take(2)
-    last = Exchange(ng_held.at[3], ngz_land, ngz_send, ngz_recv, d, z, nt)
-    last.start()
-    last.wait()
-    norm_o[...] = last.total()
-    for thing in (chain, one, two, three, sums, norms):
+    chain.finish(da)
+    gt_o[...] = norm_back(da[...], tok[...].astype(F32), gain[...], dh[...]).astype(BF16)
+    for thing in (chain, one, two, three, sums):
         thing.drain()
 
 
@@ -1928,16 +2009,18 @@
     n, lanes = 256 + 3 * inner, 128
     s_rows, s_lanes = 128, args[16].shape[1]
     f_rows = feed_own.shape[2]
+    late = (len(args) - 2, 3, 5, 6, 4, len(args) - 1, 0, 2)
     dma = pltpu.SemaphoreType.DMA
     sds = jax.ShapeDtypeStruct
     vmem = pl.BlockSpec(memory_space=pltpu.VMEM)
     return pl.pallas_call(
         partial(tail_kernel, nt),
-        in_specs=[vmem] * len(args),
-        out_specs=[vmem] * 6,
+        in_specs=[pl.BlockSpec(memory_space=pl.ANY) if i in late else vmem for i in range(len(args))],
+        out_specs=[vmem] * 5,
         out_shape=[sds((rows, width), BF16), sds((n, lanes), F32), sds((f_rows, 128), F32),
-                   sds((s_rows // nt, s_lanes), F32), sds((SMALL_ROWS, 128), F32), sds((8, 128), F32)],
-        scratch_shapes=[pltpu.VMEM((rows, width), F32), pltpu.VMEM((nt, rows, width), BF16),
+                   sds((s_rows // nt, s_lanes), F32), sds((SMALL_ROWS, 128), F32)],
+        scratch_shapes=[pltpu.VMEM(args[i].shape, args[i].dtype) for i in late] + [dma((len(late),))]
+        + [pltpu.VMEM((rows, width), F32), pltpu.VMEM((1, width), F32), pltpu.VMEM((nt, rows, width), BF16),
                         pltpu.VMEM((4, 2, n, lanes), BF16), pltpu.VMEM((4, 2, s_rows, s_lanes), BF16),
                         pltpu.VMEM((128, total), BF16), pltpu.VMEM((inner, total), BF16)]
         + chain_scratch(nt, rows, width)
@@ -1946,9 +2029,7 @@
            dma((nt - 1,)), dma((nt - 1,)),
            pltpu.VMEM((4, SMALL_ROWS, 128), F32), pltpu.VMEM((3, SMALL_ROWS, 128), F32), dma((3,)), dma((3,)),
            pltpu.VMEM((SMALL_ALL, 128), F32), pltpu.VMEM((nt - 1, SMALL_ALL, 128), F32), dma((nt - 1,)),
-           dma((nt - 1,)),
-           pltpu.VMEM((4, 8, 128), F32), pltpu.VMEM((3, 8, 128), F32), dma((3,)), dma((3,)),
-           pltpu.VMEM((nt - 1, 8, 128), F32), dma((nt - 1,)), dma((nt - 1,))],
+           dma((nt - 1,))],
         compiler_params=pltpu.CompilerParams(
             vmem_limit_bytes=VMEM_LIMIT, collective_id=3, has_side_effects=True
         ),
@@ -1958,9 +2039,12 @@
 
 
 def finish_kernel(
-    heads, place, mixed, fed, small, norm,
-    que_o, att_o, inn_o, mam_o, hid_o, dwn_o, norms_o, taps_o, chan_o, gain_o, step_o, heads_o,
+    heads, place, mixed, fed, small, *refs
 ):
+    (que_o, att_o, inn_o, mam_o, hid_o, dwn_o, norms_o, taps_o, chan_o, gain_o, step_o) = refs[-17:-6]
+    heads_o = refs[-6:-3]
+    for src, dst in zip(refs[:3], refs[-3:]):
+        dst[...] = src[...]
     d, p = place[0], place[1]
     block = que_o.shape[0]
     inner = mam_o.shape[0]
@@ -1987,8 +2071,9 @@
 
     width = norms_o.shape[1]
     per = 128 // width
-    for i, ref in enumerate((norm, small)):
-        row = lanes_from(jnp.broadcast_to(ref[pl.ds(p // per, 1), :], (8, 128)), lax.rem(p, per) * width)
+    for i, base in enumerate((24, 0)):
+        row = jnp.broadcast_to(small[pl.ds(base + p // per, 1), :], (8, 128))
+        row = lanes_from(row, lax.rem(p, per) * width)
         norms_o[i : i + 1, :] = row[0:1, 0:width]
     width = taps_o.shape[1]
     per = 128 // width
@@ -2000,7 +2085,7 @@
     sub = lax.broadcasted_iota(jnp.int32, sums.shape, 0)
     for b in range(heads // 2):
         rows = lanes_from(small[SMALL_ALL + 8 * b : SMALL_ALL + 8 * b + 8, :], d * width)
-        raw = small[48 + 8 * b : 56 + 8 * b, :]
+        raw = small[56 + 8 * b : 64 + 8 * b, :]
         gains = lanes_from(raw, d * width)
         for k in range(2):
             h = 2 * b + k
@@ -2010,25 +2095,27 @@
             skip = jnp.sum(jnp.where(lane // SSM_DIM == k, raw[1:2, :], 0.0), axis=1, keepdims=True)
             sums = jnp.where((sub == h) & (lane == 2), skip, sums)
     for k in range(2):
-        total = jnp.sum(small[72 + 8 * k : 80 + 8 * k, :], axis=1, keepdims=True)
+        total = jnp.sum(small[80 + 8 * k : 88 + 8 * k, :], axis=1, keepdims=True)
         sums = jnp.where(lane == k, total, sums)
-    heads_o[...] = sums
-    steps = small[pl.ds(pl.multiple_of(88 + 8 * d, 8), 8), :]
-    steps = jnp.concatenate([steps, jnp.zeros((120, 128), F32)], axis=0).T
-    step_o[...] = steps[:, 0:heads]
-
-
-def finish(heads, place, mixed, fed, small, norm, shapes):
+    sums = jnp.concatenate([sums, jnp.zeros((120, 128), F32)], axis=0).T
+    for k in range(3):
+        heads_o[k][...] = sums[k : k + 1, 0:heads]
+    steps = small[pl.ds(pl.multiple_of(96 + 8 * d, 8), 8), :]
+    step_o[...] = steps[0:heads, :]
+
+
+def finish(heads, place, mixed, fed, small, shapes, passed):
     vmem = pl.BlockSpec(memory_space=pltpu.VMEM)
     sds = jax.ShapeDtypeStruct
     return pl.pallas_call(
         partial(finish_kernel, heads),
-        in_specs=[pl.BlockSpec(memory_space=pltpu.SMEM)] + [vmem] * 4,
-        out_specs=[vmem] * (len(shapes) + 1),
-        out_shape=[sds(s, F32) for s in shapes] + [sds((8, 128), F32)],
+        in_specs=[pl.BlockSpec(memory_space=pltpu.SMEM)] + [vmem] * 6,
+        out_specs=[vmem] * (len(shapes) + 6),
+        out_shape=[sds(s, F32) for s in shapes] + [sds((1, heads), F32)] * 3
+        + [sds(v.shape, v.dtype) for v in passed],
         compiler_params=pltpu.CompilerParams(vmem_limit_bytes=VMEM_LIMIT),
         name="finish",
-    )(place, mixed, fed, small, norm)
+    )(place, mixed, fed, small, *passed)
 
 
 def rope_wide(length):
@@ -2081,7 +2168,7 @@
     units = down_proj.shape[0]
     feed = ()
     if nd == 8:
-        small = pack_small(channel_taps, mixer_gain, norm_gains, shared_taps, step_proj)
+        small = pack_small(channel_taps, mixer_gain, norm_gains, shared_taps, step_proj.T)
         (tok_full, full_query, full_attend, full_inner, full_mamba, sha, sma) = gather_start(
             tokens, query_proj, attend_out, inner_proj, mamba_out, shared_proj, small, nd, nt
         )
@@ -2146,7 +2233,7 @@
     if nd == 8:
         full_hidden, full_down = mixed[3:]
     if nd == 8:
-        layer_out, dh, grad_gain_two, grad_mix, do, dm, dots, feed_own, feed_sums = feed_unmix(
+        layer_out, dh, grad_gain_two, grad_mix, do, dm, dots, feed_own, feed_raw, feed_sums = feed_unmix(
             nt, hidden, gain_second, cotangent, full_hidden, full_down, y, zr, gain_mix, full_attend, full_mamba
         )
         feed_own = feed_own.reshape((2, 2) + feed_own.shape[1:])
@@ -2166,7 +2253,8 @@
 
     back = mixers_back(
         heads, channels, nt, kv_head, q, k2, v2, lse, do, cosine, sine, dm, y, zr, xr, br, trow, states,
-        squares, dots, gain_mix, taps_x, taps_b, decay, bias, skip, feed_sums if nd == 8 else None,
+        squares, dots, gain_mix, taps_x, taps_b, decay, bias, skip,
+        (feed_sums, feed_raw) if nd == 8 else None,
     )
     dq, dkv, dz, dx, db, drow, grad_tx, grad_tb, grad_rows, grad_heads = back[:10]
     if nd == 8:
@@ -2174,12 +2262,12 @@
             nt, tokens, gain_first, dh, a1, grad_mix, o, m, dq, dz, dx, dkv, db, drow, full_query, full_inner,
             step_rows, full_shared, grad_gain_two, grad_tb, grad_tx, grad_rows, grad_heads, feed_own, back[10],
         )
-        gradient_tokens, mixed, fed, gradient_shared, small_sums, grad_gain_one = sums
+        gradient_tokens, mixed, fed, gradient_shared, small_sums = sums
         place = jnp.stack([d, d * nt + tensor_index]).astype(jnp.int32)
         shapes = [
             query_proj.shape, attend_out.shape, inner_proj.shape, mamba_out.shape, hidden_proj.shape,
             down_proj.shape, norm_gains.shape, shared_taps.shape, channel_taps.shape, mixer_gain.shape,
-            step_proj.shape,
+            step_proj.T.shape,
         ]
         (
             gradient_query,
@@ -2193,23 +2281,30 @@
             gradient_channel,
             gradient_mixer,
             gradient_step,
-            head_sums,
-        ) = finish(heads, place, mixed, fed, small_sums, grad_gain_one, shapes)
+            gradient_decay,
+            gradient_bias,
+            gradient_skip,
+            layer_out,
+            gradient_tokens,
+            gradient_shared,
+        ) = finish(
+            heads, place, mixed, fed, small_sums, shapes, (layer_out, gradient_tokens, gradient_shared)
+        )
         return (
             layer_out,
             gradient_tokens,
             gradient_query,
             gradient_attend,
             gradient_inner,
-            gradient_step,
+            gradient_step.T,
             gradient_mamba,
             gradient_hidden,
             gradient_down,
             gradient_channel,
             gradient_mixer,
-            head_sums[:heads, 0],
-            head_sums[:heads, 1],
-            head_sums[:heads, 2],
+            gradient_decay.reshape(heads),
+            gradient_bias.reshape(heads),
+            gradient_skip.reshape(heads),
             gradient_shared,
             gradient_norms,
             gradient_taps,

time: 317 us -> 294 us (0.927)
  Pallas kernels: 307 us -> 291 us
  local copies, waits for them, and re-layouts: 6.67 us -> 0 us
    pallas_call x1, Pallas kernels: 65.6 us -> 51.9 us  [tail(): pl.pallas_call(partial(tail_kernel, nt), in_specs=[pl.BlockSpec(memory_sp...]
    pallas_call x1, Pallas kernels: 71.8 us -> 66.4 us  [feed_unmix(): pl.pallas_call(partial(feed_unmix_kernel, nt), grid=(2 * tiles,), in_spec...]
    unnamed x11 -> x0, local copies, waits for them, and re-layouts: 5.14 us -> none
    pallas_call x1, Pallas kernels: 35.4 us -> 39 us  [mixers_back(): pl.pallas_call(partial(back_kernel, heads, channels, nt, feed is not None...]
where the time goes in v1:
time: 294 us; the launch traced here: 293 us
  Pallas kernels  291 us (99%)
    pallas_call x1, Pallas kernels, feed_unmix(): pl.pallas_call(partial(feed_unmix_kernel, nt), grid=(2 * tiles,), in_spec...  66.4 us
    pallas_call x1, Pallas kernels, tail(): pl.pallas_call(partial(tail_kernel, nt), in_specs=[pl.BlockSpec(memory_sp...  51.9 us
    pallas_call x1, Pallas kernels, mix_scatter(): pl.pallas_call(partial(mix_scatter_kernel, channels, nt, bool(feed)), in_...  48.3 us
    pallas_call x1, Pallas kernels, gather_start(): pl.pallas_call(partial(gather_kernel, nt), out_shape=[jax.ShapeDtypeStruc...  47 us
    pallas_call x1, Pallas kernels, mixers_back(): pl.pallas_call(partial(back_kernel, heads, channels, nt, feed is not None...  39 us
    pallas_call x1, Pallas kernels, mixers_forward(): pl.pallas_call(partial(forward_kernel, heads, nt, bool(feed)), grid=(tota...  31.5 us

profile of v1, /device:TPU:0, one launch (start us, length us, event | category | flops | bytes accessed | tf_op | source)
XLA Modules:
  0.0 293.4 jit_solution(9845194097936297566)
XLA Ops:
  0.7 0.7 pad_add_fusion.place
  1.3 1.3 maximum_convert_fusion.scal
  2.6 1.4 pack_small.1.refs_6_
  4.0 47.0 %gather_start.1 = (bf16[4,256,1024]{2,1,0:T(8,128)(2,1)}, bf16[1024,128]{1,0:T(8,128)(2,1)}, bf16[128,1024]{1,0:T(8,128)(2,1)}, bf16[2,1024,384]{2,1,0:T(8,128)(...) custom-call(bf16[256,1024]{1,0:T(8,128)(2,1)} %tok_in.1, ...), custom_call_target="tpu_custom_call" | custom-call | tf_op jit(solution)/shard_map/gather_start/pallas_call | solution.py:197
  51.1 1.7 unpack_small.1
  52.8 31.5 %mixers_forward.1 = (bf16[1024,1024]{1,0:T(8,128)(2,1)}, bf16[1024,128]{1,0:T(8,128)(2,1)}, bf16[1024,128]{1,0:T(8,128)(2,1)}, bf16[1024,128]{1,0:T(8,128)(2,1)}...) custom-call(s32[1]{0:T(128)} %bitcast.7.refs_0_.refs_2_, ...), custom_call_target="tpu_custom_call" | custom-call | flops 5000000000 | bytes 15000000 | tf_op jit(solution)/shard_map/mixers_forward/pallas_call | solution.py:616
  84.3 48.3 %mix_scatter.1 = (bf16[1024,384]{1,0:T(8,128)(2,1)}, f32[8,1024]{1,0:T(8,128)}, f32[256,1024]{1,0:T(8,128)}, bf16[8,4,2,128,512]{4,3,2,1,0:T(8,128)(2,1)}, bf16[8,4,512,128]{3,2,1,0:T(8,128)(2,1)}) custom-call(bf16[1024,128]{1,0:T(8,128)(2,1)} %get-tuple-element.110.refs_0_.o_in, ...), custom_call_target="tpu_custom_call", output_to_operand_aliasing={{3}: (8, {}), {4}: (9, {})} | custom-call | flops 1000000000 | bytes 130000000 | tf_op jit(solution)/shard_map/mix_scatter/pallas_call | solution.py:1367
  132.6 66.4 %feed_unmix.1 = (bf16[256,1024]{1,0:T(8,128)(2,1)}, f32[256,1024]{1,0:T(8,128)}, f32[1,1024]{1,0:T(1,128)}, bf16[1024,1024]{1,0:T(8,128)(2,1)}, bf16[1024,128]{1...) custom-call(f32[256,1024]{1,0:T(8,128)} %get-tuple-element.121.refs_, ...), custom_call_target="tpu_custom_call" | custom-call | flops 10000000000 | bytes 150000000 | tf_op jit(solution)/shard_map/feed_unmix/pallas_call | solution.py:1708
  198.9 39.0 %mixers_back.1 = (bf16[1024,128]{1,0:T(8,128)(2,1)}, bf16[1024,256]{1,0:T(8,128)(2,1)}, bf16[1024,384]{1,0:T(8,128)(2,1)}, bf16[1024,384]{1,0:T(8,128)(2,1)}, bf...) custom-call(bf16[2,1536,128]{2,1,0:T(8,128)(2,1)} %get-tuple-element, ...), custom_call_target="tpu_custom_call" | custom-call | flops 6000000000 | bytes 18000000 | tf_op jit(solution)/shard_map/mixers_back/pallas_call | solution.py:941
  238.0 51.9 %tail.1 = (bf16[256,1024]{1,0:T(8,128)(2,1)}, f32[1408,128]{1,0:T(8,128)}, f32[1536,128]{1,0:T(8,128)}, f32[32,512]{1,0:T(8,128)}, f32[160,128]{1,0:T(8,128)}) custom-call(bf16[256,1024]{1,0:T(8,128)(2,1)} %tok_in.1, f32[1,1024]{1,0:T(1,128)} %get-tuple-element.99.refs_2_.gain, f32[256,1024]{1,0:T(8,128)} %get-tuple-element.125.dh_in, ...), custom_call_target="tpu_custom_call" | custom-call | flops 7000000000 | bytes 150000000 | tf_op jit(solution)/shard_map/tail/pallas_call | solution.py:2016
  289.9 3.4 %finish.1 = (f32[128,128]{1,0:T(8,128)}, f32[128,128]{1,0:T(8,128)}, f32[2,128,384]{2,1,0:T(8,128)}, f32[384,128]{1,0:T(8,128)}, f32[2,128,512]{2,1,0:T(8,128)},...) custom-call(s32[2]{0:T(128)} %pad_add_fusion.place, ...), custom_call_target="tpu_custom_call" | custom-call | tf_op jit(solution)/shard_map/finish/pallas_call | solution.py:2110

commit v2 on v1

--- a/solution.py
+++ b/solution.py
@@ -398,6 +398,13 @@
     for j in range(1, CONV):
         total = total + taps[j : j + 1, :] * ref[pl.ds(first + j, rows), :]
     return total
+
+
+def quarter_at(i, z, nt):
+    near = jnp.where(z < nt - 1, z + 1, z - 1)
+    far = jnp.where(z < nt - 1, lax.rem(z + 3, nt), lax.rem(z + 1, nt))
+    order = jnp.where(i == 0, lax.rem(z + 2, nt), far)
+    return jnp.where(i == 2, near, jnp.where(i == 3, z, order))
 
 
 class FeedGather:
@@ -693,30 +700,29 @@
         z = lax.axis_index("tensor")
         sums, raw, refs = refs[0], refs[1], refs[2:]
         feed_o, refs = refs[37], refs[:37] + refs[38:]
-        (came, f_send, f_recv, held), box, refs = refs[44:48], refs[48:56], refs[:44]
+        parts, chain_boxes, box, refs = refs[44], refs[45:49], refs[49:57], refs[:44]
         peers = cube_peers(d)
         square = SquareScatter(
             lambda i, j: (2 * i + j,), raw, box[:6], box[6], box[7], peers, dp_bits(d), z
         )
-        sources = [sums.at[k] for k in range(nt - 2)] + [held]
-        copies = [
-            remote_copy(sources[k], came.at[k], f_send.at[k], f_recv.at[k], peer)
-            for k, peer in enumerate(other_quarters(d, z, nt))
-        ]
+        chain = ChainScatter(parts, *chain_boxes, d, z, nt)
 
         @pl.when(step == 0)
         def _():
             greet([(p, z) for p in peers[1:]] + other_quarters(d, z, nt))
-            for copy in copies[:-1]:
-                copy.start()
+            for k in range(nt - 2):
+                parts[quarter_at(k, z, nt)] = sums[k]
+            parts[z] = jnp.zeros(parts.shape[1:], BF16)
+            chain.step(0)
             square.start()
 
+        pl.when(step == 3)(lambda: chain.step(1))
         pl.when(step == 3)(square.middle)
 
-        @pl.when(step == 4)
+        @pl.when(step == 5)
         def _():
-            square.finish(held)
-            copies[-1].start()
+            square.finish(parts.at[quarter_at(nt - 2, z, nt)])
+            chain.step(2)
 
     attend_back(step, *refs[:10], *refs[27:29], *refs[37:39])
     scan_back(heads, channels, step, *refs[10:27], *refs[29:37], *refs[39:44])
@@ -724,12 +730,8 @@
 
         @pl.when(step == pl.num_programs(0) - 1)
         def _():
-            total = None
-            for k, copy in enumerate(copies):
-                copy.wait()
-                value = came[k].astype(F32)
-                total = value if total is None else total + value
-            feed_o[...] = total
+            chain.finish(feed_o)
+            chain.drain()
             square.drain()
 
 
@@ -929,14 +931,13 @@
             rsum, dots, gain, tapx, tapb, decay, bias, skip]
     extra = {}
     if feed is not None:
-        dma = pltpu.SemaphoreType.DMA
         piece = feed[0].shape[1:]
         args = list(feed) + args
         in_specs = [whole(v) for v in feed] + in_specs
         out_specs = out_specs + [fixed(*piece)]
         out_shape = out_shape + [sds(piece, F32)]
-        scratch = scratch + [pltpu.VMEM((nt - 1,) + piece, BF16), dma((nt - 1,)), dma((nt - 1,)),
-                             pltpu.VMEM(piece, BF16)] + square_scratch(*piece)
+        scratch = scratch + [pltpu.VMEM((nt,) + piece, BF16)] + chain_scratch(nt, *piece)
+        scratch = scratch + square_scratch(*piece)
         extra = dict(collective_id=5, has_side_effects=True)
     return pl.pallas_call(
         partial(back_kernel, heads, channels, nt, feed is not None),
@@ -1527,7 +1528,7 @@
     chain = ChainGather(dmix, slots, g_send, g_recv, d, z, nt)
     cubes = []
     for k in range(1, nt - 1):
-        q = lax.rem(z + k, nt)
+        q = quarter_at(k - 1, z, nt)
         box = boxes[8 * k - 8 : 8 * k]
         cubes.append(
             SquareScatter(lambda i, j, q=q: (2 * i + j, q), piece, box[:6], box[6], box[7], peers, bits, z)
@@ -1556,7 +1557,7 @@
                 (dh, dh_o),
                 (dmix, g_o.at[rows_of(z)]),
                 (piece.at[:, z], own_o),
-                (piece.at[:, lax.rem(z + nt - 1, nt)], raw_o),
+                (piece.at[:, quarter_at(2, z, nt)], raw_o),
             )
         )
     ]
@@ -1590,7 +1591,7 @@
         )
 
     def places(turn_):
-        quarter = lax.rem(z + 1 + turn_ // tiles_per, nt)
+        quarter = quarter_at(turn_ // tiles_per, z, nt)
         part = lax.rem(turn_, tiles_per)
         return quarter, part, piece_rows(part, units, quarter_units)
 
@@ -1622,6 +1623,7 @@
             sent[box, :, first : first + n, :] = jnp.where(core == 0, odd, even)
             first += n
         swap(turn_).start()
+        pl.when(turn_ == tiles - 1)(lambda: chain.hop(1))
         pl.when(turn_ >= 1)(lambda: take(turn_ - 1))
         for k in range(1, nt - 1):
             pl.when(turn_ == k * tiles_per)(cubes[k - 1].start)
@@ -1644,7 +1646,8 @@
             store_dm(q).start()
 
         for dist in range(1, nt):
-            chain.hop(dist)
+            if dist > 1:
+                chain.hop(dist)
             work.around(z, dist, nt, slots, after)
             if dist == 1:
                 cubes[0].middle()
@@ -1792,22 +1795,22 @@
 
 class CubeScatter:
     def __init__(self, pieces, bufs, peers, bits, z):
-        (self.rc, self.held, send, recv) = bufs[:4]
+        (self.rc, self.held, self.send, self.recv) = bufs[:4]
         self.p = pieces
         self.core = bits[0]
-        self.first = remote_copy(
-            pieces.at[:, 1 - self.core], self.rc, send.at[0], recv.at[0], (peers[0], z)
-        )
+        self.peer = (peers[0], z)
         self.square = SquareScatter(
             lambda i, j: (2 * i + j,), self.held, bufs[4:10], bufs[10], bufs[11], peers, bits, z
         )
 
-    def start(self):
-        self.first.start()
+    def swap(self, i):
+        return remote_copy(
+            self.p.at[i, 1 - self.core], self.rc.at[i], self.send.at[i], self.recv.at[i], self.peer
+        )
 
     def middle(self):
-        self.first.wait_recv()
         for i in range(4):
+            self.swap(i).wait_recv()
             self.held[i] = add_refs(self.p[i, self.core], self.rc[i]).astype(BF16)
         self.square.start()
 
@@ -1818,7 +1821,8 @@
         self.square.finish(out)
 
     def drain(self):
-        self.first.wait_send()
+        for i in range(4):
+            self.swap(i).wait_send()
         self.square.drain()
 
 
@@ -1827,8 +1831,8 @@
     return [
         pltpu.VMEM((4, n, lanes), BF16),
         pltpu.VMEM((4, n, lanes), BF16),
-        dma((1,)),
-        dma((1,)),
+        dma((4,)),
+        dma((4,)),
     ] + square_scratch(n, lanes)
 
 
@@ -1912,24 +1916,6 @@
     lax.fori_loop(0, nt - 1, others, 0)
     for copy in late[1:5]:
         copy.wait()
-    ot[...] = o[...].T
-    mt[...] = m[...].T
-
-    def columns(i, carry):
-        at = pl.ds(pl.multiple_of(i * 256, 256), 256)
-
-        def put(k, first, values):
-            pieces[i, k, first : first + values.shape[0], :] = values
-
-        def put_shared(k, first, values):
-            shared[i, k, :, first : first + values.shape[1]] = values
-
-        weight_columns(a1[:, at], dmix[:, at], dq, dz, dx, dkv, db, ot, mt, put, put_shared)
-        return carry
-
-    lax.fori_loop(0, 2, columns, 0)
-    chain.step(1)
-    lax.fori_loop(2, 4, columns, 0)
     gone[...] = jnp.zeros(gone.shape, F32)
 
     def gain_sums(q, carry):
@@ -1939,8 +1925,6 @@
 
     lax.fori_loop(0, nt, gain_sums, 0)
     gone[...] = gone[...] / gain[...]
-    one = CubeScatter(pieces, cube_a, peers, bits, z)
-    two = CubeScatter(shared, cube_b, peers, bits, z)
     sums = CubeTotal(sm_held, sm_land, sm_send, sm_recv, peers, z)
     for k in range(8):
         sm_held[0, k : k + 1, :] = gg[:, 128 * k : 128 * k + 128]
@@ -1953,17 +1937,39 @@
     for k in range(8):
         sm_held[0, 96 + 8 * k : 104 + 8 * k, :] = steps[:, 128 * k : 128 * k + 128]
     sums.start(0)
-    two.start()
-    one.start()
+    ot[...] = o[...].T
+    mt[...] = m[...].T
+
+    def columns(i, carry):
+        at = pl.ds(pl.multiple_of(i * 256, 256), 256)
+
+        def put(k, first, values):
+            pieces[i, k, first : first + values.shape[0], :] = values
+
+        def put_shared(k, first, values):
+            shared[i, k, :, first : first + values.shape[1]] = values
+
+        weight_columns(a1[:, at], dmix[:, at], dq, dz, dx, dkv, db, ot, mt, put, put_shared)
+        two.swap(i).start()
+        one.swap(i).start()
+        return carry
+
+    one = CubeScatter(pieces, cube_a, peers, bits, z)
+    two = CubeScatter(shared, cube_b, peers, bits, z)
+    lax.fori_loop(0, 1, columns, 0)
+    chain.step(1)
     three.middle()
     sums.take(0)
     sums.start(1)
+    lax.fori_loop(1, 4, columns, 0)
+    sums.take(1)
+    sums.start(2)
     two.middle()
     one.middle()
-    sums.take(1)
-    sums.start(2)
     for t in range(2, nt - 1):
         chain.step(t)
+    two.last()
+    one.last()
     sums.take(2)
     all_own[...] = sm_held[3, 0:SMALL_ALL, :]
     over_all = Exchange(all_own, all_land, all_send, all_recv, d, z, nt)
@@ -1972,8 +1978,6 @@
     for copy in late[5:]:
         copy.wait()
     fed_o[...] += feed_rest[...]
-    two.last()
-    one.last()
     two.finish(sh_sum)
     per = sh_sum.shape[0] // nt
     copies = []

time: 294 us -> 286 us (0.973)
  Pallas kernels: 291 us -> 283 us
    pallas_call x1, Pallas kernels: 51.9 us -> 47.7 us  [tail(): pl.pallas_call(partial(tail_kernel, nt), in_specs=[pl.BlockSpec(memory_sp...]
where the time goes in v2:
time: 286 us
  Pallas kernels  283 us (99%)
    pallas_call x1, Pallas kernels, feed_unmix(): pl.pallas_call(partial(feed_unmix_kernel, nt), grid=(2 * tiles,), in_spec...  64.8 us
    pallas_call x1, Pallas kernels, mix_scatter(): pl.pallas_call(partial(mix_scatter_kernel, channels, nt, bool(feed)), in_...  48.3 us
    pallas_call x1, Pallas kernels, tail(): pl.pallas_call(partial(tail_kernel, nt), in_specs=[pl.BlockSpec(memory_sp...  47.7 us
    pallas_call x1, Pallas kernels, gather_start(): pl.pallas_call(partial(gather_kernel, nt), out_shape=[jax.ShapeDtypeStruc...  47 us
    pallas_call x1, Pallas kernels, mixers_back(): pl.pallas_call(partial(back_kernel, heads, channels, nt, feed is not None...  37.2 us
    pallas_call x1, Pallas kernels, mixers_forward(): pl.pallas_call(partial(forward_kernel, heads, nt, bool(feed)), grid=(tota...  31.5 us

profile of v2, /device:TPU:0, one launch (start us, length us, event | category | flops | bytes accessed | tf_op | source)
XLA Modules:
  0.0 285.7 jit_solution(813072939792811053)
XLA Ops:
  0.7 0.7 pad_add_fusion.place
  1.3 1.3 maximum_convert_fusion.scal
  2.6 1.4 pack_small.1.refs_6_
  4.0 47.0 %gather_start.1 = (bf16[4,256,1024]{2,1,0:T(8,128)(2,1)}, bf16[1024,128]{1,0:T(8,128)(2,1)}, bf16[128,1024]{1,0:T(8,128)(2,1)}, bf16[2,1024,384]{2,1,0:T(8,128)(...) custom-call(bf16[256,1024]{1,0:T(8,128)(2,1)} %tok_in.1, ...), custom_call_target="tpu_custom_call" | custom-call | tf_op jit(solution)/shard_map/gather_start/pallas_call | solution.py:197
  51.1 1.7 unpack_small.1
  52.8 31.5 %mixers_forward.1 = (bf16[1024,1024]{1,0:T(8,128)(2,1)}, bf16[1024,128]{1,0:T(8,128)(2,1)}, bf16[1024,128]{1,0:T(8,128)(2,1)}, bf16[1024,128]{1,0:T(8,128)(2,1)}...) custom-call(s32[1]{0:T(128)} %bitcast.7.refs_0_.refs_2_, ...), custom_call_target="tpu_custom_call" | custom-call | flops 5000000000 | bytes 15000000 | tf_op jit(solution)/shard_map/mixers_forward/pallas_call | solution.py:623
  84.3 48.3 %mix_scatter.1 = (bf16[1024,384]{1,0:T(8,128)(2,1)}, f32[8,1024]{1,0:T(8,128)}, f32[256,1024]{1,0:T(8,128)}, bf16[8,4,2,128,512]{4,3,2,1,0:T(8,128)(2,1)}, bf16[8,4,512,128]{3,2,1,0:T(8,128)(2,1)}) custom-call(bf16[1024,128]{1,0:T(8,128)(2,1)} %get-tuple-element.110.refs_0_.o_in, ...), custom_call_target="tpu_custom_call", output_to_operand_aliasing={{3}: (8, {}), {4}: (9, {})} | custom-call | flops 1000000000 | bytes 130000000 | tf_op jit(solution)/shard_map/mix_scatter/pallas_call | solution.py:1368
  132.6 64.8 %feed_unmix.1 = (bf16[256,1024]{1,0:T(8,128)(2,1)}, f32[256,1024]{1,0:T(8,128)}, f32[1,1024]{1,0:T(1,128)}, bf16[1024,1024]{1,0:T(8,128)(2,1)}, bf16[1024,128]{1...) custom-call(f32[256,1024]{1,0:T(8,128)} %get-tuple-element.121.refs_, ...), custom_call_target="tpu_custom_call" | custom-call | flops 10000000000 | bytes 150000000 | tf_op jit(solution)/shard_map/feed_unmix/pallas_call | solution.py:1711
  197.3 37.2 %mixers_back.1 = (bf16[1024,128]{1,0:T(8,128)(2,1)}, bf16[1024,256]{1,0:T(8,128)(2,1)}, bf16[1024,384]{1,0:T(8,128)(2,1)}, bf16[1024,384]{1,0:T(8,128)(2,1)}, bf...) custom-call(bf16[2,1536,128]{2,1,0:T(8,128)(2,1)} %get-tuple-element, ...), custom_call_target="tpu_custom_call" | custom-call | flops 6000000000 | bytes 18000000 | tf_op jit(solution)/shard_map/mixers_back/pallas_call | solution.py:942
  234.5 47.7 %tail.1 = (bf16[256,1024]{1,0:T(8,128)(2,1)}, f32[1408,128]{1,0:T(8,128)}, f32[1536,128]{1,0:T(8,128)}, f32[32,512]{1,0:T(8,128)}, f32[160,128]{1,0:T(8,128)}) custom-call(bf16[256,1024]{1,0:T(8,128)(2,1)} %tok_in.1, f32[1,1024]{1,0:T(1,128)} %get-tuple-element.99.refs_2_.gain, f32[256,1024]{1,0:T(8,128)} %get-tuple-element.125.dh_in, ...), custom_call_target="tpu_custom_call" | custom-call | flops 7000000000 | bytes 150000000 | tf_op jit(solution)/shard_map/tail/pallas_call | solution.py:2020
  282.2 3.4 %finish.1 = (f32[128,128]{1,0:T(8,128)}, f32[128,128]{1,0:T(8,128)}, f32[2,128,384]{2,1,0:T(8,128)}, f32[384,128]{1,0:T(8,128)}, f32[2,128,512]{2,1,0:T(8,128)},...) custom-call(s32[2]{0:T(128)} %pad_add_fusion.place, ...), custom_call_target="tpu_custom_call" | custom-call | tf_op jit(solution)/shard_map/finish/pallas_call | solution.py:2114

commit v3 on v2

--- a/solution.py
+++ b/solution.py
@@ -680,7 +680,7 @@
         dq_o[...] = turn(jnp.where(low, dqs[0], dqs[1]), cosine[...], -sine[...]).astype(BF16)
 
     for i in range(steps):
-        pl.when(step == 2 * i)(partial(back, i + 1))
+        pl.when(step == 2 * (steps - 1 - i))(partial(back, i + 1))
 
     @pl.when(step == 2 * steps - 1)
     def _():
@@ -700,12 +700,14 @@
         z = lax.axis_index("tensor")
         sums, raw, refs = refs[0], refs[1], refs[2:]
         feed_o, refs = refs[37], refs[:37] + refs[38:]
-        parts, chain_boxes, box, refs = refs[44], refs[45:49], refs[49:57], refs[:44]
+        parts, chain_boxes, box = refs[44], refs[45:49], refs[49:57]
+        (dot_sum, dot_land, d_send, d_recv), refs = refs[57:61], refs[:44]
         peers = cube_peers(d)
         square = SquareScatter(
             lambda i, j: (2 * i + j,), raw, box[:6], box[6], box[7], peers, dp_bits(d), z
         )
         chain = ChainScatter(parts, *chain_boxes, d, z, nt)
+        dots = Exchange(refs[20], dot_land, d_send, d_recv, d, z, nt)
 
         @pl.when(step == 0)
         def _():
@@ -713,6 +715,7 @@
             for k in range(nt - 2):
                 parts[quarter_at(k, z, nt)] = sums[k]
             parts[z] = jnp.zeros(parts.shape[1:], BF16)
+            dots.start()
             chain.step(0)
             square.start()
 
@@ -725,6 +728,15 @@
             chain.step(2)
 
     attend_back(step, *refs[:10], *refs[27:29], *refs[37:39])
+    if feed:
+
+        @pl.when(step == 0)
+        def _():
+            dots.wait()
+            dot_sum[...] = dots.total()
+
+        at = pl.ds(pl.multiple_of((pl.num_programs(0) - 1 - step) * block_len, block_len), block_len)
+        refs = refs[:20] + (dot_sum.at[:, at],) + refs[21:]
     scan_back(heads, channels, step, *refs[10:27], *refs[29:37], *refs[39:44])
     if feed:
 
@@ -907,14 +919,14 @@
         return pl.BlockSpec((8, n), lambda i: (jnp.maximum((steps - 1 - i) * per - 1, 0), 0))
 
     wide = pl.BlockSpec((8, rows), lambda i: (0, steps - 1 - i))
-    ask = pl.BlockSpec((q_rows, 128), lambda i: (i // 2, 0))
+    ask = pl.BlockSpec((q_rows, 128), lambda i: (steps // 2 - 1 - i // 2, 0))
     sds = jax.ShapeDtypeStruct
 
     def fixed(*shape):
         return pl.BlockSpec(shape, lambda i: (0,) * len(shape))
 
     in_specs = [pl.BlockSpec(memory_space=pltpu.SMEM), ask, whole(k2), whole(v2),
-                pl.BlockSpec((8, q_rows), lambda i: (0, i // 2)), ask, ask, ask, whole(cosine), whole(sine),
+                pl.BlockSpec((8, q_rows), lambda i: (0, steps // 2 - 1 - i // 2)), ask, ask, ask, whole(cosine), whole(sine),
                 tall(inner), tall(inner), tall(inner), tall(inner), before(inner), tall(pair),
                 before(pair), wide, pl.BlockSpec((1, pair // 2, inner), lambda i: (steps - 1 - i, 0, 0)),
                 wide, wide, whole(gain), whole(tapx), whole(tapb), whole(decay), whole(bias), whole(skip)]
@@ -932,12 +944,16 @@
     extra = {}
     if feed is not None:
         piece = feed[0].shape[1:]
+        dma = pltpu.SemaphoreType.DMA
+        in_specs[20] = whole(dots)
         args = list(feed) + args
         in_specs = [whole(v) for v in feed] + in_specs
         out_specs = out_specs + [fixed(*piece)]
         out_shape = out_shape + [sds(piece, F32)]
         scratch = scratch + [pltpu.VMEM((nt,) + piece, BF16)] + chain_scratch(nt, *piece)
         scratch = scratch + square_scratch(*piece)
+        scratch = scratch + [pltpu.VMEM(dots.shape, F32), pltpu.VMEM((nt - 1,) + dots.shape, F32),
+                             dma((nt - 1,)), dma((nt - 1,))]
         extra = dict(collective_id=5, has_side_effects=True)
     return pl.pallas_call(
         partial(back_kernel, heads, channels, nt, feed is not None),
@@ -1297,14 +1313,19 @@
     greet(peers + other_quarters(d, z, nt))
     squares = Exchange(sq, sq_land, sq_send, sq_recv, d, z, nt)
     squares.start()
-    n = 2 * (nt - 1)
+    n = 2 * nt - 1
     if feed:
         items = []
         for k in range(1, nt):
             q = lax.rem(z - k + nt, nt)
             items.append((hid_z.at[q], lambda s, q=q: hid_f.at[s, q]))
-            items.append((dwn_z.at[q], lambda s, q=q: dwn_f.at[s, q]))
-        cube = CubeGather(items, (0, 3, 4), f_send, f_recv, d, z)
+            if k < nt - 1:
+                items.append((dwn_z.at[q], lambda s, q=q: dwn_f.at[s, q]))
+        half = dwn_z.shape[1] // 2
+        for first_row in (0, half):
+            at = pl.ds(first_row, half)
+            items.append((dwn_z.at[q, at], lambda s, q=q, at=at: dwn_f.at[s, q, at]))
+        cube = CubeGather(items, (0, 2, 5), f_send, f_recv, d, z)
         for i in range(n):
             cube.start(i)
         locals_ = []
@@ -1360,7 +1381,7 @@
     anywhere = pl.BlockSpec(memory_space=pl.ANY)
     outs = [sds((total, inner), BF16), sds((8, total), F32), sds((rows, width), F32)]
     scratch = []
-    n = 2 * (nt - 1)
+    n = 2 * nt - 1
     if feed:
         for v in feed[:2]:
             outs.append(sds(v.shape, BF16))
@@ -1517,7 +1538,7 @@
     (y, z_in, watt, wmam, out, dh, dm, in_sem, out_sem, g_sem, dm_sem), refs = refs[:11], refs[11:]
     (a2, a2t, acc, dacc, fs, dgs, dus, dmix, piece, sent, came, b_send, b_recv), refs = refs[:13], refs[13:]
     boxes, refs = refs[: 8 * (nt - 2)], refs[8 * (nt - 2) :]
-    (slots, g_send, g_recv, dot_own, dot_land, d_send, d_recv) = refs
+    (slots, g_send, g_recv) = refs
     step = pl.program_id(0)
     tiles = pl.num_programs(0) // 2
     d = lax.axis_index("dp")
@@ -1637,7 +1658,7 @@
             copy.start()
         for copy in late:
             copy.wait()
-        work = Unmix(y, z_in, mgain, watt, wmam, None, do_o, dm, dot_own, rows)
+        work = Unmix(y, z_in, mgain, watt, wmam, None, do_o, dm, dot_o, rows)
         work(z, dmix[...])
         store_dm(z).start()
 
@@ -1653,16 +1674,11 @@
                 cubes[0].middle()
             if dist < nt - 2:
                 cubes[dist].middle()
-            elif dist == nt - 1:
-                dots = Exchange(dot_own, dot_land, d_send, d_recv, d, z, nt)
-                dots.start()
         for k, cube in enumerate(cubes):
             cube.finish(sum_o.at[k])
         chain.drain()
         for cube in cubes:
             cube.drain()
-        dots.wait()
-        dot_o[...] = dots.total()
         for copy in ready:
             copy.wait()
         for q in range(nt):
@@ -1715,7 +1731,7 @@
                   anywhere, anywhere],
         out_specs=[anywhere if i in (0, 1, 3, 5, 7, 8) else fixed(v) for i, v in enumerate(out_shape)],
         out_shape=out_shape,
-        scratch_shapes=late + scratch + unmix_scratch(nt, rows, width, total),
+        scratch_shapes=late + scratch + unmix_scratch(nt, rows, width, total)[:3],
         compiler_params=pltpu.CompilerParams(
             vmem_limit_bytes=60 * 1024 * 1024, collective_id=4, has_side_effects=True
         ),

time: 286 us -> 284 us (level)
    pallas_call x1, Pallas kernels: 64.8 us -> 60.1 us  [feed_unmix(): pl.pallas_call(partial(feed_unmix_kernel, nt), grid=(2 * tiles,), in_spec...]
where the time goes in v3:
time: 284 us
  Pallas kernels  281 us (99%)
    pallas_call x1, Pallas kernels, feed_unmix(): pl.pallas_call(partial(feed_unmix_kernel, nt), grid=(2 * tiles,), in_spec...  60.1 us
    pallas_call x1, Pallas kernels, tail(): pl.pallas_call(partial(tail_kernel, nt), in_specs=[pl.BlockSpec(memory_sp...  49.7 us
    pallas_call x1, Pallas kernels, gather_start(): pl.pallas_call(partial(gather_kernel, nt), out_shape=[jax.ShapeDtypeStruc...  47 us
    pallas_call x1, Pallas kernels, mix_scatter(): pl.pallas_call(partial(mix_scatter_kernel, channels, nt, bool(feed)), in_...  46.9 us
    pallas_call x1, Pallas kernels, mixers_back(): pl.pallas_call(partial(back_kernel, heads, channels, nt, feed is not None...  39.2 us
    pallas_call x1, Pallas kernels, mixers_forward(): pl.pallas_call(partial(forward_kernel, heads, nt, bool(feed)), grid=(tota...  31.5 us

profile of v3, /device:TPU:0, one launch (start us, length us, event | category | flops | bytes accessed | tf_op | source)
XLA Modules:
  0.0 283.7 jit_solution(12592979318887670012)
XLA Ops:
  0.7 0.7 pad_add_fusion.place
  1.3 1.3 maximum_convert_fusion.scal
  2.6 1.4 pack_small.1.refs_6_
  4.0 47.0 %gather_start.1 = (bf16[4,256,1024]{2,1,0:T(8,128)(2,1)}, bf16[1024,128]{1,0:T(8,128)(2,1)}, bf16[128,1024]{1,0:T(8,128)(2,1)}, bf16[2,1024,384]{2,1,0:T(8,128)(...) custom-call(bf16[256,1024]{1,0:T(8,128)(2,1)} %tok_in.1, ...), custom_call_target="tpu_custom_call" | custom-call | tf_op jit(solution)/shard_map/gather_start/pallas_call | solution.py:197
  51.1 1.7 unpack_small.1
  52.8 31.5 %mixers_forward.1 = (bf16[1024,1024]{1,0:T(8,128)(2,1)}, bf16[1024,128]{1,0:T(8,128)(2,1)}, bf16[1024,128]{1,0:T(8,128)(2,1)}, bf16[1024,128]{1,0:T(8,128)(2,1)}...) custom-call(s32[1]{0:T(128)} %bitcast.7.refs_0_.refs_2_, ...), custom_call_target="tpu_custom_call" | custom-call | flops 5000000000 | bytes 15000000 | tf_op jit(solution)/shard_map/mixers_forward/pallas_call | solution.py:623
  84.3 46.9 %mix_scatter.1 = (bf16[1024,384]{1,0:T(8,128)(2,1)}, f32[8,1024]{1,0:T(8,128)}, f32[256,1024]{1,0:T(8,128)}, bf16[8,4,2,128,512]{4,3,2,1,0:T(8,128)(2,1)}, bf16[8,4,512,128]{3,2,1,0:T(8,128)(2,1)}) custom-call(bf16[1024,128]{1,0:T(8,128)(2,1)} %get-tuple-element.110.refs_0_.o_in, ...), custom_call_target="tpu_custom_call", output_to_operand_aliasing={{3}: (8, {}), {4}: (9, {})} | custom-call | flops 1000000000 | bytes 130000000 | tf_op jit(solution)/shard_map/mix_scatter/pallas_call | solution.py:1389
  131.2 60.1 %feed_unmix.1 = (bf16[256,1024]{1,0:T(8,128)(2,1)}, f32[256,1024]{1,0:T(8,128)}, f32[1,1024]{1,0:T(1,128)}, bf16[1024,1024]{1,0:T(8,128)(2,1)}, bf16[1024,128]{1...) custom-call(f32[256,1024]{1,0:T(8,128)} %get-tuple-element.121.refs_, ...), custom_call_target="tpu_custom_call" | custom-call | flops 10000000000 | bytes 150000000 | tf_op jit(solution)/shard_map/feed_unmix/pallas_call | solution.py:1727
  191.3 39.2 %mixers_back.1 = (bf16[1024,128]{1,0:T(8,128)(2,1)}, bf16[1024,256]{1,0:T(8,128)(2,1)}, bf16[1024,384]{1,0:T(8,128)(2,1)}, bf16[1024,384]{1,0:T(8,128)(2,1)}, bf...) custom-call(bf16[2,1536,128]{2,1,0:T(8,128)(2,1)} %get-tuple-element, ...), custom_call_target="tpu_custom_call" | custom-call | flops 6000000000 | bytes 18000000 | tf_op jit(solution)/shard_map/mixers_back/pallas_call | solution.py:958
  230.5 49.7 %tail.1 = (bf16[256,1024]{1,0:T(8,128)(2,1)}, f32[1408,128]{1,0:T(8,128)}, f32[1536,128]{1,0:T(8,128)}, f32[32,512]{1,0:T(8,128)}, f32[160,128]{1,0:T(8,128)}) custom-call(bf16[256,1024]{1,0:T(8,128)(2,1)} %tok_in.1, f32[1,1024]{1,0:T(1,128)} %get-tuple-element.99.refs_2_.gain, f32[256,1024]{1,0:T(8,128)} %get-tuple-element.125.dh_in, ...), custom_call_target="tpu_custom_call" | custom-call | flops 7000000000 | bytes 150000000 | tf_op jit(solution)/shard_map/tail/pallas_call | solution.py:2036
  280.2 3.4 %finish.1 = (f32[128,128]{1,0:T(8,128)}, f32[128,128]{1,0:T(8,128)}, f32[2,128,384]{2,1,0:T(8,128)}, f32[384,128]{1,0:T(8,128)}, f32[2,128,512]{2,1,0:T(8,128)},...) custom-call(s32[2]{0:T(128)} %pad_add_fusion.place, ...), custom_call_target="tpu_custom_call" | custom-call | tf_op jit(solution)/shard_map/finish/pallas_call | solution.py:2130

commit v4 on v3

--- a/solution.py
+++ b/solution.py
@@ -234,9 +234,9 @@
 
 
 def unpack_kernel(
-    heads, where, scal, packed, first_o, second_o, gain_o, tapx_o, tapb_o, step_o, decay_o, bias_o, skip_o
+    heads, scal, packed, first_o, second_o, gain_o, tapx_o, tapb_o, step_o, decay_o, bias_o, skip_o
 ):
-    z = where[0]
+    z = lax.axis_index("tensor")
     f32 = jnp.float32
     nd, nt = packed.shape[:2]
     tiles = [[packed[k, q].astype(f32) for q in range(nt)] for k in range(nd)]
@@ -272,7 +272,7 @@
     bias_o[...] = bias
 
 
-def unpack_small(heads, where, scal, packed, width):
+def unpack_small(heads, scal, packed, width):
     inner = heads * SSM_DIM
     vmem = pl.BlockSpec(memory_space=pltpu.VMEM)
     smem = pl.BlockSpec(memory_space=pltpu.SMEM)
@@ -281,12 +281,12 @@
     shapes = [(1, width), (1, width), (1, inner), (8, inner), (8, 256)]
     return pl.pallas_call(
         partial(unpack_kernel, heads),
-        in_specs=[smem, smem, vmem],
+        in_specs=[smem, vmem],
         out_specs=[vmem] * 9,
         out_shape=[sds(s, f32) for s in shapes]
         + [sds((8, width), jnp.bfloat16), sds((8, 128), f32), sds((8, 128), f32), sds((1, inner), f32)],
         name="unpack_small",
-    )(where, scal, packed)
+    )(scal, packed)
 
 
 def pick(values, index, axis=0):
@@ -336,6 +336,10 @@
 
 def sigmoid(v):
     return 1.0 / (1.0 + jnp.exp(-v))
+
+
+def second_head():
+    return lax.axis_index("tensor") * 2 // (QHEADS // KVHEADS) == 1
 
 
 def lanes_of(shape):
@@ -439,10 +443,14 @@
                 copy.start()
 
         self.at(0, act)
+        def first():
+            for chain in self.chains:
+                chain.hop(1)
+
+        self.at(1, first)
+
     def middle(self):
         def near():
-            for chain in self.chains:
-                chain.hop(1)
             for i in range(2):
                 self.cube.near(i)
 
@@ -471,9 +479,9 @@
 def forward_kernel(heads, nt, feed, *refs):
     if feed:
         beside = FeedGather(
-            pl.program_id(0), nt, *refs[14:16], *refs[29:33], refs[38], refs[39:45]
+            pl.program_id(0), nt, *refs[13:15], *refs[28:32], refs[37], refs[38:44]
         )
-        refs = refs[:14] + refs[16:29] + refs[33:38]
+        refs = refs[:13] + refs[15:28] + refs[32:37]
         beside.begin()
         forward_step(heads, beside.middle, *refs)
         beside.end()
@@ -482,13 +490,13 @@
 
 
 def forward_step(
-    heads, middle, kvh, tok, gain, wq, win, stp, wsh, cosine, sine, tapx, tapb, decay, bias, skip,
+    heads, middle, tok, gain, wq, win, stp, wsh, cosine, sine, tapx, tapb, decay, bias, skip,
     a1_o, q_o, k_o, v_o, lse_o, o_o, x_o, z_o, b_o, y_o, t_o, s_o, sq_o,
     keys, vals, xs, bs, state,
 ):
     step = pl.program_id(0)
     rows = tok.shape[0]
-    second = kvh[0] == 1
+    second = second_head()
 
     @pl.when(step == 0)
     def _():
@@ -594,7 +602,7 @@
 
 
 def mixers_forward(
-    heads, nt, kvh, tok, gain, wq, win, stp, wsh, cosine, sine, tapx, tapb, decay, bias, skip, feed=()
+    heads, nt, tok, gain, wq, win, stp, wsh, cosine, sine, tapx, tapb, decay, bias, skip, feed=()
 ):
     total, width = tok.shape
     rows = 256
@@ -623,7 +631,7 @@
     return pl.pallas_call(
         partial(forward_kernel, heads, nt, bool(feed)),
         grid=(total // rows,),
-        in_specs=[pl.BlockSpec(memory_space=pltpu.SMEM), tall(width), whole(gain), whole(wq), whole(win),
+        in_specs=[tall(width), whole(gain), whole(wq), whole(win),
                   whole(stp), whole(wsh), tall(128), tall(128), whole(tapx), whole(tapb),
                   whole(decay), whole(bias), whole(skip)] + more_in,
         out_specs=[tall(width), tall(128), tall(128), tall(128), wide, tall(128), tall(inner),
@@ -640,10 +648,10 @@
         compiler_params=pltpu.CompilerParams(vmem_limit_bytes=VMEM_LIMIT, **extra),
         cost_estimate=pl.CostEstimate(flops=int(5e9), bytes_accessed=int(15e6), transcendentals=int(4e6)),
         name="mixers_forward",
-    )(kvh, tok, gain, wq, win, stp, wsh, cosine, sine, tapx, tapb, decay, bias, skip, *feed)
-
-
-def attend_back(step, kvh, q, k2, v2, lse, do, cosine, sine, cos_all, sin_all, dq_o, dkv_o, dk, dv):
+    )(tok, gain, wq, win, stp, wsh, cosine, sine, tapx, tapb, decay, bias, skip, *feed)
+
+
+def attend_back(step, q, k2, v2, lse, do, cosine, sine, cos_all, sin_all, dq_o, dkv_o, dk, dv):
     rows = q.shape[0]
     steps = k2.shape[0] // rows
     scale = HEAD_SIZE**-0.5
@@ -684,7 +692,7 @@
 
     @pl.when(step == 2 * steps - 1)
     def _():
-        own = (lanes_of(dk.shape) < HEAD_SIZE) != (kvh[0] == 1)
+        own = (lanes_of(dk.shape) < HEAD_SIZE) != second_head()
         g = dk[...]
         g = turn(g + pltpu.roll(g, 64, 1), cos_all[...], -sin_all[...])
         dkv_o[:, 0:128] = jnp.where(own, g, 0.0).astype(BF16)
@@ -699,15 +707,15 @@
         d = lax.axis_index("dp")
         z = lax.axis_index("tensor")
         sums, raw, refs = refs[0], refs[1], refs[2:]
-        feed_o, refs = refs[37], refs[:37] + refs[38:]
-        parts, chain_boxes, box = refs[44], refs[45:49], refs[49:57]
-        (dot_sum, dot_land, d_send, d_recv), refs = refs[57:61], refs[:44]
+        feed_o, refs = refs[36], refs[:36] + refs[37:]
+        parts, chain_boxes, box = refs[43], refs[44:48], refs[48:56]
+        (dot_sum, dot_land, d_send, d_recv), refs = refs[56:60], refs[:43]
         peers = cube_peers(d)
         square = SquareScatter(
             lambda i, j: (2 * i + j,), raw, box[:6], box[6], box[7], peers, dp_bits(d), z
         )
         chain = ChainScatter(parts, *chain_boxes, d, z, nt)
-        dots = Exchange(refs[20], dot_land, d_send, d_recv, d, z, nt)
+        dots = Exchange(refs[19], dot_land, d_send, d_recv, d, z, nt)
 
         @pl.when(step == 0)
         def _():
@@ -727,7 +735,7 @@
             square.finish(parts.at[quarter_at(nt - 2, z, nt)])
             chain.step(2)
 
-    attend_back(step, *refs[:10], *refs[27:29], *refs[37:39])
+    attend_back(step, *refs[:9], *refs[26:28], *refs[36:38])
     if feed:
 
         @pl.when(step == 0)
@@ -736,8 +744,8 @@
             dot_sum[...] = dots.total()
 
         at = pl.ds(pl.multiple_of((pl.num_programs(0) - 1 - step) * block_len, block_len), block_len)
-        refs = refs[:20] + (dot_sum.at[:, at],) + refs[21:]
-    scan_back(heads, channels, step, *refs[10:27], *refs[29:37], *refs[39:44])
+        refs = refs[:19] + (dot_sum.at[:, at],) + refs[20:]
+    scan_back(heads, channels, step, *refs[9:26], *refs[28:36], *refs[38:43])
     if feed:
 
         @pl.when(step == pl.num_programs(0) - 1)
@@ -899,7 +907,7 @@
 
 
 def mixers_back(
-    heads, channels, nt, kvh, q, k2, v2, lse, do, cosine, sine, dm, y, zr, xr, br, trow, states, rsum, dots,
+    heads, channels, nt, q, k2, v2, lse, do, cosine, sine, dm, y, zr, xr, br, trow, states, rsum, dots,
     gain, tapx, tapb, decay, bias, skip, feed=None,
 ):
     total, inner = y.shape
@@ -925,7 +933,7 @@
     def fixed(*shape):
         return pl.BlockSpec(shape, lambda i: (0,) * len(shape))
 
-    in_specs = [pl.BlockSpec(memory_space=pltpu.SMEM), ask, whole(k2), whole(v2),
+    in_specs = [ask, whole(k2), whole(v2),
                 pl.BlockSpec((8, q_rows), lambda i: (0, steps // 2 - 1 - i // 2)), ask, ask, ask, whole(cosine), whole(sine),
                 tall(inner), tall(inner), tall(inner), tall(inner), before(inner), tall(pair),
                 before(pair), wide, pl.BlockSpec((1, pair // 2, inner), lambda i: (steps - 1 - i, 0, 0)),
@@ -939,13 +947,13 @@
                pltpu.VMEM((rows + 8, inner), F32), pltpu.VMEM((rows + 8, pair), F32),
                pltpu.VMEM((rows + 8, inner), F32), pltpu.VMEM((rows + 8, pair), F32),
                pltpu.VMEM((pair // 2, inner), F32)]
-    args = [kvh, q, k2, v2, lse, do, cosine, sine, cosine, sine, dm, y, zr, xr, xr, br, br, trow, states,
+    args = [q, k2, v2, lse, do, cosine, sine, cosine, sine, dm, y, zr, xr, xr, br, br, trow, states,
             rsum, dots, gain, tapx, tapb, decay, bias, skip]
     extra = {}
     if feed is not None:
         piece = feed[0].shape[1:]
         dma = pltpu.SemaphoreType.DMA
-        in_specs[20] = whole(dots)
+        in_specs[19] = whole(dots)
         args = list(feed) + args
         in_specs = [whole(v) for v in feed] + in_specs
         out_specs = out_specs + [fixed(*piece)]
@@ -1283,17 +1291,23 @@
 
 
 def mix_scatter_kernel(channels, nt, feed, *refs):
-    (o, y_in, gate_in, sq, gain, watt, wmam, tok), refs = refs[:8], refs[8:]
+    (o_in, y_in, gate_in, sq, gain, watt_in, wmam_in, tok_in), refs = refs[:8], refs[8:]
     if feed:
         (hid_z, dwn_z), refs = refs[2:4], refs[4:]
         (m_o, sq_o, hid_o, hid_f, dwn_f), refs = refs[:5], refs[5:]
         (lsem, f_send, f_recv), refs = refs[:3], refs[3:]
     else:
         (m_o, sq_o, hid_o), refs = refs[:3], refs[3:]
-    (y, z_in, in_sem, sq_land, sq_send, sq_recv, parts, bufs, landed, c_send, c_recv) = refs
+    (y, z_in, in_sem, o, watt, wmam, tok, late_sem, sq_land, sq_send, sq_recv, parts, bufs, landed, c_send, c_recv) = refs
     d = lax.axis_index("dp")
     z = lax.axis_index("tensor")
     rows = tok.shape[0]
+    late = [
+        pltpu.make_async_copy(src, dst, late_sem.at[i])
+        for i, (src, dst) in enumerate(((o_in, o), (watt_in, watt), (wmam_in, wmam), (tok_in, tok)))
+    ]
+    for copy in late:
+        copy.start()
 
     def rows_of(q):
         return pl.ds(pl.multiple_of(q * rows, rows), rows)
@@ -1347,6 +1361,8 @@
         m_o[at, :] = m
         parts[q] = (dot_nn(o[at, :], watt[...]) + dot_nn(m, wmam[...])).astype(BF16)
 
+    for copy in late:
+        copy.wait()
     part(first)
     chain.step(0)
 
@@ -1388,12 +1404,14 @@
         scratch = [dma((n,)), dma((n, 7)), dma((n, 7))]
     return pl.pallas_call(
         partial(mix_scatter_kernel, channels, nt, bool(feed)),
-        in_specs=[vmem, anywhere, anywhere] + [vmem] * 5 + [anywhere] * len(feed[:2]) + [vmem] * len(feed[2:]),
+        in_specs=[anywhere] * 3 + [vmem] * 2 + [anywhere] * 3 + [anywhere] * len(feed[:2]) + [vmem] * len(feed[2:]),
         out_specs=[vmem] * 3 + [anywhere] * (len(outs) - 3),
         out_shape=outs,
         input_output_aliases={8: 3, 9: 4} if feed else {},
         scratch_shapes=scratch + [pltpu.VMEM((total, inner), F32), pltpu.VMEM((total, inner), F32),
-                                  dma((2, nt)), pltpu.VMEM((nt - 1, 8, total), F32), dma((nt - 1,)), dma((nt - 1,)),
+                                  dma((2, nt))]
+        + [pltpu.VMEM(v.shape, v.dtype) for v in (o, watt, wmam, tok)]
+        + [dma((4,)), pltpu.VMEM((nt - 1, 8, total), F32), dma((nt - 1,)), dma((nt - 1,)),
                         pltpu.VMEM((nt, rows, width), BF16)] + chain_scratch(nt, rows, width),
         compiler_params=pltpu.CompilerParams(
             vmem_limit_bytes=VMEM_LIMIT, collective_id=1, has_side_effects=True
@@ -2059,13 +2077,14 @@
 
 
 def finish_kernel(
-    heads, place, mixed, fed, small, *refs
+    heads, nt, mixed, fed, small, *refs
 ):
     (que_o, att_o, inn_o, mam_o, hid_o, dwn_o, norms_o, taps_o, chan_o, gain_o, step_o) = refs[-17:-6]
     heads_o = refs[-6:-3]
     for src, dst in zip(refs[:3], refs[-3:]):
         dst[...] = src[...]
-    d, p = place[0], place[1]
+    d = lax.axis_index("dp")
+    p = d * nt + lax.axis_index("tensor")
     block = que_o.shape[0]
     inner = mam_o.shape[0]
     first = 0
@@ -2124,18 +2143,18 @@
     step_o[...] = steps[0:heads, :]
 
 
-def finish(heads, place, mixed, fed, small, shapes, passed):
+def finish(heads, nt, mixed, fed, small, shapes, passed):
     vmem = pl.BlockSpec(memory_space=pltpu.VMEM)
     sds = jax.ShapeDtypeStruct
     return pl.pallas_call(
-        partial(finish_kernel, heads),
-        in_specs=[pl.BlockSpec(memory_space=pltpu.SMEM)] + [vmem] * 6,
+        partial(finish_kernel, heads, nt),
+        in_specs=[vmem] * 6,
         out_specs=[vmem] * (len(shapes) + 6),
         out_shape=[sds(s, F32) for s in shapes] + [sds((1, heads), F32)] * 3
         + [sds(v.shape, v.dtype) for v in passed],
         compiler_params=pltpu.CompilerParams(vmem_limit_bytes=VMEM_LIMIT),
         name="finish",
-    )(place, mixed, fed, small, *passed)
+    )(mixed, fed, small, *passed)
 
 
 def rope_wide(length):
@@ -2193,10 +2212,9 @@
             tokens, query_proj, attend_out, inner_proj, mamba_out, shared_proj, small, nd, nt
         )
         scal = jnp.stack([decay_log, step_bias, skip_weight]).astype(F32)
-        where = tensor_index.astype(jnp.int32).reshape(1)
         (
             gain_first, gain_second, gain_mix, taps_x, taps_b, step_rows, decay, bias, skip,
-        ) = unpack_small(heads, where, scal, sma, width)
+        ) = unpack_small(heads, scal, sma, width)
         full_shared = sha.reshape(width, -1)
         feed = (hidden_proj, down_proj)
     else:
@@ -2238,12 +2256,10 @@
         decay = head_rows(-jnp.exp(decay_log.astype(F32)))
         bias = head_rows(step_bias.astype(F32))
         skip = jnp.repeat(skip_weight.astype(F32), SSM_DIM)[None, :]
-    q_heads = query_proj.shape[1] // HEAD_SIZE
-    kv_head = (tensor_index * q_heads // (QHEADS // KVHEADS)).astype(jnp.int32).reshape(1)
     cosine, sine = rope_wide(group_rows)
 
     (a1, q, k2, v2, lse, o, xr, zr, br, y, trow, states, squares, *feed) = mixers_forward(
-        heads, nt, kv_head, tok_full.reshape(group_rows, width), gain_first, full_query, full_inner, step_rows,
+        heads, nt, tok_full.reshape(group_rows, width), gain_first, full_query, full_inner, step_rows,
         full_shared, cosine, sine, taps_x, taps_b, decay, bias, skip, feed,
     )
     mixed = mix_scatter(
@@ -2272,7 +2288,7 @@
         gradient_down = chain_scatter(down_sum, nt)
 
     back = mixers_back(
-        heads, channels, nt, kv_head, q, k2, v2, lse, do, cosine, sine, dm, y, zr, xr, br, trow, states,
+        heads, channels, nt, q, k2, v2, lse, do, cosine, sine, dm, y, zr, xr, br, trow, states,
         squares, dots, gain_mix, taps_x, taps_b, decay, bias, skip,
         (feed_sums, feed_raw) if nd == 8 else None,
     )
@@ -2283,7 +2299,6 @@
             step_rows, full_shared, grad_gain_two, grad_tb, grad_tx, grad_rows, grad_heads, feed_own, back[10],
         )
         gradient_tokens, mixed, fed, gradient_shared, small_sums = sums
-        place = jnp.stack([d, d * nt + tensor_index]).astype(jnp.int32)
         shapes = [
             query_proj.shape, attend_out.shape, inner_proj.shape, mamba_out.shape, hidden_proj.shape,
             down_proj.shape, norm_gains.shape, shared_taps.shape, channel_taps.shape, mixer_gain.shape,
@@ -2308,7 +2323,7 @@
             gradient_tokens,
             gradient_shared,
         ) = finish(
-            heads, place, mixed, fed, small_sums, shapes, (layer_out, gradient_tokens, gradient_shared)
+            heads, nt, mixed, fed, small_sums, shapes, (layer_out, gradient_tokens, gradient_shared)
         )
         return (
             layer_out,

time: 284 us -> 283 us (level)
  no operation moved by 1% of the time
where the time goes in v4:
time: 283 us
  Pallas kernels  281 us (99%)
    pallas_call x1, Pallas kernels, feed_unmix(): pl.pallas_call(partial(feed_unmix_kernel, nt), grid=(2 * tiles,), in_spec...  60.1 us
    pallas_call x1, Pallas kernels, tail(): pl.pallas_call(partial(tail_kernel, nt), in_specs=[pl.BlockSpec(memory_sp...  49.4 us
    pallas_call x1, Pallas kernels, mix_scatter(): pl.pallas_call(partial(mix_scatter_kernel, channels, nt, bool(feed)), in_...  47.2 us
    pallas_call x1, Pallas kernels, gather_start(): pl.pallas_call(partial(gather_kernel, nt), out_shape=[jax.ShapeDtypeStruc...  47 us
    pallas_call x1, Pallas kernels, mixers_back(): pl.pallas_call(partial(back_kernel, heads, channels, nt, feed is not None...  39.2 us
    pallas_call x1, Pallas kernels, mixers_forward(): pl.pallas_call(partial(forward_kernel, heads, nt, bool(feed)), grid=(tota...  31.4 us

profile of v4, /device:TPU:0, one launch (start us, length us, event | category | flops | bytes accessed | tf_op | source)
XLA Modules:
  0.0 282.9 jit_solution(6461387460261347771)
XLA Ops:
  0.7 1.3 maximum_convert_fusion.scal
  1.9 1.4 pack_small.1.refs_6_
  3.4 47.0 %gather_start.1 = (bf16[4,256,1024]{2,1,0:T(8,128)(2,1)}, bf16[1024,128]{1,0:T(8,128)(2,1)}, bf16[128,1024]{1,0:T(8,128)(2,1)}, bf16[2,1024,384]{2,1,0:T(8,128)(...) custom-call(bf16[256,1024]{1,0:T(8,128)(2,1)} %tok_in.1, ...), custom_call_target="tpu_custom_call" | custom-call | tf_op jit(solution)/shard_map/gather_start/pallas_call | solution.py:197
  50.4 1.7 unpack_small.1
  52.1 31.4 %mixers_forward.1 = (bf16[1024,1024]{1,0:T(8,128)(2,1)}, bf16[1024,128]{1,0:T(8,128)(2,1)}, bf16[1024,128]{1,0:T(8,128)(2,1)}, bf16[1024,128]{1,0:T(8,128)(2,1)}...) custom-call(bf16[1024,1024]{1,0:T(8,128)(2,1)} %bitcast.15, ...), custom_call_target="tpu_custom_call" | custom-call | flops 5000000000 | bytes 15000000 | tf_op jit(solution)/shard_map/mixers_forward/pallas_call | solution.py:631
  83.5 47.2 %mix_scatter.1 = (bf16[1024,384]{1,0:T(8,128)(2,1)}, f32[8,1024]{1,0:T(8,128)}, f32[256,1024]{1,0:T(8,128)}, bf16[8,4,2,128,512]{4,3,2,1,0:T(8,128)(2,1)}, bf16[8,4,512,128]{3,2,1,0:T(8,128)(2,1)}) custom-call(bf16[1024,128]{1,0:T(8,128)(2,1)} %get-tuple-element.110.refs_0_.o_in, ...), custom_call_target="tpu_custom_call", output_to_operand_aliasing={{3}: (8, {}), {4}: (9, {})} | custom-call | flops 1000000000 | bytes 130000000 | tf_op jit(solution)/shard_map/mix_scatter/pallas_call | solution.py:1405
  130.7 60.1 %feed_unmix.1 = (bf16[256,1024]{1,0:T(8,128)(2,1)}, f32[256,1024]{1,0:T(8,128)}, f32[1,1024]{1,0:T(1,128)}, bf16[1024,1024]{1,0:T(8,128)(2,1)}, bf16[1024,128]{1...) custom-call(f32[256,1024]{1,0:T(8,128)} %get-tuple-element.121.refs_, ...), custom_call_target="tpu_custom_call" | custom-call | flops 10000000000 | bytes 150000000 | tf_op jit(solution)/shard_map/feed_unmix/pallas_call | solution.py:1745
  190.8 39.2 %mixers_back.1 = (bf16[1024,128]{1,0:T(8,128)(2,1)}, bf16[1024,256]{1,0:T(8,128)(2,1)}, bf16[1024,384]{1,0:T(8,128)(2,1)}, bf16[1024,384]{1,0:T(8,128)(2,1)}, bf...) custom-call(bf16[2,1536,128]{2,1,0:T(8,128)(2,1)} %get-tuple-element, ...), custom_call_target="tpu_custom_call" | custom-call | flops 6000000000 | bytes 18000000 | tf_op jit(solution)/shard_map/mixers_back/pallas_call | solution.py:966
  230.1 49.4 %tail.1 = (bf16[256,1024]{1,0:T(8,128)(2,1)}, f32[1408,128]{1,0:T(8,128)}, f32[1536,128]{1,0:T(8,128)}, f32[32,512]{1,0:T(8,128)}, f32[160,128]{1,0:T(8,128)}) custom-call(bf16[256,1024]{1,0:T(8,128)(2,1)} %tok_in.1, f32[1,1024]{1,0:T(1,128)} %get-tuple-element.99.refs_1_.gain, f32[256,1024]{1,0:T(8,128)} %get-tuple-element.125.dh_in, ...), custom_call_target="tpu_custom_call" | custom-call | flops 7000000000 | bytes 150000000 | tf_op jit(solution)/shard_map/tail/pallas_call | solution.py:2054
  279.4 3.3 %finish.1 = (f32[128,128]{1,0:T(8,128)}, f32[128,128]{1,0:T(8,128)}, f32[2,128,384]{2,1,0:T(8,128)}, f32[384,128]{1,0:T(8,128)}, f32[2,128,512]{2,1,0:T(8,128)},...) custom-call(f32[1408,128]{1,0:T(8,128)} %get-tuple-element.156.mixed, ...), custom_call_target="tpu_custom_call" | custom-call | tf_op jit(solution)/shard_map/finish/pallas_call | solution.py:2149
